TPU v7x, 256 devices: a whole 4x4x8 slice. The times are simulated.
256 devices in a mesh: wide: 64 (over z, y, core), narrow: 4 (over x).
Axes of the slice: x: 4, y: 4, z: 8, core: 2. Of those that a mesh axis runs over, the one named last changes fastest.
Arguments:
- xblk: bfloat16 [3, 576, 9, 16384], P(None, 'narrow', None, 'wide')
- link: int32 [256], replicated, may hold values from 0 to 1, as said below
- order: int32 [16384], P('wide'), may hold values from 0 to 255, as said below
Outputs:
- relaid: bfloat16 [9, 5, 576, 16384], P(None, None, 'narrow', 'wide')
Inputs may be any that keep to these rules, and one draw needn't show every extreme that they name: `order`: each aligned run of 256 entries is a permutation of 0 to 255. link[r] is 0 or 1 for every r.
All inputs are finite; a program needn't handle non-finite values.
Results may differ from a plain program's by a relative error of at most 0.001.
Values may be sent and summed in bfloat16 or wider, within the bound.
No kernel may reach another device: no remote copies, remote signals or barrier semaphores. Data moves between devices by JAX's collectives and lax.ppermute only.
A program may use at most 192 MiB of HBM per device.

v0:
```python
import jax
import jax.numpy as jnp
from jax import lax
from jax.sharding import PartitionSpec as P

ORBITALS = 9
BLOCK_ATOMS = 64


def with_halo(block, sides, width):
    for axis, dim in sides:
        count = lax.axis_size(axis)
        forward = [(i, i + 1) for i in range(count - 1)]
        forward.append((count - 1, 0))
        backward = [(target, source) for source, target in forward]
        low = lax.ppermute(
            lax.slice_in_dim(block, block.shape[dim] - width, None, axis=dim), axis, forward
        )
        high = lax.ppermute(lax.slice_in_dim(block, 0, width, axis=dim), axis, backward)
        block = jnp.concatenate([low, block, high], axis=dim)
    return block


def masked_blocks(xblk, link, first_row):
    col_width = xblk.shape[1]
    row_count = xblk.shape[3] // BLOCK_ATOMS
    shaped = xblk.reshape(3, col_width, ORBITALS, row_count, BLOCK_ATOMS)
    stored = jnp.transpose(shaped, (3, 0, 4, 2, 1)).reshape(
        row_count, 3, BLOCK_ATOMS * ORBITALS, col_width
    )
    total_rows = link.shape[0]
    global_rows = first_row + jnp.arange(row_count, dtype=jnp.int32)
    present = jnp.take(link, global_rows).astype(jnp.bfloat16)
    previous = jnp.take(link, (global_rows - 1) % total_rows).astype(jnp.bfloat16)
    factors = jnp.stack([previous, jnp.ones_like(present), present], axis=1)
    return stored * factors[:, :, None, None]


def to_atoms(values):
    row_count, slab_count, block_width, col_width = values.shape
    atom_count = block_width // ORBITALS
    shaped = values.reshape(row_count, slab_count, atom_count, ORBITALS, col_width)
    return jnp.transpose(shaped, (3, 1, 4, 0, 2)).reshape(
        ORBITALS, slab_count, col_width, row_count * atom_count
    )


def local_trace(slab, narrow_pos):
    col_width = slab.shape[2]
    square = lax.dynamic_slice_in_dim(slab, narrow_pos * col_width, col_width, 1)
    return jnp.sum(jnp.diagonal(square, axis1=1, axis2=2).astype(jnp.float32))


def blend(product, initial, weight, axis_pos):
    edge = jnp.zeros_like(lax.slice_in_dim(product, 0, 1, axis=axis_pos))
    padded = jnp.concatenate([edge, initial.astype(jnp.float32), edge], axis=axis_pos)
    return product + 2.0 * weight * (padded - product)


def shards(xblk, link, order):
    row_count = xblk.shape[3] // BLOCK_ATOMS
    wide_pos = lax.axis_index("wide")
    narrow_pos = lax.axis_index("narrow")
    total_rows = row_count * lax.axis_size("wide")
    blocks = masked_blocks(xblk, link, wide_pos * row_count)
    pieces = []
    left_panels = lax.all_gather(blocks, "narrow", axis=3, tiled=True)
    nearby = with_halo(blocks, (("wide", 0),), 1)
    for target in range(-2, 3):
        summed = jnp.zeros((row_count, blocks.shape[2], blocks.shape[3]), jnp.float32)
        for offset in range(-1, 2):
            partner = target - offset
            if abs(partner) <= 1:
                summed = summed + jnp.einsum(
                    "iab,ibc->iac",
                    left_panels[:, offset + 1],
                    nearby[1 + offset : 1 + offset + row_count, partner + 1],
                    preferred_element_type=jnp.float32,
                )
        pieces.append(summed)
    product = jnp.stack(pieces, axis=1)
    trace_x = local_trace(blocks[:, 1], narrow_pos)
    trace_sq = local_trace(product[:, 2], narrow_pos)
    sum_x, sum_sq = lax.psum((trace_x, trace_sq), ("wide", "narrow"))
    weight = jax.nn.sigmoid(4.0 * (sum_x - sum_sq) / (total_rows * blocks.shape[2]) + 5.0)
    fresh = blend(product, blocks, weight, 1).astype(jnp.bfloat16)
    return lax.all_to_all(
        jnp.take(to_atoms(fresh), order, axis=3), "wide", split_axis=3, concat_axis=3, tiled=True
    )


def solution(mesh):
    return jax.shard_map(
        shards,
        mesh=mesh,
        in_specs=(P(None, "narrow", None, "wide"), P(), P("wide")),
        out_specs=P(None, None, "narrow", "wide"),
        check_vma=False,
    )
```

profile of v0, /device:TPU:8, one launch (start us, length us, event | category | flops | bytes accessed | tf_op | source)
XLA Modules:
  0.0 494.3 jit_solution(6153370804817754901)
XLA Ops:
  6.5 6.8 %reshape.35 = bf16[3,144,9,4,64]{4,3,1,2,0:T(4,128)(2,1)} reshape(bf16[3,144,9,256]{3,1,2,0:T(8,128)(2,1)} %param.5) | data formatting | bytes 3981312 | tf_op jit(solution)/shard_map/reshape | solution.py:27
  13.3 11.3 %copy.15 = bf16[4,3,64,9,144]{4,0,3,2,1:T(4,128)(2,1)S(1)} copy(bf16[4,3,64,9,144]{2,0,4,3,1:T(4,128)(2,1)} %bitcast.81) | data formatting | bytes 3981312 | tf_op jit(solution)/shard_map/transpose | solution.py:28
  24.6 5.4 %copy.16 = bf16[4,3,576,144]{2,3,0,1:T(8,128)(2,1)} copy(bf16[4,3,576,144]{3,0,2,1:T(4,128)(2,1)S(1)} %bitcast.85) | data formatting | bytes 3981312 | tf_op jit(solution)/shard_map/reshape | solution.py:28
  42.1 6.7 %multiply_convert_fusion = f32[4,3,64,9,144]{2,0,4,3,1:T(4,128)} fusion(bf16[4,3]{0,1:T(4,128)(2,1)S(1)} %pad_maximum_fusion.2, bf16[3,144,9,4,64]{4,3,1,2,0:T(4,128)(2,1)} %reshape.35), kind=kLoop, calls=%fused_computation.11 | loop fusion | flops 1990656 | bytes 5971992 | tf_op jit(solution)/shard_map/convert_element_type | solution.py:56
  48.8 5.5 %copy.37 = bf16[4,144,144]{0,2,1:T(8,128)(2,1)} copy(bf16[4,144,144]{1,2,0:T(8,128)(2,1)} %dynamic-slice_bitcast_fusion) | data formatting | bytes 331776 | tf_op jit(solution)/shard_map/dynamic_slice | solution.py:50
  54.3 6.8 %gather_fusion = bf16[144,4]{1,0:T(8,128)(2,1)S(1)} fusion(bf16[4,144,144]{0,2,1:T(8,128)(2,1)} %copy.37, s32[144]{0:T(256)S(1)} %bitcast.82), kind=kCustom, calls=%fused_computation.2 | custom fusion | bytes 3456 | tf_op jit(solution)/shard_map/jit(diagonal)/gather | solution.py:51
  61.7 65.6 %all-gather.2.cloned.1.call-done = bf16[4,3,576,576]{2,3,0,1:T(8,128)(2,1)} async-done(((bf16[4,3,576,144]{2,3,0,1:T(8,128)(2,1)}), bf16[4,3,576,576]{2,3,0,1:T(8,128)(2,1)}) %all-gather.2.cloned.1.call-update) | async-done | bytes 7962640 | tf_op jit(solution)/shard_map/all_gather | solution.py:67
  132.8 3.9 add_add_fusion
  142.5 3.8 fusion.4
  146.3 3.6 copy.18
  149.9 5.2 %copy.31 = f32[4,1,64,9,144]{2,0,4,3,1:T(4,128)} copy(f32[4,1,64,9,144]{4,0,3,2,1:T(4,128)} %bitcast.88) | data formatting | bytes 2654208 | tf_op jit(solution)/shard_map/stack | solution.py:81
  161.3 3.9 fusion.14
  165.1 3.6 copy.21
  168.8 5.2 %copy.32 = f32[4,1,64,9,144]{2,0,4,3,1:T(4,128)} copy(f32[4,1,64,9,144]{4,0,3,2,1:T(4,128)} %bitcast.89) | data formatting | bytes 2654208 | tf_op jit(solution)/shard_map/stack | solution.py:81
  174.0 5.2 %copy.33 = f32[4,1,64,9,144]{2,0,4,3,1:T(4,128)} copy(f32[4,1,64,9,144]{4,0,3,2,1:T(4,128)} %bitcast.86) | data formatting | bytes 2654208 | tf_op jit(solution)/shard_map/stack | solution.py:81
  181.9 3.9 fusion.13
  185.8 3.6 copy.28
  189.5 5.2 %copy.34 = f32[4,1,64,9,144]{2,0,4,3,1:T(4,128)} copy(f32[4,1,64,9,144]{4,0,3,2,1:T(4,128)} %bitcast.90) | data formatting | bytes 2654208 | tf_op jit(solution)/shard_map/stack | solution.py:81
  194.7 3.9 fusion.12
  198.6 3.7 copy.30
  202.3 6.0 %copy.38 = f32[4,144,144]{0,2,1:T(8,128)} copy(f32[4,144,144]{1,2,0:T(8,128)S(1)} %copy-done.7) | data formatting | bytes 663552 | tf_op jit(solution)/shard_map/dynamic_slice | solution.py:50
  208.3 6.1 %gather_fusion.1 = f32[144,4]{1,0:T(8,128)S(1)} fusion(f32[4,144,144]{0,2,1:T(8,128)} %copy.38, s32[144]{0:T(256)S(1)} %bitcast.83), kind=kCustom, calls=%fused_computation.3 | custom fusion | bytes 5760 | tf_op jit(solution)/shard_map/jit(diagonal)/gather | solution.py:51
  215.0 5.2 %copy.35 = f32[4,1,64,9,144]{2,0,4,3,1:T(4,128)} copy(f32[4,1,64,9,144]{4,0,3,2,1:T(4,128)} %bitcast.87) | data formatting | bytes 2654208 | tf_op jit(solution)/shard_map/stack | solution.py:81
  220.2 75.5 %all-reduce = (f32[]{:T(128)}, f32[]{:T(128)}) all-reduce(f32[]{:T(128)} %convert_reduce_fusion, f32[]{:T(128)} %reduce_sum.19), channel_id=1, replica_groups=mesh['wide'=64,'narrow'=4] {'wide','narrow'}, use_global_device_ids=true, to_apply=%region_1.3 | all-reduce | flops 2 | bytes 16 | tf_op jit(solution)/shard_map/psum | solution.py:84
  307.4 12.5 %fusion.3 = bf16[9,5,144,4,64]{4,3,2,0,1:T(4,128)(2,1)} fusion(f32[4,5,64,9,144]{2,0,4,3,1:T(4,128)} %constant_dynamic-update-slice_fusion, f32[4,1,64,9,144]{2,0,4,3,1:T(4,128)S(1)} %broadcast_in_dim.28, f32[4,3,64,9,144]{2,0,4,3,1:T(4,128)} %multiply_convert_fusion, f32[]{:T(128)S(6)} %mul_shard_map.4), kind=kLoop, calls=%fused_computation.10 | loop fusion | flops 9953280 | bytes 15261700 | tf_op jit(solution)/shard_map/transpose | solution.py:43
  319.9 18.9 %copy.55 = bf16[9,5,144,4,64]{2,1,4,3,0:T(8,128)(2,1)} copy(bf16[9,5,144,4,64]{4,3,2,0,1:T(4,128)(2,1)} %fusion.3) | data formatting | bytes 6635520 | tf_op jit(solution)/shard_map/reshape | solution.py:43
  338.9 13.4 %gather_fusion.2 = bf16[256,9,5,144]{3,2,1,0:T(8,128)(2,1)} fusion(bf16[9,5,144,256]{2,1,3,0:T(8,128)(2,1)} %bitcast.84, s32[1024]{0:T(1024)S(1)} %pad_clamp_fusion), kind=kCustom, calls=%fused_computation.4 | custom fusion | bytes 6636544 | tf_op jit(solution)/shard_map/jit(_take)/gather | solution.py:88
  352.3 8.5 %fusion.39 = bf16[256,9,5,144]{3,2,1,0:T(8,128)(2,1)} fusion(bf16[256,9,5,144]{3,2,1,0:T(8,128)(2,1)} %gather_fusion.2, pred[256]{0:T(512)(128)(4,1)S(1)} %compare_and_fusion), kind=kLoop, calls=%fused_computation.83 | loop fusion | flops 1658880 | bytes 6635776
  360.8 14.2 %reshape.83 = bf16[64,2,12960]{2,1,0:T(2,128)(2,1)S(1)} reshape(bf16[256,9,5,144]{3,2,1,0:T(8,128)(2,1)} %fusion.39) | data formatting | bytes 6635520
  375.1 86.6 %all_to_all.5 = bf16[64,2,12960]{2,1,0:T(2,128)(2,1)} all-to-all(bf16[64,2,12960]{2,1,0:T(2,128)(2,1)S(1)} %reshape.83), channel_id=1, replica_groups=mesh['wide'=64,'narrow'=4] {'wide'}, dimensions={0} | all-to-all | bytes 6635520 | tf_op jit(solution)/shard_map/all_to_all | solution.py:87
  461.7 15.6 %reshape.84 = bf16[256,9,5,144]{3,2,1,0:T(8,128)(2,1)} reshape(bf16[64,2,12960]{2,1,0:T(2,128)(2,1)} %all_to_all.5) | data formatting | bytes 6635520
  477.2 10.3 %copy.41 = bf16[9,5,144,256]{3,2,1,0:T(8,128)(2,1)} copy(bf16[9,5,144,256]{2,1,0,3:T(8,128)(2,1)} %bitcast.80) | data formatting | bytes 6635520 | tf_op jit(solution)/shard_map/all_to_all | solution.py:87
  (55 shorter events, 43.8 us)
Async XLA Ops:
  6.5 23.5 %copy-start = (s32[256]{0:T(256)S(1)}, s32[256]{0:T(256)}, u32[]{:S(2)}) copy-start(s32[256]{0:T(256)} %param.6) | copy-start | bytes 3076
  6.5 120.8 %all-gather.2.cloned.1.call-start = ((), (), s32[]{:S(2)}) async-start(), calls=%async_computation.1 | async-start | bytes 11059200 | tf_op jit(solution)/shard_map/all_gather | solution.py:67
  34.7 1.6 copy-start.2
  34.7 7.4 %copy-start.8 = (s32[256]{0:T(256)S(1)}, s32[256]{0:T(256)}, u32[]{:S(2)}) copy-start(s32[256]{0:T(256)} %param.7) | copy-start | bytes 3076
  37.5 24.2 %collective-permute-start = (bf16[1,3,576,144]{2,3,0,1:T(8,128)(2,1)}, bf16[1,3,576,144]{2,3,0,1:T(8,128)(2,1)S(1)}, u32[]{:S(2)}, u32[]{:S(2)}) collective-permute-start(bf16[1,3,576,144]{2,3,0,1:T(8,128)(2,1)} %get-tuple-element.9), channel_id=1, source_target_pairs={{0,4},{4,8},{8,12},{12,16},{16,20},{20,24},{24,28},{28,32},{32,36}... | collective-permute-start | bytes 1493000 | tf_op jit(solution)/shard_map/ppermute | solution.py:16
  37.5 95.2 %collective-permute-start.1 = (bf16[1,3,576,144]{2,3,0,1:T(8,128)(2,1)}, bf16[1,3,576,144]{2,3,0,1:T(8,128)(2,1)S(1)}, u32[]{:S(2)}, u32[]{:S(2)}) collective-permute-start(bf16[1,3,576,144]{2,3,0,1:T(8,128)(2,1)} %get-tuple-element.8), channel_id=1, source_target_pairs={{4,0},{8,4},{12,8},{16,12},{20,16},{24,20},{28,24},{32,28},{36,32}... | collective-permute-start | bytes 1493000 | tf_op jit(solution)/shard_map/ppermute | solution.py:19
  198.6 3.7 copy-start.7
  208.3 88.8 %copy-start.3 = (f32[4,1,64,9,144]{2,0,4,3,1:T(4,128)S(1)}, f32[4,1,64,9,144]{2,0,4,3,1:T(4,128)}, u32[]{:S(2)}) copy-start(f32[4,1,64,9,144]{2,0,4,3,1:T(4,128)} %copy.32) | copy-start | bytes 3981316
  297.1 2.7 copy-start.4
  299.8 2.7 copy-start.5
  302.5 2.7 copy-start.6
  477.2 10.3 %copy-start.1 = (s32[256]{0:T(256)S(1)}, s32[256]{0:T(256)}, u32[]{:S(2)}) copy-start(s32[256]{0:T(256)} %param.6) | copy-start | bytes 3076
Sparse Core Ops, SparseCore 0:
  34.9 92.4 all-gather.1
where the time goes:
time: 498 us; the launch traced here: 494 us
  local copies, waits for them, and re-layouts  188 us (38%)
  blocking collectives  162 us (33%)
  waiting for transfers between devices  65.6 us (13%)
  other arithmetic  32.3 us (6%)
  matrix products  30.1 us (6%)
  between operations  14.8 us (3%)
    all_to_all x1, blocking collectives, shards(): lax.all_to_all(jnp.take(to_atoms(fresh), order, axis=3), 'wide', split_ax...  86.6 us
    psum x1, blocking collectives, shards(): sum_x, sum_sq = lax.psum((trace_x, trace_sq), ('wide', 'narrow'))  75.5 us
    all_gather x1, waiting for transfers between devices, shards(): left_panels = lax.all_gather(blocks, 'narrow', axis=3, tiled=True)  65.6 us
    unnamed x24, local copies, waits for them, and re-layouts  43 us
    dot_general x9, matrix products, shards(): jnp.einsum('iab,ibc->iac', left_panels[:, offset + 1], nearby[1 + offset:...  30.1 us
    another operation x6, local copies, waits for them, and re-layouts, shards(): product = jnp.stack(pieces, axis=1)  27.9 us
    reshape x1, local copies, waits for them, and re-layouts, to_atoms(): jnp.transpose(shaped, (3, 1, 4, 0, 2))  18.9 us
    dynamic_slice x4, local copies, waits for them, and re-layouts, local_trace(): lax.dynamic_slice_in_dim(slab, narrow_pos * col_width, col_width, 1)  15.7 us
  transfers between devices with their start and end apart: 3, of which 1 were waited for; matrix products, arithmetic and copies ran while one was open for 6% of the time, Pallas kernels for 0%

commit v1 on v0

v1 whole, which is shorter than its diff:
```python
import functools
import jax
import jax.numpy as jnp
import numpy as np
from jax import lax
from jax.experimental import pallas as pl
from jax.experimental.pallas import tpu as pltpu
from jax.sharding import PartitionSpec as P

ORB = 9
ATOMS = 64
BLOCK = 576
PANEL = 144
LANES = 640
ROWS = 4
NARROW = 4
WIDE = 64
SLABS = 5
MAIN = 512
CHUNK = 1664
QUARTERS = ((0, 192), (192, 384), (384, 560), (560, 720))
F32 = jnp.float32
BF16 = jnp.bfloat16
VMEM_LIMIT = 58 * 1024 * 1024

VM = pl.BlockSpec(memory_space=pltpu.VMEM)
SM = pl.BlockSpec(memory_space=pltpu.SMEM)


def params():
    return pltpu.CompilerParams(vmem_limit_bytes=VMEM_LIMIT)


def one_hot(rows, cols, wanted):
    lanes = lax.broadcasted_iota(jnp.int32, (rows, cols), 1)
    return jnp.where(lanes == wanted, 1.0, 0.0).astype(BF16)


def lane_mask(link, first, shift):
    lanes = lax.broadcasted_iota(jnp.int32, (1, ROWS * ATOMS), 1) // ATOMS
    total = link.shape[0]
    mask = jnp.zeros((1, ROWS * ATOMS), F32)
    for r in range(ROWS):
        value = link[lax.rem(first + (r + shift + total), total)].astype(F32)
        mask = jnp.where(lanes == r, value, mask)
    return mask


def prep_kernel(link, pos, x, ga, gb, a_first, a_mid, a_last):
    first = pos[0] * ROWS
    masks = (
        lane_mask(link, first, -1).astype(BF16),
        None,
        lane_mask(link, first, 0).astype(BF16),
    )
    i = lax.broadcasted_iota(jnp.int32, (PANEL, PANEL), 0)
    c = lax.broadcasted_iota(jnp.int32, (PANEL, PANEL), 1)
    reorder = jnp.where(c == (i % 16) * ORB + i // 16, 1.0, 0.0).astype(BF16)
    zeros = jnp.zeros((PANEL, ATOMS), BF16)

    def row(tiles, r):
        parts = [t[:, r * ATOMS : (r + 1) * ATOMS] for t in tiles] + [zeros]
        return jnp.concatenate(parts, axis=1)

    for j in range(3):
        tiles = [x[j, o] for o in range(ORB)]
        if masks[j] is not None:
            tiles = [t * masks[j] for t in tiles]
        for r in range(ROWS):
            value = row(tiles, r)
            if r == 0:
                a_first[j] = value
            elif r == ROWS - 1:
                a_last[j] = value
            else:
                a_mid[r - 1, j] = value
            turned = None
            if j < 2 or r == ROWS - 1:
                turned = jnp.dot(reorder, value, preferred_element_type=F32).astype(BF16)
            if j == 0:
                ga[r] = turned
            elif j == 1:
                gb[r] = turned
            elif r == ROWS - 1:
                ga[ROWS] = turned


def trace_kernel(link, pos, x, out):
    first = pos[0] * ROWS
    narrow = pos[1]
    masks = (lane_mask(link, first, -1), None, lane_mask(link, first, 0))
    squares = jnp.zeros((PANEL, ROWS * ATOMS), F32)
    for j in range(3):
        total = jnp.zeros((PANEL, ROWS * ATOMS), F32)
        for o in range(ORB):
            t = x[j, o].astype(F32)
            total = total + t * t
        if masks[j] is not None:
            total = total * masks[j]
        squares = squares + total
    rows = lax.broadcasted_iota(jnp.int32, (PANEL, ROWS * ATOMS), 0) + narrow * PANEL
    lanes = lax.broadcasted_iota(jnp.int32, (PANEL, ROWS * ATOMS), 1) % ATOMS
    diagonal = jnp.zeros((PANEL, ROWS * ATOMS), F32)
    for o in range(ORB):
        diagonal = diagonal + jnp.where(rows == lanes * ORB + o, x[1, o].astype(F32), 0.0)
    sq = jnp.sum(squares, axis=0, keepdims=True)
    tx = jnp.sum(diagonal, axis=0, keepdims=True)
    sq = jnp.sum(sq, axis=1, keepdims=True)
    tx = jnp.sum(tx, axis=1, keepdims=True)
    lane = lax.broadcasted_iota(jnp.int32, (1, 128), 1)
    out[...] = jnp.where(lane == 0, tx, jnp.where(lane == 1, sq, 0.0))


def deal_kernel(want_quad, want_last, quad, last):
    step = 128
    for k in range(0, 1024, step):
        quad[k : k + step, :] = one_hot(step, 1024, want_quad[k : k + step, :])
        last[k : k + step, :] = one_hot(step, 1024, want_last[k : k + step, :])


def nt(a, b):
    return lax.dot_general(a, b, (((1,), (1,)), ((), ())), preferred_element_type=F32)


def tn(a, b):
    return lax.dot_general(a, b, (((0,), (0,)), ((), ())), preferred_element_type=F32)


def product_kernel(
    weight, pos,
    ga0, ga1, ga2, ga3, gb0, gb1, gb2, gb3,
    a_prev, a_first, a_mid, a_last, a_next, quad, last,
    out, full, acc, fresh, fresh_last,
):
    narrow = pos[1]
    twice = 2.0 * weight[0]
    for shift, (a, b) in enumerate(((ga0, gb0), (ga1, gb1), (ga2, gb2), (ga3, gb3))):
        owner = lax.rem(narrow + shift, NARROW)
        for p in range(9):
            src = a[p] if p < 5 else b[p - 5]
            full[p, :, pl.ds(owner, 1)] = src.reshape(ORB, 1, 16, LANES)
    lefts = [
        lambda j: a_prev[j],
        lambda j: a_first[j],
        lambda j: a_mid[0, j],
        lambda j: a_mid[1, j],
        lambda j: a_last[j],
        lambda j: a_next[j],
    ]

    def left(r):
        return jnp.concatenate([lefts[r + 1](j)[:, :BLOCK] for j in range(3)], axis=0)

    def block(p):
        return full[p].reshape(BLOCK, LANES)

    fresh_last[...] = jnp.zeros_like(fresh_last)
    for r in range(ROWS):
        acc[...] = jnp.zeros_like(acc)
        for d in range(-1, 2):
            stack = left(r + d)
            if d == -1:
                value = jnp.dot(stack, block(r), preferred_element_type=F32)
            elif d == 0:
                value = jnp.dot(stack, block(5 + r), preferred_element_type=F32)
            elif r < ROWS - 1:
                value = nt(stack, block(r + 1)[:, :BLOCK])
            else:
                value = jnp.dot(stack, block(4), preferred_element_type=F32)
            for j in range(3):
                e = d + j - 1
                piece = value[j * PANEL : (j + 1) * PANEL]
                if piece.shape[1] == BLOCK:
                    acc[e + 2, :, :BLOCK] += piece
                else:
                    acc[e + 2] += piece
        for s in range(SLABS):
            prod = acc[s]
            if 1 <= s <= 3:
                start = lefts[r + 1](s - 1).astype(F32)
                value = prod + twice * (start - prod)
            else:
                value = prod + twice * (0.0 - prod)
            fresh[s, :, r * MAIN : (r + 1) * MAIN] = value[:, :MAIN].astype(BF16)
            tail = value[:, MAIN:].astype(BF16)
            for q, (low, high) in enumerate(QUARTERS):
                begin, end = max(low, s * PANEL), min(high, (s + 1) * PANEL)
                if begin < end:
                    lane = q * 256 + r * ATOMS
                    fresh_last[begin - low : end - low, lane : lane + ATOMS] = tail[
                        begin - s * PANEL : end - s * PANEL, :ATOMS
                    ]
    rems = []
    for g in range(2):
        lanes = [slice(r * MAIN + g * 256, r * MAIN + g * 256 + 256) for r in range(ROWS)]
        main = jnp.concatenate([fresh[:, :128, l].reshape(SLABS * 128, 256) for l in lanes], axis=1)
        rem = jnp.concatenate([fresh[:, 128:, l].reshape(SLABS * 16, 256) for l in lanes], axis=1)
        out[:, g * 640 : (g + 1) * 640] = nt(quad[...], main).astype(BF16)
        rems.append(nt(quad[...], rem))
    rems.append(nt(last[...], fresh_last[...]))
    rems.append(jnp.zeros((1024, 32), F32))
    out[:, 1280:] = jnp.concatenate(rems, axis=1).astype(BF16)


def unpack_kernel(z, spread, out):
    for g in range(2):
        main = tn(z[:, g * 640 : (g + 1) * 640], spread[...]).astype(BF16)
        for q in range(4):
            for s in range(SLABS):
                out[g * 4 + q, s * PANEL : s * PANEL + 128, :] = main[
                    s * 128 : (s + 1) * 128, q * 256 : (q + 1) * 256
                ]
    rest = tn(z[:, 1280:], spread[...]).astype(BF16)
    for g in range(2):
        for q in range(4):
            for s in range(SLABS):
                out[g * 4 + q, s * PANEL + 128 : (s + 1) * PANEL, :] = rest[
                    g * 80 + s * 16 : g * 80 + s * 16 + 16, q * 256 : (q + 1) * 256
                ]
    for q, (low, high) in enumerate(QUARTERS):
        out[8, low:high, :] = rest[160 : 160 + high - low, q * 256 : (q + 1) * 256]


def spread_matrix():
    w, q, j = np.meshgrid(np.arange(64), np.arange(4), np.arange(4), indexing="ij")
    table = np.zeros((1024, 1024), np.float32)
    table[np.arange(1024), (q * 256 + w * 4 + j).reshape(-1)] = 1.0
    return table


def shift_perm(count, step):
    return [(i, (i - step) % count) for i in range(count)]


def total_sum(value):
    for axis, count, strides in (("narrow", 4, (1,)), ("wide", 64, (1, 4, 16))):
        for stride in strides:
            others = []
            for m in (1, 2, 3):
                perm = []
                for i in range(count):
                    digit = (i // stride) % 4
                    perm.append((i, i + (((digit + m) % 4) - digit) * stride))
                others.append(lax.ppermute(value, axis, perm))
            value = value + others[0] + others[1] + others[2]
    return value


def shards(xblk, link, order):
    wide_pos = lax.axis_index("wide")
    narrow_pos = lax.axis_index("narrow")
    pos = jnp.stack([wide_pos, narrow_pos]).astype(jnp.int32)
    x = jnp.transpose(xblk, (0, 2, 1, 3))
    sds = jax.ShapeDtypeStruct
    ga, gb, a_first, a_mid, a_last = pl.pallas_call(
        prep_kernel,
        out_shape=[
            sds((5, PANEL, LANES), BF16),
            sds((4, PANEL, LANES), BF16),
            sds((3, PANEL, LANES), BF16),
            sds((2, 3, PANEL, LANES), BF16),
            sds((3, PANEL, LANES), BF16),
        ],
        in_specs=[SM, SM, VM],
        out_specs=[VM] * 5,
        compiler_params=params(),
        name="prep",
    )(link, pos, x)
    gas, gbs = [ga], [gb]
    for step in (1, 2, 3):
        gas.append(lax.ppermute(ga, "narrow", shift_perm(NARROW, step)))
    a_prev = lax.ppermute(a_last, "wide", shift_perm(WIDE, -1))
    a_next = lax.ppermute(a_first, "wide", shift_perm(WIDE, 1))
    for step in (1, 2, 3):
        gbs.append(lax.ppermute(gb, "narrow", shift_perm(NARROW, step)))
    traces = pl.pallas_call(
        trace_kernel,
        out_shape=sds((1, 128), F32),
        in_specs=[SM, SM, VM],
        out_specs=VM,
        compiler_params=params(),
        name="traces",
    )(link, pos, x)
    sums = total_sum(traces)
    weight = jax.nn.sigmoid(4.0 * (sums[0, 0] - sums[0, 1]) / (link.shape[0] * BLOCK) + 5.0)
    wanted = jnp.broadcast_to(order.reshape(64, 1, 4), (64, 4, 4))
    quarter = jnp.arange(4, dtype=jnp.int32).reshape(1, 4, 1)
    want_quad = ((wanted // ATOMS) * 256 + quarter * ATOMS + wanted % ATOMS).reshape(1024, 1)
    want_last = (quarter * 256 + wanted).reshape(1024, 1)
    quad, last = pl.pallas_call(
        deal_kernel,
        out_shape=[sds((1024, 1024), BF16)] * 2,
        in_specs=[VM, VM],
        out_specs=[VM] * 2,
        compiler_params=params(),
        name="deal",
    )(want_quad, want_last)
    packed = pl.pallas_call(
        product_kernel,
        out_shape=sds((1024, CHUNK), BF16),
        in_specs=[SM, SM] + [VM] * 15,
        out_specs=VM,
        scratch_shapes=[
            pltpu.VMEM((9, ORB, NARROW, 16, LANES), BF16),
            pltpu.VMEM((SLABS, PANEL, LANES), F32),
            pltpu.VMEM((SLABS, PANEL, ROWS * MAIN), BF16),
            pltpu.VMEM((192, 1024), BF16),
        ],
        compiler_params=params(),
        name="product",
    )(weight.reshape(1), pos, *gas, *gbs, a_prev, a_first, a_mid, a_last, a_next, quad, last)
    received = lax.all_to_all(
        packed.reshape(WIDE, 16, CHUNK), "wide", split_axis=0, concat_axis=0, tiled=True
    )
    spread = jnp.asarray(spread_matrix(), BF16)
    out = pl.pallas_call(
        unpack_kernel,
        out_shape=sds((ORB, SLABS * PANEL, 256), BF16),
        in_specs=[VM, VM],
        out_specs=VM,
        compiler_params=params(),
        name="unpack",
    )(received.reshape(1024, CHUNK), spread)
    return out.reshape(ORB, SLABS, PANEL, 256)


def solution(mesh):
    return jax.shard_map(
        shards,
        mesh=mesh,
        in_specs=(P(None, "narrow", None, "wide"), P(), P("wide")),
        out_specs=P(None, None, "narrow", "wide"),
        check_vma=False,
    )
```

time: 498 us -> 233 us (0.47)
  local copies, waits for them, and re-layouts: 188 us -> 6.26 us
  blocking collectives: 162 us -> 87.4 us
  Pallas kernels: 0 us -> 37.4 us
  matrix products: 30.1 us -> 0 us
  other arithmetic: 32.3 us -> 2.8 us
  starting transfers between devices: 1.75 us -> 29.3 us
  between operations: 14.8 us -> 1.49 us
    psum x1 -> x0, blocking collectives: 75.5 us -> none  [shards(): sum_x, sum_sq = lax.psum((trace_x, trace_sq), ('wide', 'narrow'))]
    ppermute x2 -> x20, waiting for transfers between devices: 0.01 us -> 67.6 us  [the longest x3 54.5 us: shards(): gbs.append(lax.ppermute(gb, 'narrow', shift_perm(NARROW, step)))]
    all_gather x1 -> x0, waiting for transfers between devices: 65.6 us -> none  [shards(): left_panels = lax.all_gather(blocks, 'narrow', axis=3, tiled=True)]
    unnamed x24 -> x10, local copies, waits for them, and re-layouts: 43 us -> 1.61 us
    pallas_call x0 -> x5, Pallas kernels: none -> 37.4 us  [the longest x1 18.5 us: shards(): pl.pallas_call(product_kernel, out_shape=sds((1024, CHUNK), BF16), in_spe...]
    reshape x3 -> x0, local copies, waits for them, and re-layouts: 31.1 us -> none  [the longest x1 18.9 us: to_atoms(): jnp.transpose(shaped, (3, 1, 4, 0, 2))]
    dot_general x9 -> x0, matrix products: 30.1 us -> none  [shards(): jnp.einsum('iab,ibc->iac', left_panels[:, offset + 1], nearby[1 + offset:...]
    another operation x7 -> x0, local copies, waits for them, and re-layouts: 28 us -> none  [the longest x6 27.9 us: shards(): product = jnp.stack(pieces, axis=1)]
  transfers between devices with their start and end apart: 3 -> 20, of which waited for: 1 -> 9; matrix products, arithmetic and copies ran while one was open for 6% -> 3% of each run, Pallas kernels for 0% -> 3%
where the time goes in v1:
time: 233 us; the launch traced here: 232 us
  blocking collectives  87.4 us (38%)
  waiting for transfers between devices  67.6 us (29%)
  Pallas kernels  37.4 us (16%)
  starting transfers between devices  29.3 us (13%)
  local copies, waits for them, and re-layouts  6.26 us (3%)
  other arithmetic  2.8 us (1%)
    all_to_all x1, blocking collectives, shards(): lax.all_to_all(packed.reshape(WIDE, 16, CHUNK), 'wide', split_axis=0, con...  87.4 us
    ppermute x3, waiting for transfers between devices, shards(): gbs.append(lax.ppermute(gb, 'narrow', shift_perm(NARROW, step)))  54.5 us
    ppermute x12, starting transfers between devices, total_sum(): others.append(lax.ppermute(value, axis, perm))  20.6 us
    pallas_call x1, Pallas kernels, shards(): pl.pallas_call(product_kernel, out_shape=sds((1024, CHUNK), BF16), in_spe...  18.5 us
    ppermute x12, waiting for transfers between devices, total_sum(): others.append(lax.ppermute(value, axis, perm))  13.1 us
    pallas_call x1, Pallas kernels, shards(): pl.pallas_call(unpack_kernel, out_shape=sds((ORB, SLABS * PANEL, 256), BF...  8.04 us
  transfers between devices with their start and end apart: 20, of which 9 were waited for; matrix products, arithmetic and copies ran while one was open for 3% of the time, Pallas kernels for 3%

profile of v1, /device:TPU:8, one launch (start us, length us, event | category | flops | bytes accessed | tf_op | source)
XLA Modules:
  0.0 232.2 jit_solution(3639757506192642328)
XLA Ops:
  0.6 2.7 %traces.1 = f32[1,128]{1,0:T(1,128)} custom-call(s32[256]{0:T(256)} %link.3, s32[2]{0:T(128)} %pad_add_fusion.pos, bf16[3,9,144,256]{3,2,1,0:T(8,128)(2,1)} %bitcast.9), custom_call_target="tpu_custom_call" | custom-call | tf_op jit(solution)/shard_map/traces/pallas_call | solution.py:276
  3.3 2.8 %collective-permute-start.2 = (f32[1,128]{1,0:T(1,128)}, f32[1,128]{1,0:T(1,128)S(1)}, u32[]{:S(2)}, u32[]{:S(2)}) collective-permute-start(f32[1,128]{1,0:T(1,128)} %traces.1), channel_id=1, source_target_pairs={{0,3},{1,0},{2,1},{3,2},{4,7},{5,4},{6,5},{7,6},{8,11},{9,8},{10,9... | collective-permute-start | bytes 1544 | tf_op jit(solution)/shard_map/ppermute | solution.py:244
  6.0 0.8 collective-permute-start.1
  6.8 0.9 collective-permute-start
  7.7 3.5 %collective-permute-done.1 = f32[1,128]{1,0:T(1,128)S(1)} collective-permute-done((f32[1,128]{1,0:T(1,128)}, f32[1,128]{1,0:T(1,128)S(1)}, u32[]{:S(2)}, u32[]{:S(2)}) %collective-permute-start.1) | collective-permute-done | bytes 544 | tf_op jit(solution)/shard_map/ppermute | solution.py:244
  11.7 0.7 add_add_fusion.4
  13.7 2.2 collective-permute-done.4
  15.9 3.8 %collective-permute-start.8 = (f32[1,128]{1,0:T(1,128)S(1)}, f32[1,128]{1,0:T(1,128)S(1)}, u32[]{:S(2)}, u32[]{:S(2)}) collective-permute-start(f32[1,128]{1,0:T(1,128)S(1)} %add_add_fusion.3), channel_id=1, source_target_pairs={{0,48},{4,52},{8,56},{12,60},{16,0},{20,4},{24,8},{28,12},{32,16},... | collective-permute-start | bytes 1544 | tf_op jit(solution)/shard_map/ppermute | solution.py:244
  19.8 4.2 %prep.1 = (bf16[5,144,640]{2,1,0:T(8,128)(2,1)}, bf16[4,144,640]{2,1,0:T(8,128)(2,1)}, bf16[3,144,640]{2,1,0:T(8,128)(2,1)}, bf16[2,3,144,640]{3,2,1,0:T(8,128)(2,1)}, bf16[3,144,640]{2,1,0:T(8,128)(2,1)}) custom-call(s32[256]{0:T(256)} %link.3, s32[2]{0:T(128)} %pad_add_fusion.pos, bf16[3,9,144,256]{3,2,1,0:T(8,128)(2,1)} %bitcast.10), custom_call_target="tpu_custom_call" | custom-call | tf_op jit(solution)/shard_map/prep/pallas_call | solution.py:255
  24.1 1.6 collective-permute-start.6
  25.7 1.7 collective-permute-start.19
  27.6 2.4 %collective-permute-done.6 = f32[1,128]{1,0:T(1,128)S(1)} collective-permute-done((f32[1,128]{1,0:T(1,128)S(1)}, f32[1,128]{1,0:T(1,128)S(1)}, u32[]{:S(2)}, u32[]{:S(2)}) %collective-permute-start.6) | collective-permute-done | bytes 544 | tf_op jit(solution)/shard_map/ppermute | solution.py:244
  30.0 6.3 %collective-permute-start.11 = (f32[1,128]{1,0:T(1,128)S(1)}, f32[1,128]{1,0:T(1,128)S(1)}, u32[]{:S(2)}, u32[]{:S(2)}) collective-permute-start(f32[1,128]{1,0:T(1,128)S(1)} %add_add_fusion.2), channel_id=1, source_target_pairs={{0,192},{4,196},{8,200},{12,204},{16,208},{20,212},{24,216},{28,22... | collective-permute-start | bytes 1544 | tf_op jit(solution)/shard_map/ppermute | solution.py:244
  36.3 1.0 collective-permute-start.10
  37.6 2.6 %collective-permute-start.9 = (f32[1,128]{1,0:T(1,128)S(1)}, f32[1,128]{1,0:T(1,128)S(1)}, u32[]{:S(2)}, u32[]{:S(2)}) collective-permute-start(f32[1,128]{1,0:T(1,128)S(1)} %add_add_fusion.2), channel_id=1, source_target_pairs={{0,64},{4,68},{8,72},{12,76},{16,80},{20,84},{24,88},{28,92},{32,9... | collective-permute-start | bytes 1544 | tf_op jit(solution)/shard_map/ppermute | solution.py:244
  40.3 3.6 %collective-permute-done.10 = f32[1,128]{1,0:T(1,128)S(1)} collective-permute-done((f32[1,128]{1,0:T(1,128)S(1)}, f32[1,128]{1,0:T(1,128)S(1)}, u32[]{:S(2)}, u32[]{:S(2)}) %collective-permute-start.10) | collective-permute-done | bytes 544 | tf_op jit(solution)/shard_map/ppermute | solution.py:244
  43.9 1.8 collective-permute-start.13
  45.7 2.4 %collective-permute-start.12 = (bf16[5,144,640]{2,1,0:T(8,128)(2,1)}, bf16[5,144,640]{2,1,0:T(8,128)(2,1)S(1)}, u32[]{:S(2)}, u32[]{:S(2)}) collective-permute-start(bf16[5,144,640]{2,1,0:T(8,128)(2,1)} %get-tuple-element.12.ga0), channel_id=1, source_target_pairs={{0,3},{1,0},{2,1},{3,2},{4,7},{5,4},{6,5},{7,6},{8,11},{9,8},{10,9... | collective-permute-start | bytes 2764808 | tf_op jit(solution)/shard_map/ppermute | solution.py:271
  48.0 2.0 collective-permute-start.16
  50.0 0.7 collective-permute-start.15
  50.7 0.8 add_add_fusion
  51.5 2.0 reshape.180.want_quad
  53.5 0.7 broadcast_add_fusion
  54.2 1.9 add.122.want_last
  56.2 3.9 %deal.1 = (bf16[1024,1024]{1,0:T(8,128)(2,1)}, bf16[1024,1024]{1,0:T(8,128)(2,1)}) custom-call(s32[1024,1]{1,0:T(8,128)} %reshape.180.want_quad, s32[1024,1]{1,0:T(8,128)} %add.122.want_last), custom_call_target="tpu_custom_call" | custom-call | tf_op jit(solution)/shard_map/deal/pallas_call | solution.py:290
  60.1 0.6 fusion.1
  62.1 40.3 %collective-permute-done.16.gb2 = bf16[4,144,640]{2,1,0:T(8,128)(2,1)} collective-permute-done((bf16[4,144,640]{2,1,0:T(8,128)(2,1)}, bf16[4,144,640]{2,1,0:T(8,128)(2,1)}, u32[]{:S(2)}, u32[]{:S(2)}) %collective-permute-start.16) | collective-permute-done | bytes 737312 | tf_op jit(solution)/shard_map/ppermute | solution.py:275
  102.5 14.2 %collective-permute-done.15.gb1 = bf16[4,144,640]{2,1,0:T(8,128)(2,1)} collective-permute-done((bf16[4,144,640]{2,1,0:T(8,128)(2,1)}, bf16[4,144,640]{2,1,0:T(8,128)(2,1)}, u32[]{:S(2)}, u32[]{:S(2)}) %collective-permute-start.15) | collective-permute-done | bytes 737312 | tf_op jit(solution)/shard_map/ppermute | solution.py:275
  116.7 0.9 copy-done
  118.3 18.5 %product.1 = bf16[1024,1664]{1,0:T(8,128)(2,1)} custom-call(f32[1]{0:T(128)} %bitcast.3.weight, s32[2]{0:T(128)} %pad_add_fusion.pos, bf16[5,144,640]{2,1,0:T(8,128)(2,1)} %get-tuple-element.12.ga0, bf16[5,144,640]{2,1,0:T(8,128)(2,1)} %copy-done.2, bf16[5,144,640]{2,1,0:T(8,128)(2,1)} %copy-done.1, bf16[5,144,640]{2,1,0:T(8,128)(2,1)} %copy-done, ...), custom_call_target="tpu_custom_call" | custom-call | tf_op jit(solution)/shard_map/product/pallas_call | solution.py:298
  136.8 87.4 %all_to_all.5 = bf16[64,16,1664]{2,1,0:T(8,128)(2,1)} all-to-all(bf16[64,16,1664]{2,1,0:T(8,128)(2,1)} %bitcast.7), channel_id=1, replica_groups=mesh['wide'=64,'narrow'=4] {'wide'}, dimensions={0} | all-to-all | bytes 6815744 | tf_op jit(solution)/shard_map/all_to_all | solution.py:312
  224.1 8.0 %unpack.1 = bf16[9,720,256]{2,1,0:T(8,128)(2,1)} custom-call(bf16[1024,1664]{1,0:T(8,128)(2,1)} %bitcast.8, bf16[1024,1024]{1,0:T(8,128)(2,1)} %constant.56.clone.spread), custom_call_target="tpu_custom_call" | custom-call | tf_op jit(solution)/shard_map/unpack/pallas_call | solution.py:316
  (39 shorter events, 3.7 us)
Async XLA Ops:
  0.0 27.4 %copy-start.4 = (s32[256]{0:T(256)S(1)}, s32[256]{0:T(256)}, u32[]{:S(2)}) copy-start(s32[256]{0:T(256)} %param.6) | copy-start | bytes 3076
  3.3 4.4 %collective-permute-start.2 = (f32[1,128]{1,0:T(1,128)}, f32[1,128]{1,0:T(1,128)S(1)}, u32[]{:S(2)}, u32[]{:S(2)}) collective-permute-start(f32[1,128]{1,0:T(1,128)} %traces.1), channel_id=1, source_target_pairs={{0,3},{1,0},{2,1},{3,2},{4,7},{5,4},{6,5},{7,6},{8,11},{9,8},{10,9... | collective-permute-start | bytes 1544 | tf_op jit(solution)/shard_map/ppermute | solution.py:244
  6.0 5.2 %collective-permute-start.1 = (f32[1,128]{1,0:T(1,128)}, f32[1,128]{1,0:T(1,128)S(1)}, u32[]{:S(2)}, u32[]{:S(2)}) collective-permute-start(f32[1,128]{1,0:T(1,128)} %traces.1), channel_id=1, source_target_pairs={{0,2},{1,3},{2,0},{3,1},{4,6},{5,7},{6,4},{7,5},{8,10},{9,11},{10,... | collective-permute-start | bytes 1544 | tf_op jit(solution)/shard_map/ppermute | solution.py:244
  6.8 4.9 %collective-permute-start = (f32[1,128]{1,0:T(1,128)}, f32[1,128]{1,0:T(1,128)S(1)}, u32[]{:S(2)}, u32[]{:S(2)}) collective-permute-start(f32[1,128]{1,0:T(1,128)} %traces.1), channel_id=1, source_target_pairs={{0,1},{1,2},{2,3},{3,0},{4,5},{5,6},{6,7},{7,4},{8,9},{9,10},{10,1... | collective-permute-start | bytes 1544 | tf_op jit(solution)/shard_map/ppermute | solution.py:244
  12.4 1.3 collective-permute-start.5
  12.4 3.5 %collective-permute-start.4 = (f32[1,128]{1,0:T(1,128)S(1)}, f32[1,128]{1,0:T(1,128)S(1)}, u32[]{:S(2)}, u32[]{:S(2)}) collective-permute-start(f32[1,128]{1,0:T(1,128)S(1)} %add_add_fusion.4), channel_id=1, source_target_pairs={{0,8},{4,12},{8,0},{12,4},{16,24},{20,28},{24,16},{28,20},{32,40},... | collective-permute-start | bytes 1544 | tf_op jit(solution)/shard_map/ppermute | solution.py:244
  12.8 3.1 %collective-permute-start.3 = (f32[1,128]{1,0:T(1,128)S(1)}, f32[1,128]{1,0:T(1,128)S(1)}, u32[]{:S(2)}, u32[]{:S(2)}) collective-permute-start(f32[1,128]{1,0:T(1,128)S(1)} %add_add_fusion.4), channel_id=1, source_target_pairs={{0,4},{4,8},{8,12},{12,0},{16,20},{20,24},{24,28},{28,16},{32,36},... | collective-permute-start | bytes 1544 | tf_op jit(solution)/shard_map/ppermute | solution.py:244
  15.9 11.6 %collective-permute-start.8 = (f32[1,128]{1,0:T(1,128)S(1)}, f32[1,128]{1,0:T(1,128)S(1)}, u32[]{:S(2)}, u32[]{:S(2)}) collective-permute-start(f32[1,128]{1,0:T(1,128)S(1)} %add_add_fusion.3), channel_id=1, source_target_pairs={{0,48},{4,52},{8,56},{12,60},{16,0},{20,4},{24,8},{28,12},{32,16},... | collective-permute-start | bytes 1544 | tf_op jit(solution)/shard_map/ppermute | solution.py:244
  23.9 3.7 %collective-permute-start.7 = (f32[1,128]{1,0:T(1,128)S(1)}, f32[1,128]{1,0:T(1,128)S(1)}, u32[]{:S(2)}, u32[]{:S(2)}) collective-permute-start(f32[1,128]{1,0:T(1,128)S(1)} %add_add_fusion.3), channel_id=1, source_target_pairs={{0,32},{4,36},{8,40},{12,44},{16,48},{20,52},{24,56},{28,60},{32,0... | collective-permute-start | bytes 1544 | tf_op jit(solution)/shard_map/ppermute | solution.py:244
  24.1 5.9 %collective-permute-start.6 = (f32[1,128]{1,0:T(1,128)S(1)}, f32[1,128]{1,0:T(1,128)S(1)}, u32[]{:S(2)}, u32[]{:S(2)}) collective-permute-start(f32[1,128]{1,0:T(1,128)S(1)} %add_add_fusion.3), channel_id=1, source_target_pairs={{0,16},{4,20},{8,24},{12,28},{16,32},{20,36},{24,40},{28,44},{32,4... | collective-permute-start | bytes 1544 | tf_op jit(solution)/shard_map/ppermute | solution.py:244
  25.7 20.0 %collective-permute-start.18 = (bf16[3,144,640]{2,1,0:T(8,128)(2,1)}, bf16[3,144,640]{2,1,0:T(8,128)(2,1)}, u32[]{:S(2)}, u32[]{:S(2)}) collective-permute-start(bf16[3,144,640]{2,1,0:T(8,128)(2,1)} %get-tuple-element.14.a_last), channel_id=1, source_target_pairs={{0,4},{4,8},{8,12},{12,16},{16,20},{20,24},{24,28},{28,32},{32,36}... | collective-permute-start | bytes 1658888 | tf_op jit(solution)/shard_map/ppermute | solution.py:272
  25.7 22.4 %collective-permute-start.19 = (bf16[3,144,640]{2,1,0:T(8,128)(2,1)}, bf16[3,144,640]{2,1,0:T(8,128)(2,1)}, u32[]{:S(2)}, u32[]{:S(2)}) collective-permute-start(bf16[3,144,640]{2,1,0:T(8,128)(2,1)} %get-tuple-element.15.a_first), channel_id=1, source_target_pairs={{0,252},{4,0},{8,4},{12,8},{16,12},{20,16},{24,20},{28,24},{32,28}... | collective-permute-start | bytes 1658888 | tf_op jit(solution)/shard_map/ppermute | solution.py:273
  27.5 22.5 %collective-permute-start.17 = (bf16[4,144,640]{2,1,0:T(8,128)(2,1)}, bf16[4,144,640]{2,1,0:T(8,128)(2,1)S(1)}, u32[]{:S(2)}, u32[]{:S(2)}) collective-permute-start(bf16[4,144,640]{2,1,0:T(8,128)(2,1)} %get-tuple-element.13.gb0), channel_id=1, source_target_pairs={{0,1},{1,2},{2,3},{3,0},{4,5},{5,6},{6,7},{7,4},{8,9},{9,10},{10,1... | collective-permute-start | bytes 2211848 | tf_op jit(solution)/shard_map/ppermute | solution.py:275
  30.0 7.6 %collective-permute-start.11 = (f32[1,128]{1,0:T(1,128)S(1)}, f32[1,128]{1,0:T(1,128)S(1)}, u32[]{:S(2)}, u32[]{:S(2)}) collective-permute-start(f32[1,128]{1,0:T(1,128)S(1)} %add_add_fusion.2), channel_id=1, source_target_pairs={{0,192},{4,196},{8,200},{12,204},{16,208},{20,212},{24,216},{28,22... | collective-permute-start | bytes 1544 | tf_op jit(solution)/shard_map/ppermute | solution.py:244
  36.3 7.5 %collective-permute-start.10 = (f32[1,128]{1,0:T(1,128)S(1)}, f32[1,128]{1,0:T(1,128)S(1)}, u32[]{:S(2)}, u32[]{:S(2)}) collective-permute-start(f32[1,128]{1,0:T(1,128)S(1)} %add_add_fusion.2), channel_id=1, source_target_pairs={{0,128},{4,132},{8,136},{12,140},{16,144},{20,148},{24,152},{28,15... | collective-permute-start | bytes 1544 | tf_op jit(solution)/shard_map/ppermute | solution.py:244
  37.6 6.3 %collective-permute-start.9 = (f32[1,128]{1,0:T(1,128)S(1)}, f32[1,128]{1,0:T(1,128)S(1)}, u32[]{:S(2)}, u32[]{:S(2)}) collective-permute-start(f32[1,128]{1,0:T(1,128)S(1)} %add_add_fusion.2), channel_id=1, source_target_pairs={{0,64},{4,68},{8,72},{12,76},{16,80},{20,84},{24,88},{28,92},{32,9... | collective-permute-start | bytes 1544 | tf_op jit(solution)/shard_map/ppermute | solution.py:244
  43.9 72.8 %collective-permute-start.14 = (bf16[5,144,640]{2,1,0:T(8,128)(2,1)}, bf16[5,144,640]{2,1,0:T(8,128)(2,1)S(1)}, u32[]{:S(2)}, u32[]{:S(2)}) collective-permute-start(bf16[5,144,640]{2,1,0:T(8,128)(2,1)} %get-tuple-element.12.ga0), channel_id=1, source_target_pairs={{0,1},{1,2},{2,3},{3,0},{4,5},{5,6},{6,7},{7,4},{8,9},{9,10},{10,1... | collective-permute-start | bytes 2764808 | tf_op jit(solution)/shard_map/ppermute | solution.py:271
  43.9 72.8 %collective-permute-start.13 = (bf16[5,144,640]{2,1,0:T(8,128)(2,1)}, bf16[5,144,640]{2,1,0:T(8,128)(2,1)S(1)}, u32[]{:S(2)}, u32[]{:S(2)}) collective-permute-start(bf16[5,144,640]{2,1,0:T(8,128)(2,1)} %get-tuple-element.12.ga0), channel_id=1, source_target_pairs={{0,2},{1,3},{2,0},{3,1},{4,6},{5,7},{6,4},{7,5},{8,10},{9,11},{10,... | collective-permute-start | bytes 2764808 | tf_op jit(solution)/shard_map/ppermute | solution.py:271
  45.7 71.0 %collective-permute-start.12 = (bf16[5,144,640]{2,1,0:T(8,128)(2,1)}, bf16[5,144,640]{2,1,0:T(8,128)(2,1)S(1)}, u32[]{:S(2)}, u32[]{:S(2)}) collective-permute-start(bf16[5,144,640]{2,1,0:T(8,128)(2,1)} %get-tuple-element.12.ga0), channel_id=1, source_target_pairs={{0,3},{1,0},{2,1},{3,2},{4,7},{5,4},{6,5},{7,6},{8,11},{9,8},{10,9... | collective-permute-start | bytes 2764808 | tf_op jit(solution)/shard_map/ppermute | solution.py:271
  48.0 54.4 %collective-permute-start.16 = (bf16[4,144,640]{2,1,0:T(8,128)(2,1)}, bf16[4,144,640]{2,1,0:T(8,128)(2,1)}, u32[]{:S(2)}, u32[]{:S(2)}) collective-permute-start(bf16[4,144,640]{2,1,0:T(8,128)(2,1)} %get-tuple-element.13.gb0), channel_id=1, source_target_pairs={{0,2},{1,3},{2,0},{3,1},{4,6},{5,7},{6,4},{7,5},{8,10},{9,11},{10,... | collective-permute-start | bytes 2211848 | tf_op jit(solution)/shard_map/ppermute | solution.py:275
  50.0 66.6 %copy-start.3 = (bf16[4,144,640]{2,1,0:T(8,128)(2,1)}, bf16[4,144,640]{2,1,0:T(8,128)(2,1)S(1)}, u32[]{:S(2)}) copy-start(bf16[4,144,640]{2,1,0:T(8,128)(2,1)S(1)} %collective-permute-done.17.gb3) | copy-start | bytes 2211844
  50.0 66.6 %collective-permute-start.15 = (bf16[4,144,640]{2,1,0:T(8,128)(2,1)}, bf16[4,144,640]{2,1,0:T(8,128)(2,1)}, u32[]{:S(2)}, u32[]{:S(2)}) collective-permute-start(bf16[4,144,640]{2,1,0:T(8,128)(2,1)} %get-tuple-element.13.gb0), channel_id=1, source_target_pairs={{0,3},{1,0},{2,1},{3,2},{4,7},{5,4},{6,5},{7,6},{8,11},{9,8},{10,9... | collective-permute-start | bytes 2211848 | tf_op jit(solution)/shard_map/ppermute | solution.py:275
  116.6 0.9 copy-start
  116.6 1.3 copy-start.1
  116.6 1.6 copy-start.2

commit v2 on v1

v2 whole, which is shorter than its diff:
```python
import jax
import jax.numpy as jnp
import numpy as np
from jax import lax
from jax.experimental import pallas as pl
from jax.experimental.pallas import tpu as pltpu
from jax.sharding import PartitionSpec as P

ORB = 9
ATOMS = 64
BLOCK = 576
PANEL = 144
LANES = 640
ROWS = 4
NARROW = 4
WIDE = 64
MAIN = 512
OUTER_CHUNK = 640
INNER_CHUNK = 1024
INNER_QUARTERS = ((0, 112), (112, 224), (224, 336), (336, 432))
F32 = jnp.float32
BF16 = jnp.bfloat16
OUTER_FLOPS = 30 * 10**9
INNER_FLOPS = 70 * 10**9
VMEM_LIMIT = 56 * 1024 * 1024

VM = pl.BlockSpec(memory_space=pltpu.VMEM)
SM = pl.BlockSpec(memory_space=pltpu.SMEM)
ANY = pl.BlockSpec(memory_space=pl.ANY)
sds = jax.ShapeDtypeStruct


def params():
    return pltpu.CompilerParams(vmem_limit_bytes=VMEM_LIMIT)


def lane_mask(link, first, shift):
    lanes = lax.broadcasted_iota(jnp.int32, (1, ROWS * ATOMS), 1) // ATOMS
    total = link.shape[0]
    mask = jnp.zeros((1, ROWS * ATOMS), F32)
    for r in range(ROWS):
        value = link[lax.rem(first + (r + shift + total), total)].astype(F32)
        mask = jnp.where(lanes == r, value, mask)
    return mask


def reorder_matrix():
    i = lax.broadcasted_iota(jnp.int32, (PANEL, PANEL), 0)
    c = lax.broadcasted_iota(jnp.int32, (PANEL, PANEL), 1)
    return jnp.where(c == (i % 16) * ORB + i // 16, 1.0, 0.0).astype(BF16)


def packed_row(tiles, r, pad):
    parts = [t[:, r * ATOMS : (r + 1) * ATOMS] for t in tiles]
    if pad:
        parts.append(jnp.zeros((PANEL, ATOMS), BF16))
    return jnp.concatenate(parts, axis=1)


def put_panel(out, count, p, value):
    out[:, p * MAIN : (p + 1) * MAIN] = value[:, :MAIN]
    tail = count * MAIN + p * ATOMS
    out[:, tail : tail + ATOMS] = value[:, MAIN:BLOCK]


def prep_kernel(link, x, traces, ga, gb, a_first, a_mid, a_last):
    del traces
    first = lax.axis_index("wide") * ROWS
    masks = (
        lane_mask(link, first, -1).astype(BF16),
        None,
        lane_mask(link, first, 0).astype(BF16),
    )
    reorder = reorder_matrix()
    for j in range(3):
        tiles = [x[j, o] for o in range(ORB)]
        if masks[j] is not None:
            tiles = [t * masks[j] for t in tiles]
        for r in range(ROWS):
            value = packed_row(tiles, r, True)
            if r == 0:
                a_first[j] = value
            elif r == ROWS - 1:
                a_last[j] = value
            else:
                a_mid[r - 1, j] = value
            if j == 2 and r < ROWS - 1:
                continue
            turned = jnp.dot(reorder, value, preferred_element_type=F32).astype(BF16)
            if j == 1:
                put_panel(gb, ROWS, r, turned)
            else:
                put_panel(ga, ROWS + 1, r if j == 0 else ROWS, turned)
    ga[:, (ROWS + 1) * BLOCK :] = jnp.zeros((PANEL, ATOMS), BF16)


def trace_kernel(link, x, out):
    first = lax.axis_index("wide") * ROWS
    narrow = lax.axis_index("narrow")
    masks = (lane_mask(link, first, -1), None, lane_mask(link, first, 0))
    squares = jnp.zeros((PANEL, ROWS * ATOMS), F32)
    for j in range(3):
        total = jnp.zeros((PANEL, ROWS * ATOMS), F32)
        for o in range(ORB):
            t = x[j, o].astype(F32)
            total = total + t * t
        if masks[j] is not None:
            total = total * masks[j]
        squares = squares + total
    rows = lax.broadcasted_iota(jnp.int32, (PANEL, ROWS * ATOMS), 0) + narrow * PANEL
    lanes = lax.broadcasted_iota(jnp.int32, (PANEL, ROWS * ATOMS), 1) % ATOMS
    diagonal = jnp.zeros((PANEL, ROWS * ATOMS), F32)
    for o in range(ORB):
        diagonal = diagonal + jnp.where(rows == lanes * ORB + o, x[1, o].astype(F32), 0.0)
    sq = jnp.sum(squares, axis=0, keepdims=True)
    tx = jnp.sum(diagonal, axis=0, keepdims=True)
    sq = jnp.sum(sq, axis=1, keepdims=True)
    tx = jnp.sum(tx, axis=1, keepdims=True)
    lane = lax.broadcasted_iota(jnp.int32, (1, 128), 1)
    out[...] = jnp.where(lane == 0, tx, jnp.where(lane == 1, sq, 0.0))


def deal_kernel(wanted, quad):
    step = 128
    for k in range(0, 1024, step):
        lanes = lax.broadcasted_iota(jnp.int32, (step, 1024), 1)
        quad[k : k + step, :] = jnp.where(lanes == wanted[k : k + step, :], 1.0, 0.0).astype(BF16)


def nt(a, b):
    return lax.dot_general(a, b, (((1,), (1,)), ((), ())), preferred_element_type=F32)


def tn(a, b):
    return lax.dot_general(a, b, (((0,), (0,)), ((), ())), preferred_element_type=F32)


def twice_weight(sums, rows_total):
    total = jnp.sum(sums[...], axis=0)
    tx = total[:, 0:1]
    sq = total[:, 1:2]
    return 2.0 * jax.nn.sigmoid(4.0 * (tx - sq) / (rows_total * BLOCK) + 5.0)


def assemble(full, base, count, sources):
    narrow = lax.axis_index("narrow")
    for shift, src in enumerate(sources):
        owner = lax.rem(narrow + shift, NARROW)
        for p in range(count):
            value = src[:, p * MAIN : (p + 1) * MAIN]
            full[base + p, :, pl.ds(owner, 1), :, :MAIN] = value.reshape(
                ORB, 1, 16, MAIN
            )
            tail = count * MAIN + p * ATOMS
            value = src[:, tail : tail + ATOMS]
            full[base + p, :, pl.ds(owner, 1), :, MAIN:BLOCK] = value.reshape(
                ORB, 1, 16, ATOMS
            )


def deal(quad, fresh, group, slabs):
    lanes = [slice(r * MAIN + group * 256, r * MAIN + group * 256 + 256) for r in range(ROWS)]
    main = jnp.concatenate([fresh[:, :128, l].reshape(slabs * 128, 256) for l in lanes], axis=1)
    rem = jnp.concatenate([fresh[:, 128:, l].reshape(slabs * 16, 256) for l in lanes], axis=1)
    return nt(quad[...], main), nt(quad[...], rem)


def outer_kernel(
    rows_total, sums, ga0, ga1, ga2, ga3, a_prev, a_first, a_mid, a_last, a_next, quad,
    out, left_over, full, fresh, last,
):
    gas = (ga0, ga1, ga2, ga3)
    twice = twice_weight(sums, rows_total)
    assemble(full, 0, ROWS + 1, gas)
    lefts = [a_prev, a_first, a_mid.at[0], a_mid.at[1], a_last, a_next]
    left_over[...] = jnp.zeros_like(left_over)
    for r in range(ROWS):
        for s in range(2):
            if s == 0:
                b = full[r].reshape(BLOCK, LANES)
                prod = jnp.dot(lefts[r][0][:, :BLOCK], b, preferred_element_type=F32)
            elif r < ROWS - 1:
                b = full[r + 1].reshape(BLOCK, LANES)[:, :BLOCK]
                prod = nt(lefts[r + 2][2][:, :BLOCK], b)
            else:
                b = full[ROWS].reshape(BLOCK, LANES)
                prod = jnp.dot(lefts[r + 2][2][:, :BLOCK], b, preferred_element_type=F32)
            value = prod + twice * (0.0 - prod)
            fresh[s, :, r * MAIN : (r + 1) * MAIN] = value[:, :MAIN].astype(BF16)
            tail = value[:, MAIN:BLOCK].astype(BF16)
            for half in range(2):
                lane = r * 256 + (2 * s + half) * ATOMS
                last[:, lane : lane + ATOMS] = tail[half * 64 : half * 64 + 64]
            lane = r * 256 + s * ATOMS
            left_over[:, lane : lane + ATOMS] = tail[128:]
    rems = []
    for g in range(2):
        main, rem = deal(quad, fresh, g, 2)
        out[:, g * 256 : (g + 1) * 256] = main.astype(BF16)
        rems.append(rem)
    rems.append(nt(quad[...], last[...]))
    out[:, 512:] = jnp.concatenate(rems, axis=1).astype(BF16)


def inner_kernel(
    rows_total, sums, ga0, ga1, ga2, ga3, gb0, gb1, gb2, gb3,
    a_prev, a_first, a_mid, a_last, a_next, quad, left_over,
    out, full, acc, fresh, last,
):
    gas = (ga0, ga1, ga2, ga3)
    gbs = (gb0, gb1, gb2, gb3)
    twice = twice_weight(sums, rows_total)
    assemble(full, 0, ROWS + 1, gas)
    assemble(full, ROWS + 1, ROWS, gbs)
    lefts = [a_prev, a_first, a_mid.at[0], a_mid.at[1], a_last, a_next]

    def left(r, low, high):
        return jnp.concatenate([lefts[r + 1][j][:, :BLOCK] for j in range(low, high)], axis=0)

    last[112:, :] = left_over[...]
    last[96:112, :] = jnp.zeros((16, 1024), BF16)
    for r in range(ROWS):
        value = jnp.dot(
            left(r, 0, 3), full[ROWS + 1 + r].reshape(BLOCK, LANES), preferred_element_type=F32
        )
        for s in range(3):
            acc[s] = value[s * PANEL : (s + 1) * PANEL]
        value = jnp.dot(
            left(r - 1, 1, 3), full[r].reshape(BLOCK, LANES), preferred_element_type=F32
        )
        for s in range(2):
            acc[s] += value[s * PANEL : (s + 1) * PANEL]
        if r < ROWS - 1:
            value = nt(left(r + 1, 0, 2), full[r + 1].reshape(BLOCK, LANES)[:, :BLOCK])
        else:
            value = jnp.dot(
                left(r + 1, 0, 2), full[ROWS].reshape(BLOCK, LANES), preferred_element_type=F32
            )[:, :BLOCK]
        for s in range(2):
            acc[s + 1, :, :BLOCK] += value[s * PANEL : (s + 1) * PANEL]
        for s in range(3):
            prod = acc[s]
            value = prod + twice * (lefts[r + 1][s].astype(F32) - prod)
            fresh[s, :, r * MAIN : (r + 1) * MAIN] = value[:, :MAIN].astype(BF16)
            tail = value[:, MAIN:BLOCK].astype(BF16)
            for q, (low, high) in enumerate(INNER_QUARTERS):
                begin, end = max(low, s * PANEL), min(high, (s + 1) * PANEL)
                if begin < end:
                    lane = r * 256 + q * ATOMS
                    last[begin - low : end - low, lane : lane + ATOMS] = tail[
                        begin - s * PANEL : end - s * PANEL
                    ]
    rems = []
    for g in range(2):
        main, rem = deal(quad, fresh, g, 3)
        out[:, g * 384 : (g + 1) * 384] = main.astype(BF16)
        rems.append(rem)
    rems.append(nt(quad[...], last[...]))
    rems.append(jnp.zeros((1024, 32), F32))
    out[:, 768:] = jnp.concatenate(rems, axis=1).astype(BF16)


def unpack_outer_kernel(z, spread, out, held, sems):
    copies = []

    def send(o, s, high):
        row = s * 4 * PANEL
        copies.append(
            pltpu.make_async_copy(
                held.at[o, s, :high], out.at[o, row : row + high], sems.at[len(copies)]
            )
        )
        copies[-1].start()

    rest = tn(z[:, 512:], spread[...]).astype(BF16)
    for q in range(4):
        piece = rest[64:, q * 256 : (q + 1) * 256]
        held[8, q // 2, (q % 2) * 64 : (q % 2) * 64 + 64, :] = piece
    for s in range(2):
        send(8, s, 128)
    for g in range(2):
        main = tn(z[:, g * 256 : (g + 1) * 256], spread[...]).astype(BF16)
        for q in range(4):
            for s in range(2):
                lanes = slice(q * 256, (q + 1) * 256)
                held[4 * g + q, s, :128, :] = main[s * 128 : (s + 1) * 128, lanes]
                begin = g * 32 + s * 16
                held[4 * g + q, s, 128:, :] = rest[begin : begin + 16, lanes]
                send(4 * g + q, s, PANEL)
    for copy in copies:
        copy.wait()


def unpack_inner_kernel(z, spread, begun, out, held, edge, sems):
    del begun
    copies = []

    def send(src, dst):
        copies.append(pltpu.make_async_copy(src, dst, sems.at[len(copies)]))
        copies[-1].start()

    rest = tn(z[:, 768:], spread[...]).astype(BF16)
    for q, (low, high) in enumerate(INNER_QUARTERS):
        held[8, low:high, :] = rest[96 : 96 + high - low, q * 256 : (q + 1) * 256]
    send(held.at[8], out.at[8, PANEL : 4 * PANEL])
    for s in range(2):
        edge[s] = rest[208:224, s * 256 : (s + 1) * 256]
        row = s * 4 * PANEL + 128
        send(edge.at[s], out.at[8, row : row + 16])
    for g in range(2):
        main = tn(z[:, g * 384 : (g + 1) * 384], spread[...]).astype(BF16)
        for q in range(4):
            for s in range(3):
                lanes = slice(q * 256, (q + 1) * 256)
                held[4 * g + q, s * PANEL : s * PANEL + 128, :] = main[s * 128 : (s + 1) * 128, lanes]
                begin = g * 48 + s * 16
                held[4 * g + q, s * PANEL + 128 : (s + 1) * PANEL, :] = rest[begin : begin + 16, lanes]
            send(held.at[4 * g + q], out.at[4 * g + q, PANEL : 4 * PANEL])
    for copy in copies:
        copy.wait()


def spread_matrix():
    w, q, j = np.meshgrid(np.arange(64), np.arange(4), np.arange(4), indexing="ij")
    table = np.zeros((1024, 1024), np.float32)
    table[np.arange(1024), (q * 256 + w * 4 + j).reshape(-1)] = 1.0
    return table


def shift_perm(count, step):
    return [(i, (i - step) % count) for i in range(count)]


def gather(own):
    return [own] + [lax.ppermute(own, "narrow", shift_perm(NARROW, step)) for step in (1, 2, 3)]


def narrow_sum(value):
    first, *others = gather(value)
    return first + others[0] + others[1] + others[2]


def wide_copies(value):
    copies = jnp.broadcast_to(value.reshape(1, 1, 128), (WIDE, 1, 128))
    return lax.all_to_all(copies, "wide", split_axis=0, concat_axis=0, tiled=True)


def exchange(packed, chunk):
    parts = packed.reshape(WIDE, 16, chunk)
    got = lax.all_to_all(parts, "wide", split_axis=0, concat_axis=0, tiled=True)
    return got.reshape(1024, chunk)


def shards(xblk, link, order):
    rows_total = link.shape[0]
    x = jnp.transpose(xblk, (0, 2, 1, 3))
    traces = pl.pallas_call(
        trace_kernel,
        out_shape=sds((1, 128), F32),
        in_specs=[SM, VM],
        out_specs=VM,
        compiler_params=params(),
        name="traces",
    )(link, x)
    line = narrow_sum(traces)
    sums = wide_copies(line)
    ga, gb, a_first, a_mid, a_last = pl.pallas_call(
        prep_kernel,
        out_shape=[
            sds((PANEL, 2944), BF16),
            sds((PANEL, 2304), BF16),
            sds((3, PANEL, LANES), BF16),
            sds((2, 3, PANEL, LANES), BF16),
            sds((3, PANEL, LANES), BF16),
        ],
        in_specs=[SM, VM, ANY],
        out_specs=[VM] * 5,
        compiler_params=params(),
        name="prep",
    )(link, x, traces)
    ga, a_first, a_last, _ = lax.optimization_barrier((ga, a_first, a_last, line))
    gas = gather(ga)
    a_prev = lax.ppermute(a_last, "wide", shift_perm(WIDE, -1))
    a_next = lax.ppermute(a_first, "wide", shift_perm(WIDE, 1))
    wanted = jnp.broadcast_to(order.reshape(64, 1, 4), (64, 4, 4))
    quarter = jnp.arange(4, dtype=jnp.int32).reshape(1, 4, 1)
    wanted = ((wanted // ATOMS) * 256 + quarter * ATOMS + wanted % ATOMS).reshape(1024, 1)
    quad = pl.pallas_call(
        deal_kernel,
        out_shape=sds((1024, 1024), BF16),
        in_specs=[VM],
        out_specs=VM,
        compiler_params=params(),
        name="deal",
    )(wanted)
    gb, sums, quad, a_prev, a_next, *gas = lax.optimization_barrier(
        (gb, sums, quad, a_prev, a_next, *gas)
    )
    gbs = gather(gb)
    lefts = (a_prev, a_first, a_mid, a_last, a_next)
    packed_outer, left_over = pl.pallas_call(
        lambda *refs: outer_kernel(rows_total, *refs),
        out_shape=[sds((1024, OUTER_CHUNK), BF16), sds((16, 1024), BF16)],
        in_specs=[VM] * 11,
        out_specs=[VM, VM],
        scratch_shapes=[
            pltpu.VMEM((ROWS + 1, ORB, NARROW, 16, LANES), BF16),
            pltpu.VMEM((2, PANEL, ROWS * MAIN), BF16),
            pltpu.VMEM((64, 1024), BF16),
        ],
        compiler_params=params(),
        cost_estimate=pl.CostEstimate(
            flops=OUTER_FLOPS, bytes_accessed=8 << 20, transcendentals=0
        ),
        name="outer",
    )(sums, *gas, *lefts, quad)
    got_outer = exchange(packed_outer, OUTER_CHUNK)
    packed_inner = pl.pallas_call(
        lambda *refs: inner_kernel(rows_total, *refs),
        out_shape=sds((1024, INNER_CHUNK), BF16),
        in_specs=[VM] * 16,
        out_specs=VM,
        scratch_shapes=[
            pltpu.VMEM((2 * ROWS + 1, ORB, NARROW, 16, LANES), BF16),
            pltpu.VMEM((3, PANEL, LANES), F32),
            pltpu.VMEM((3, PANEL, ROWS * MAIN), BF16),
            pltpu.VMEM((128, 1024), BF16),
        ],
        compiler_params=params(),
        cost_estimate=pl.CostEstimate(
            flops=INNER_FLOPS, bytes_accessed=12 << 20, transcendentals=0
        ),
        name="inner",
    )(sums, *gas, *gbs, *lefts, quad, left_over)
    packed_inner, got_outer = lax.optimization_barrier((packed_inner, got_outer))
    got_inner = exchange(packed_inner, INNER_CHUNK)
    spread = jnp.asarray(spread_matrix(), BF16)
    out = pl.pallas_call(
        unpack_outer_kernel,
        out_shape=sds((ORB, 5 * PANEL, 256), BF16),
        in_specs=[VM, VM],
        out_specs=ANY,
        scratch_shapes=[
            pltpu.VMEM((ORB, 2, PANEL, 256), BF16),
            pltpu.SemaphoreType.DMA((18,)),
        ],
        compiler_params=params(),
        name="unpack_outer",
    )(got_outer, spread)
    out = pl.pallas_call(
        unpack_inner_kernel,
        out_shape=sds((ORB, 5 * PANEL, 256), BF16),
        in_specs=[VM, VM, ANY],
        out_specs=ANY,
        scratch_shapes=[
            pltpu.VMEM((ORB, 3 * PANEL, 256), BF16),
            pltpu.VMEM((2, 16, 256), BF16),
            pltpu.SemaphoreType.DMA((11,)),
        ],
        input_output_aliases={2: 0},
        compiler_params=params(),
        name="unpack_inner",
    )(got_inner, spread, out)
    return out.reshape(ORB, 5, PANEL, 256)


def solution(mesh):
    return jax.shard_map(
        shards,
        mesh=mesh,
        in_specs=(P(None, "narrow", None, "wide"), P(), P("wide")),
        out_specs=P(None, None, "narrow", "wide"),
        check_vma=False,
    )
```

time: 233 us -> 180 us (0.77)
  blocking collectives: 87.4 us -> 0 us
  waiting for transfers between devices: 67.6 us -> 83.5 us
  starting transfers between devices: 29.3 us -> 45 us
  Pallas kernels: 37.4 us -> 44.7 us
    all_to_all x1 -> x0, blocking collectives: 87.4 us -> none  [shards(): lax.all_to_all(packed.reshape(WIDE, 16, CHUNK), 'wide', split_axis=0, con...]
    all_to_all x0 -> x3, waiting for transfers between devices: none -> 63.9 us  [the longest x2 59.3 us: exchange(): got = lax.all_to_all(parts, 'wide', split_axis=0, concat_axis=0, tiled=True)]
    ppermute x18 -> x9, waiting for transfers between devices: 67.6 us -> 19.5 us  [gather(): lax.ppermute(own, 'narrow', shift_perm(NARROW, step))]
    all_to_all x0 -> x3, starting transfers between devices: none -> 30.4 us  [the longest x2 17.6 us: exchange(): got = lax.all_to_all(parts, 'wide', split_axis=0, concat_axis=0, tiled=True)]
    ppermute x18 -> x9, starting transfers between devices: 27.5 us -> 12.8 us  [gather(): lax.ppermute(own, 'narrow', shift_perm(NARROW, step))]
    pallas_call x4 -> x6, Pallas kernels: 34.6 us -> 41.9 us  [the longest x1 15.1 us: shards(): pl.pallas_call(lambda *refs: inner_kernel(rows_total, *refs), out_shape=s...]
  transfers between devices with their start and end apart: 20 -> 14, of which waited for: 9 -> 6; matrix products, arithmetic and copies ran while one was open for 3% -> 1% of each run, Pallas kernels for 3% -> 20%
where the time goes in v2:
time: 180 us; the launch traced here: 179 us
  waiting for transfers between devices  83.5 us (46%)
  starting transfers between devices  45 us (25%)
  Pallas kernels  44.7 us (25%)
  local copies, waits for them, and re-layouts  4.2 us (2%)
    all_to_all x2, waiting for transfers between devices, exchange(): got = lax.all_to_all(parts, 'wide', split_axis=0, concat_axis=0, tiled=True)  59.3 us
    ppermute x9, waiting for transfers between devices, gather(): lax.ppermute(own, 'narrow', shift_perm(NARROW, step))  19.5 us
    all_to_all x2, starting transfers between devices, exchange(): got = lax.all_to_all(parts, 'wide', split_axis=0, concat_axis=0, tiled=True)  17.6 us
    pallas_call x1, Pallas kernels, shards(): pl.pallas_call(lambda *refs: inner_kernel(rows_total, *refs), out_shape=s...  15.1 us
    all_to_all x1, starting transfers between devices, wide_copies(): lax.all_to_all(copies, 'wide', split_axis=0, concat_axis=0, tiled=True)  12.8 us
    ppermute x9, starting transfers between devices, gather(): lax.ppermute(own, 'narrow', shift_perm(NARROW, step))  12.8 us
    pallas_call x1, Pallas kernels, shards(): pl.pallas_call(lambda *refs: outer_kernel(rows_total, *refs), out_shape=[...  9.84 us
    pallas_call x1, Pallas kernels, shards(): pl.pallas_call(unpack_inner_kernel, out_shape=sds((ORB, 5 * PANEL, 256),...  5.52 us
  transfers between devices with their start and end apart: 14, of which 6 were waited for; matrix products, arithmetic and copies ran while one was open for 1% of the time, Pallas kernels for 20%

profile of v2, /device:TPU:8, one launch (start us, length us, event | category | flops | bytes accessed | tf_op | source)
XLA Modules:
  0.0 178.5 jit_solution(3673347307438968641)
XLA Ops:
  0.0 2.8 %traces.1 = f32[1,128]{1,0:T(1,128)} custom-call(s32[256]{0:T(256)} %link.3, bf16[3,9,144,256]{3,2,1,0:T(8,128)(2,1)} %bitcast.8), custom_call_target="tpu_custom_call" | custom-call | tf_op jit(solution)/shard_map/traces/pallas_call | solution.py:357
  2.8 1.5 collective-permute-start.2
  4.3 2.7 %collective-permute-start.1 = (f32[1,128]{1,0:T(1,128)}, f32[1,128]{1,0:T(1,128)S(1)}, u32[]{:S(2)}, u32[]{:S(2)}) collective-permute-start(f32[1,128]{1,0:T(1,128)} %traces.1), channel_id=1, source_target_pairs={{0,2},{1,3},{2,0},{3,1},{4,6},{5,7},{6,4},{7,5},{8,10},{9,11},{10,... | collective-permute-start | bytes 1544 | tf_op jit(solution)/shard_map/ppermute | solution.py:335
  7.0 1.4 collective-permute-start
  8.4 4.2 %prep.1 = (bf16[144,2944]{1,0:T(8,128)(2,1)}, bf16[144,2304]{1,0:T(8,128)(2,1)}, bf16[3,144,640]{2,1,0:T(8,128)(2,1)}, bf16[2,3,144,640]{3,2,1,0:T(8,128)(2,1)}, bf16[3,144,640]{2,1,0:T(8,128)(2,1)}) custom-call(s32[256]{0:T(256)} %link.3, bf16[3,9,144,256]{3,2,1,0:T(8,128)(2,1)} %bitcast.9, f32[1,128]{1,0:T(1,128)} %traces.1), custom_call_target="tpu_custom_call" | custom-call | tf_op jit(solution)/shard_map/prep/pallas_call | solution.py:367
  12.7 0.7 add_add_fusion.1
  13.4 0.6 collective-permute-start.7
  14.0 1.4 collective-permute-start.6
  15.4 1.2 collective-permute-start.5
  16.7 0.1 broadcast_in_dim.26
  16.9 1.7 collective-permute-start.4
  18.7 0.6 broadcast_in_dim.25
  19.3 12.8 %all-to-all-start = ((f32[64,1,128]{2,1,0:T(1,128)}), f32[64,1,128]{2,1,0:T(1,128)S(1)}, u32[]{:S(2)}, u32[]{:S(2)}) async-start(f32[64,1,128]{2,1,0:T(1,128)} %broadcast_in_dim.25), calls=%async_computation | async-start | bytes 65536 | tf_op jit(solution)/shard_map/all_to_all | solution.py:345
  32.1 0.1 add_add_fusion
  32.2 1.0 reshape.148.wanted
  33.2 2.8 %deal.1.refs_10_.refs_14_ = bf16[1024,1024]{1,0:T(8,128)(2,1)} custom-call(s32[1024,1]{1,0:T(8,128)} %reshape.148.wanted), custom_call_target="tpu_custom_call" | custom-call | tf_op jit(solution)/shard_map/deal/pallas_call | solution.py:388
  36.0 4.6 %all-to-all-done.refs_0_ = f32[64,1,128]{2,1,0:T(1,128)S(1)} async-done(((f32[64,1,128]{2,1,0:T(1,128)}), f32[64,1,128]{2,1,0:T(1,128)S(1)}, u32[]{:S(2)}, u32[]{:S(2)}) %all-to-all-start) | async-done | bytes 32800 | tf_op jit(solution)/shard_map/all_to_all | solution.py:345
  40.7 12.1 %collective-permute-done.7.refs_4_ = bf16[144,2944]{1,0:T(8,128)(2,1)S(1)} collective-permute-done((bf16[144,2944]{1,0:T(8,128)(2,1)}, bf16[144,2944]{1,0:T(8,128)(2,1)S(1)}, u32[]{:S(2)}, u32[]{:S(2)}) %collective-permute-start.7) | collective-permute-done | bytes 847904 | tf_op jit(solution)/shard_map/ppermute | solution.py:335
  52.8 0.6 collective-permute-done.5.refs_2_
  53.4 0.3 collective-permute-start.10
  53.7 3.6 %collective-permute-start.9 = (bf16[144,2304]{1,0:T(8,128)(2,1)S(1)}, bf16[144,2304]{1,0:T(8,128)(2,1)}, u32[]{:S(2)}, u32[]{:S(2)}) collective-permute-start(bf16[144,2304]{1,0:T(8,128)(2,1)S(1)} %copy-done.7), channel_id=1, source_target_pairs={{0,2},{1,3},{2,0},{3,1},{4,6},{5,7},{6,4},{7,5},{8,10},{9,11},{10,... | collective-permute-start | bytes 1990664 | tf_op jit(solution)/shard_map/ppermute | solution.py:335
  57.2 9.8 %outer.1 = (bf16[1024,640]{1,0:T(8,128)(2,1)}, bf16[16,1024]{1,0:T(8,128)(2,1)}) custom-call(f32[64,1,128]{2,1,0:T(1,128)} %copy-done.2, bf16[144,2944]{1,0:T(8,128)(2,1)} %get-tuple-element.34.refs_1_, bf16[144,2944]{1,0:T(8,128)(2,1)} %copy-done.6, bf16[144,2944]{1,0:T(8,128)(2,1)} %copy-done.5, bf16[144,2944]{1,0:T(8,128)(2,1)} %copy-done.4, ...), custom_call_target="tpu_custom_call" | custom-call | flops 30000001024 | bytes 8388608 | tf_op jit(solution)/shard_map/outer/pallas_call | solution.py:401
  67.1 12.1 %all-to-all-start.1 = ((bf16[64,16,640]{2,1,0:T(8,128)(2,1)}), bf16[64,16,640]{2,1,0:T(8,128)(2,1)S(1)}, u32[]{:S(2)}, u32[]{:S(2)}) async-start(bf16[64,16,640]{2,1,0:T(8,128)(2,1)} %bitcast.12), calls=%async_computation.1 | async-start | bytes 2621440 | tf_op jit(solution)/shard_map/all_to_all | solution.py:350
  79.2 6.8 %collective-permute-done.9.refs_7_ = bf16[144,2304]{1,0:T(8,128)(2,1)} collective-permute-done((bf16[144,2304]{1,0:T(8,128)(2,1)S(1)}, bf16[144,2304]{1,0:T(8,128)(2,1)}, u32[]{:S(2)}, u32[]{:S(2)}) %collective-permute-start.9) | collective-permute-done | bytes 663584 | tf_op jit(solution)/shard_map/ppermute | solution.py:335
  86.0 15.1 %inner.1 = bf16[1024,1024]{1,0:T(8,128)(2,1)} custom-call(f32[64,1,128]{2,1,0:T(1,128)} %copy-done.2, bf16[144,2944]{1,0:T(8,128)(2,1)} %get-tuple-element.34.refs_1_, bf16[144,2944]{1,0:T(8,128)(2,1)} %copy-done.6, bf16[144,2944]{1,0:T(8,128)(2,1)} %copy-done.5, bf16[144,2944]{1,0:T(8,128)(2,1)} %copy-done.4, bf16[144,2304]{1,0:T(8,128)(2,1)} %get-tuple-element.38.refs_5_, ...), custom_call_target="tpu_custom_call" | custom-call | flops 70000001024 | bytes 12582912 | tf_op jit(solution)/shard_map/inner/pallas_call | solution.py:418
  101.2 12.4 %all-to-all-done.1 = bf16[64,16,640]{2,1,0:T(8,128)(2,1)S(1)} async-done(((bf16[64,16,640]{2,1,0:T(8,128)(2,1)}), bf16[64,16,640]{2,1,0:T(8,128)(2,1)S(1)}, u32[]{:S(2)}, u32[]{:S(2)}) %all-to-all-start.1) | async-done | bytes 1310752 | tf_op jit(solution)/shard_map/all_to_all | solution.py:350
  113.6 1.1 copy-done.1
  114.7 5.5 %all-to-all-start.2 = ((bf16[64,16,1024]{2,1,0:T(8,128)(2,1)}), bf16[64,16,1024]{2,1,0:T(8,128)(2,1)S(1)}, u32[]{:S(2)}, u32[]{:S(2)}) async-start(bf16[64,16,1024]{2,1,0:T(8,128)(2,1)} %bitcast.11), calls=%async_computation.2 | async-start | bytes 4194304 | tf_op jit(solution)/shard_map/all_to_all | solution.py:350
  120.2 4.4 %unpack_outer.1.begun = bf16[9,720,256]{2,1,0:T(8,128)(2,1)} custom-call(bf16[1024,640]{1,0:T(8,128)(2,1)} %bitcast.10, bf16[1024,1024]{1,0:T(8,128)(2,1)} %constant.35.clone.spread), custom_call_target="tpu_custom_call" | custom-call | tf_op jit(solution)/shard_map/unpack_outer/pallas_call | solution.py:438
  124.6 46.8 %all-to-all-done.2 = bf16[64,16,1024]{2,1,0:T(8,128)(2,1)S(1)} async-done(((bf16[64,16,1024]{2,1,0:T(8,128)(2,1)}), bf16[64,16,1024]{2,1,0:T(8,128)(2,1)S(1)}, u32[]{:S(2)}, u32[]{:S(2)}) %all-to-all-start.2) | async-done | bytes 2097184 | tf_op jit(solution)/shard_map/all_to_all | solution.py:350
  171.5 1.3 copy-done
  172.8 5.5 %unpack_inner.1 = bf16[9,720,256]{2,1,0:T(8,128)(2,1)} custom-call(bf16[1024,1024]{1,0:T(8,128)(2,1)} %bitcast.7, bf16[1024,1024]{1,0:T(8,128)(2,1)} %constant.35.clone.spread, bf16[9,720,256]{2,1,0:T(8,128)(2,1)} %unpack_outer.1.begun), custom_call_target="tpu_custom_call", output_to_operand_aliasing={{}: (2, {})} | custom-call | tf_op jit(solution)/shard_map/unpack_inner/pallas_call | solution.py:450
  (27 shorter events, 0.2 us)
Async XLA Ops:
  0.0 16.7 %copy-start.3 = (s32[256]{0:T(256)S(1)}, s32[256]{0:T(256)}, u32[]{:S(2)}) copy-start(s32[256]{0:T(256)} %param.6) | copy-start | bytes 3076
  2.8 9.9 %collective-permute-start.2 = (f32[1,128]{1,0:T(1,128)}, f32[1,128]{1,0:T(1,128)S(1)}, u32[]{:S(2)}, u32[]{:S(2)}) collective-permute-start(f32[1,128]{1,0:T(1,128)} %traces.1), channel_id=1, source_target_pairs={{0,1},{1,2},{2,3},{3,0},{4,5},{5,6},{6,7},{7,4},{8,9},{9,10},{10,1... | collective-permute-start | bytes 1544 | tf_op jit(solution)/shard_map/ppermute | solution.py:335
  4.3 8.4 %collective-permute-start.1 = (f32[1,128]{1,0:T(1,128)}, f32[1,128]{1,0:T(1,128)S(1)}, u32[]{:S(2)}, u32[]{:S(2)}) collective-permute-start(f32[1,128]{1,0:T(1,128)} %traces.1), channel_id=1, source_target_pairs={{0,2},{1,3},{2,0},{3,1},{4,6},{5,7},{6,4},{7,5},{8,10},{9,11},{10,... | collective-permute-start | bytes 1544 | tf_op jit(solution)/shard_map/ppermute | solution.py:335
  7.0 5.7 %collective-permute-start = (f32[1,128]{1,0:T(1,128)}, f32[1,128]{1,0:T(1,128)S(1)}, u32[]{:S(2)}, u32[]{:S(2)}) collective-permute-start(f32[1,128]{1,0:T(1,128)} %traces.1), channel_id=1, source_target_pairs={{0,3},{1,0},{2,1},{3,2},{4,7},{5,4},{6,5},{7,6},{8,11},{9,8},{10,9... | collective-permute-start | bytes 1544 | tf_op jit(solution)/shard_map/ppermute | solution.py:335
  12.7 40.7 %copy-start.7 = (bf16[144,2304]{1,0:T(8,128)(2,1)S(1)}, bf16[144,2304]{1,0:T(8,128)(2,1)}, u32[]{:S(2)}) copy-start(bf16[144,2304]{1,0:T(8,128)(2,1)} %get-tuple-element.38.refs_5_) | copy-start | bytes 1990660
  13.4 39.3 %collective-permute-start.7 = (bf16[144,2944]{1,0:T(8,128)(2,1)}, bf16[144,2944]{1,0:T(8,128)(2,1)S(1)}, u32[]{:S(2)}, u32[]{:S(2)}) collective-permute-start(bf16[144,2944]{1,0:T(8,128)(2,1)} %get-tuple-element.34.refs_1_), channel_id=1, source_target_pairs={{0,1},{1,2},{2,3},{3,0},{4,5},{5,6},{6,7},{7,4},{8,9},{9,10},{10,1... | collective-permute-start | bytes 2543624 | tf_op jit(solution)/shard_map/ppermute | solution.py:335
  14.0 38.8 %collective-permute-start.6 = (bf16[144,2944]{1,0:T(8,128)(2,1)}, bf16[144,2944]{1,0:T(8,128)(2,1)S(1)}, u32[]{:S(2)}, u32[]{:S(2)}) collective-permute-start(bf16[144,2944]{1,0:T(8,128)(2,1)} %get-tuple-element.34.refs_1_), channel_id=1, source_target_pairs={{0,2},{1,3},{2,0},{3,1},{4,6},{5,7},{6,4},{7,5},{8,10},{9,11},{10,... | collective-permute-start | bytes 2543624 | tf_op jit(solution)/shard_map/ppermute | solution.py:335
  15.4 38.0 %collective-permute-start.5 = (bf16[144,2944]{1,0:T(8,128)(2,1)}, bf16[144,2944]{1,0:T(8,128)(2,1)S(1)}, u32[]{:S(2)}, u32[]{:S(2)}) collective-permute-start(bf16[144,2944]{1,0:T(8,128)(2,1)} %get-tuple-element.34.refs_1_), channel_id=1, source_target_pairs={{0,3},{1,0},{2,1},{3,2},{4,7},{5,4},{6,5},{7,6},{8,11},{9,8},{10,9... | collective-permute-start | bytes 2543624 | tf_op jit(solution)/shard_map/ppermute | solution.py:335
  16.8 23.8 %collective-permute-start.3 = (bf16[3,144,640]{2,1,0:T(8,128)(2,1)}, bf16[3,144,640]{2,1,0:T(8,128)(2,1)}, u32[]{:S(2)}, u32[]{:S(2)}) collective-permute-start(bf16[3,144,640]{2,1,0:T(8,128)(2,1)} %get-tuple-element.30.refs_8_.refs_12_), channel_id=1, source_target_pairs={{0,4},{4,8},{8,12},{12,16},{16,20},{20,24},{24,28},{28,32},{32,36}... | collective-permute-start | bytes 1658888 | tf_op jit(solution)/shard_map/ppermute | solution.py:383
  16.9 23.7 %collective-permute-start.4 = (bf16[3,144,640]{2,1,0:T(8,128)(2,1)}, bf16[3,144,640]{2,1,0:T(8,128)(2,1)}, u32[]{:S(2)}, u32[]{:S(2)}) collective-permute-start(bf16[3,144,640]{2,1,0:T(8,128)(2,1)} %get-tuple-element.31.refs_6_.refs_10_), channel_id=1, source_target_pairs={{0,252},{4,0},{8,4},{12,8},{16,12},{20,16},{24,20},{28,24},{32,28}... | collective-permute-start | bytes 1658888 | tf_op jit(solution)/shard_map/ppermute | solution.py:384
  19.3 21.4 %all-to-all-start = ((f32[64,1,128]{2,1,0:T(1,128)}), f32[64,1,128]{2,1,0:T(1,128)S(1)}, u32[]{:S(2)}, u32[]{:S(2)}) async-start(f32[64,1,128]{2,1,0:T(1,128)} %broadcast_in_dim.25), calls=%async_computation | async-start | bytes 65536 | tf_op jit(solution)/shard_map/all_to_all | solution.py:345
  40.6 16.6 %copy-start.2 = (f32[64,1,128]{2,1,0:T(1,128)}, f32[64,1,128]{2,1,0:T(1,128)S(1)}, u32[]{:S(2)}) copy-start(f32[64,1,128]{2,1,0:T(1,128)S(1)} %all-to-all-done.refs_0_) | copy-start | bytes 98308
  52.8 4.5 %copy-start.4 = (bf16[144,2944]{1,0:T(8,128)(2,1)}, bf16[144,2944]{1,0:T(8,128)(2,1)S(1)}, u32[]{:S(2)}) copy-start(bf16[144,2944]{1,0:T(8,128)(2,1)S(1)} %collective-permute-done.7.refs_4_) | copy-start | bytes 2543620
  52.8 4.5 %copy-start.5 = (bf16[144,2944]{1,0:T(8,128)(2,1)}, bf16[144,2944]{1,0:T(8,128)(2,1)S(1)}, u32[]{:S(2)}) copy-start(bf16[144,2944]{1,0:T(8,128)(2,1)S(1)} %collective-permute-done.6.refs_3_) | copy-start | bytes 2543620
  53.4 3.9 %copy-start.6 = (bf16[144,2944]{1,0:T(8,128)(2,1)}, bf16[144,2944]{1,0:T(8,128)(2,1)S(1)}, u32[]{:S(2)}) copy-start(bf16[144,2944]{1,0:T(8,128)(2,1)S(1)} %collective-permute-done.5.refs_2_) | copy-start | bytes 2543620
  53.4 25.8 %collective-permute-start.10 = (bf16[144,2304]{1,0:T(8,128)(2,1)S(1)}, bf16[144,2304]{1,0:T(8,128)(2,1)}, u32[]{:S(2)}, u32[]{:S(2)}) collective-permute-start(bf16[144,2304]{1,0:T(8,128)(2,1)S(1)} %copy-done.7), channel_id=1, source_target_pairs={{0,1},{1,2},{2,3},{3,0},{4,5},{5,6},{6,7},{7,4},{8,9},{9,10},{10,1... | collective-permute-start | bytes 1990664 | tf_op jit(solution)/shard_map/ppermute | solution.py:335
  53.7 32.4 %collective-permute-start.9 = (bf16[144,2304]{1,0:T(8,128)(2,1)S(1)}, bf16[144,2304]{1,0:T(8,128)(2,1)}, u32[]{:S(2)}, u32[]{:S(2)}) collective-permute-start(bf16[144,2304]{1,0:T(8,128)(2,1)S(1)} %copy-done.7), channel_id=1, source_target_pairs={{0,2},{1,3},{2,0},{3,1},{4,6},{5,7},{6,4},{7,5},{8,10},{9,11},{10,... | collective-permute-start | bytes 1990664 | tf_op jit(solution)/shard_map/ppermute | solution.py:335
  57.2 28.8 %collective-permute-start.8 = (bf16[144,2304]{1,0:T(8,128)(2,1)S(1)}, bf16[144,2304]{1,0:T(8,128)(2,1)}, u32[]{:S(2)}, u32[]{:S(2)}) collective-permute-start(bf16[144,2304]{1,0:T(8,128)(2,1)S(1)} %copy-done.7), channel_id=1, source_target_pairs={{0,3},{1,0},{2,1},{3,2},{4,7},{5,4},{6,5},{7,6},{8,11},{9,8},{10,9... | collective-permute-start | bytes 1990664 | tf_op jit(solution)/shard_map/ppermute | solution.py:335
  67.1 46.5 %all-to-all-start.1 = ((bf16[64,16,640]{2,1,0:T(8,128)(2,1)}), bf16[64,16,640]{2,1,0:T(8,128)(2,1)S(1)}, u32[]{:S(2)}, u32[]{:S(2)}) async-start(bf16[64,16,640]{2,1,0:T(8,128)(2,1)} %bitcast.12), calls=%async_computation.1 | async-start | bytes 2621440 | tf_op jit(solution)/shard_map/all_to_all | solution.py:350
  113.6 1.1 copy-start.1
  114.7 56.8 %all-to-all-start.2 = ((bf16[64,16,1024]{2,1,0:T(8,128)(2,1)}), bf16[64,16,1024]{2,1,0:T(8,128)(2,1)S(1)}, u32[]{:S(2)}, u32[]{:S(2)}) async-start(bf16[64,16,1024]{2,1,0:T(8,128)(2,1)} %bitcast.11), calls=%async_computation.2 | async-start | bytes 4194304 | tf_op jit(solution)/shard_map/all_to_all | solution.py:350
  171.5 1.3 copy-start

commit v3 on v2

--- a/solution.py
+++ b/solution.py
@@ -22,7 +22,6 @@
 BF16 = jnp.bfloat16
 OUTER_FLOPS = 30 * 10**9
 INNER_FLOPS = 70 * 10**9
-VMEM_LIMIT = 56 * 1024 * 1024
 
 VM = pl.BlockSpec(memory_space=pltpu.VMEM)
 SM = pl.BlockSpec(memory_space=pltpu.SMEM)
@@ -30,8 +29,8 @@
 sds = jax.ShapeDtypeStruct
 
 
-def params():
-    return pltpu.CompilerParams(vmem_limit_bytes=VMEM_LIMIT)
+def params(mib):
+    return pltpu.CompilerParams(vmem_limit_bytes=mib << 20)
 
 
 def lane_mask(link, first, shift):
@@ -63,40 +62,24 @@
     out[:, tail : tail + ATOMS] = value[:, MAIN:BLOCK]
 
 
-def prep_kernel(link, x, traces, ga, gb, a_first, a_mid, a_last):
-    del traces
+def prep_outer_kernel(link, low, high, ga):
     first = lax.axis_index("wide") * ROWS
-    masks = (
-        lane_mask(link, first, -1).astype(BF16),
-        None,
-        lane_mask(link, first, 0).astype(BF16),
-    )
+    before = lane_mask(link, first, -1).astype(BF16)
+    after = lane_mask(link, first, 0).astype(BF16)
     reorder = reorder_matrix()
-    for j in range(3):
-        tiles = [x[j, o] for o in range(ORB)]
-        if masks[j] is not None:
-            tiles = [t * masks[j] for t in tiles]
-        for r in range(ROWS):
-            value = packed_row(tiles, r, True)
-            if r == 0:
-                a_first[j] = value
-            elif r == ROWS - 1:
-                a_last[j] = value
-            else:
-                a_mid[r - 1, j] = value
-            if j == 2 and r < ROWS - 1:
-                continue
-            turned = jnp.dot(reorder, value, preferred_element_type=F32).astype(BF16)
-            if j == 1:
-                put_panel(gb, ROWS, r, turned)
-            else:
-                put_panel(ga, ROWS + 1, r if j == 0 else ROWS, turned)
+    tiles = [low[0, o] * before for o in range(ORB)]
+    for p in range(ROWS + 1):
+        if p == ROWS:
+            tiles = [high[0, o] * after for o in range(ORB)]
+        value = packed_row(tiles, min(p, ROWS - 1), False)
+        turned = jnp.dot(reorder, value, preferred_element_type=F32).astype(BF16)
+        put_panel(ga, ROWS + 1, p, turned)
     ga[:, (ROWS + 1) * BLOCK :] = jnp.zeros((PANEL, ATOMS), BF16)
 
 
-def trace_kernel(link, x, out):
+def prep_inner_kernel(link, x, ga, gb, a_first, a_mid, a_last, traces):
+    del ga
     first = lax.axis_index("wide") * ROWS
-    narrow = lax.axis_index("narrow")
     masks = (lane_mask(link, first, -1), None, lane_mask(link, first, 0))
     squares = jnp.zeros((PANEL, ROWS * ATOMS), F32)
     for j in range(3):
@@ -107,6 +90,7 @@
         if masks[j] is not None:
             total = total * masks[j]
         squares = squares + total
+    narrow = lax.axis_index("narrow")
     rows = lax.broadcasted_iota(jnp.int32, (PANEL, ROWS * ATOMS), 0) + narrow * PANEL
     lanes = lax.broadcasted_iota(jnp.int32, (PANEL, ROWS * ATOMS), 1) % ATOMS
     diagonal = jnp.zeros((PANEL, ROWS * ATOMS), F32)
@@ -117,7 +101,24 @@
     sq = jnp.sum(sq, axis=1, keepdims=True)
     tx = jnp.sum(tx, axis=1, keepdims=True)
     lane = lax.broadcasted_iota(jnp.int32, (1, 128), 1)
-    out[...] = jnp.where(lane == 0, tx, jnp.where(lane == 1, sq, 0.0))
+    value = jnp.where(lane == 0, tx, jnp.where(lane == 1, sq, 0.0))
+    traces[...] = jnp.broadcast_to(value.reshape(1, 1, 128), (WIDE, 1, 128))
+    reorder = reorder_matrix()
+    for j in range(3):
+        tiles = [x[j, o] for o in range(ORB)]
+        if masks[j] is not None:
+            tiles = [t * masks[j].astype(BF16) for t in tiles]
+        for r in range(ROWS):
+            value = packed_row(tiles, r, True)
+            if r == 0:
+                a_first[j] = value
+            elif r == ROWS - 1:
+                a_last[j] = value
+            else:
+                a_mid[r - 1, j] = value
+            if j == 1:
+                turned = jnp.dot(reorder, value, preferred_element_type=F32).astype(BF16)
+                put_panel(gb, ROWS, r, turned)
 
 
 def deal_kernel(wanted, quad):
@@ -136,7 +137,7 @@
 
 
 def twice_weight(sums, rows_total):
-    total = jnp.sum(sums[...], axis=0)
+    total = sums[0][...] + sums[1][...] + sums[2][...] + sums[3][...]
     tx = total[:, 0:1]
     sq = total[:, 1:2]
     return 2.0 * jax.nn.sigmoid(4.0 * (tx - sq) / (rows_total * BLOCK) + 5.0)
@@ -144,17 +145,21 @@
 
 def assemble(full, base, count, sources):
     narrow = lax.axis_index("narrow")
-    for shift, src in enumerate(sources):
+    if len(sources) == NARROW:
+        places = tuple((shift, 0, ORB) for shift in range(NARROW))
+    else:
+        places = ((0, 0, ORB), (1, 0, ORB), (2, 0, 5), (2, 5, 4), (3, 0, ORB))
+    for (shift, o, depth), src in zip(places, sources):
         owner = lax.rem(narrow + shift, NARROW)
         for p in range(count):
             value = src[:, p * MAIN : (p + 1) * MAIN]
-            full[base + p, :, pl.ds(owner, 1), :, :MAIN] = value.reshape(
-                ORB, 1, 16, MAIN
+            full[base + p, o : o + depth, pl.ds(owner, 1), :, :MAIN] = value.reshape(
+                depth, 1, 16, MAIN
             )
             tail = count * MAIN + p * ATOMS
             value = src[:, tail : tail + ATOMS]
-            full[base + p, :, pl.ds(owner, 1), :, MAIN:BLOCK] = value.reshape(
-                ORB, 1, 16, ATOMS
+            full[base + p, o : o + depth, pl.ds(owner, 1), :, MAIN:BLOCK] = value.reshape(
+                depth, 1, 16, ATOMS
             )
 
 
@@ -166,11 +171,11 @@
 
 
 def outer_kernel(
-    rows_total, sums, ga0, ga1, ga2, ga3, a_prev, a_first, a_mid, a_last, a_next, quad,
+    rows_total, sum0, sum1, sum2, sum3, ga0, ga1, ga2, ga3, ga4, a_prev, a_first, a_mid, a_last, a_next, quad,
     out, left_over, full, fresh, last,
 ):
-    gas = (ga0, ga1, ga2, ga3)
-    twice = twice_weight(sums, rows_total)
+    gas = (ga0, ga1, ga2, ga3, ga4)
+    twice = twice_weight((sum0, sum1, sum2, sum3), rows_total)
     assemble(full, 0, ROWS + 1, gas)
     lefts = [a_prev, a_first, a_mid.at[0], a_mid.at[1], a_last, a_next]
     left_over[...] = jnp.zeros_like(left_over)
@@ -203,13 +208,13 @@
 
 
 def inner_kernel(
-    rows_total, sums, ga0, ga1, ga2, ga3, gb0, gb1, gb2, gb3,
+    rows_total, sum0, sum1, sum2, sum3, ga0, ga1, ga2, ga3, ga4, gb0, gb1, gb2, gb3,
     a_prev, a_first, a_mid, a_last, a_next, quad, left_over,
     out, full, acc, fresh, last,
 ):
-    gas = (ga0, ga1, ga2, ga3)
+    gas = (ga0, ga1, ga2, ga3, ga4)
     gbs = (gb0, gb1, gb2, gb3)
-    twice = twice_weight(sums, rows_total)
+    twice = twice_weight((sum0, sum1, sum2, sum3), rows_total)
     assemble(full, 0, ROWS + 1, gas)
     assemble(full, ROWS + 1, ROWS, gbs)
     lefts = [a_prev, a_first, a_mid.at[0], a_mid.at[1], a_last, a_next]
@@ -331,18 +336,22 @@
     return [(i, (i - step) % count) for i in range(count)]
 
 
-def gather(own):
+def neighbours(own):
+    after = lax.ppermute(own, "narrow", shift_perm(NARROW, 1))
+    before = lax.ppermute(own, "narrow", shift_perm(NARROW, -1))
+    return after, before
+
+
+def opposite(after, before):
+    split = 80
+    top, bottom = lax.optimization_barrier((after[:split], before[split:]))
+    top = lax.ppermute(top, "narrow", shift_perm(NARROW, 1))
+    bottom = lax.ppermute(bottom, "narrow", shift_perm(NARROW, -1))
+    return top, bottom
+
+
+def direct_gather(own):
     return [own] + [lax.ppermute(own, "narrow", shift_perm(NARROW, step)) for step in (1, 2, 3)]
-
-
-def narrow_sum(value):
-    first, *others = gather(value)
-    return first + others[0] + others[1] + others[2]
-
-
-def wide_copies(value):
-    copies = jnp.broadcast_to(value.reshape(1, 1, 128), (WIDE, 1, 128))
-    return lax.all_to_all(copies, "wide", split_axis=0, concat_axis=0, tiled=True)
 
 
 def exchange(packed, chunk):
@@ -354,34 +363,42 @@
 def shards(xblk, link, order):
     rows_total = link.shape[0]
     x = jnp.transpose(xblk, (0, 2, 1, 3))
-    traces = pl.pallas_call(
-        trace_kernel,
-        out_shape=sds((1, 128), F32),
-        in_specs=[SM, VM],
-        out_specs=VM,
-        compiler_params=params(),
-        name="traces",
-    )(link, x)
-    line = narrow_sum(traces)
-    sums = wide_copies(line)
-    ga, gb, a_first, a_mid, a_last = pl.pallas_call(
-        prep_kernel,
+    slab = (1, ORB, PANEL, ROWS * ATOMS)
+    ga = pl.pallas_call(
+        prep_outer_kernel,
+        out_shape=sds((PANEL, 2944), BF16),
+        grid=(1,),
+        in_specs=[
+            SM,
+            pl.BlockSpec(slab, lambda i: (0, 0, 0, 0)),
+            pl.BlockSpec(slab, lambda i: (2, 0, 0, 0)),
+        ],
+        out_specs=pl.BlockSpec((PANEL, 2944), lambda i: (0, 0)),
+        compiler_params=params(48),
+        name="prep_outer",
+    )(link, x, x)
+    after, before = neighbours(ga)
+    gb, a_first, a_mid, a_last, traces = pl.pallas_call(
+        prep_inner_kernel,
         out_shape=[
-            sds((PANEL, 2944), BF16),
             sds((PANEL, 2304), BF16),
             sds((3, PANEL, LANES), BF16),
             sds((2, 3, PANEL, LANES), BF16),
             sds((3, PANEL, LANES), BF16),
+            sds((WIDE, 1, 128), F32),
         ],
         in_specs=[SM, VM, ANY],
         out_specs=[VM] * 5,
-        compiler_params=params(),
-        name="prep",
-    )(link, x, traces)
-    ga, a_first, a_last, _ = lax.optimization_barrier((ga, a_first, a_last, line))
-    gas = gather(ga)
+        compiler_params=params(48),
+        name="prep_inner",
+    )(link, x, ga)
     a_prev = lax.ppermute(a_last, "wide", shift_perm(WIDE, -1))
     a_next = lax.ppermute(a_first, "wide", shift_perm(WIDE, 1))
+    line = lax.all_to_all(traces, "wide", split_axis=0, concat_axis=0, tiled=True)
+    line = jnp.sum(line, axis=0)
+    sums = direct_gather(line)
+    after, before, a_prev, a_next = lax.optimization_barrier((after, before, a_prev, a_next))
+    gas = (ga, after, *opposite(after, before), before)
     wanted = jnp.broadcast_to(order.reshape(64, 1, 4), (64, 4, 4))
     quarter = jnp.arange(4, dtype=jnp.int32).reshape(1, 4, 1)
     wanted = ((wanted // ATOMS) * 256 + quarter * ATOMS + wanted % ATOMS).reshape(1024, 1)
@@ -390,35 +407,35 @@
         out_shape=sds((1024, 1024), BF16),
         in_specs=[VM],
         out_specs=VM,
-        compiler_params=params(),
+        compiler_params=params(8),
         name="deal",
     )(wanted)
-    gb, sums, quad, a_prev, a_next, *gas = lax.optimization_barrier(
-        (gb, sums, quad, a_prev, a_next, *gas)
+    gb, quad, a_prev, a_next, sums, gas = lax.optimization_barrier(
+        (gb, quad, a_prev, a_next, sums, gas)
     )
-    gbs = gather(gb)
+    gbs = direct_gather(gb)
     lefts = (a_prev, a_first, a_mid, a_last, a_next)
     packed_outer, left_over = pl.pallas_call(
         lambda *refs: outer_kernel(rows_total, *refs),
         out_shape=[sds((1024, OUTER_CHUNK), BF16), sds((16, 1024), BF16)],
-        in_specs=[VM] * 11,
+        in_specs=[VM] * 15,
         out_specs=[VM, VM],
         scratch_shapes=[
             pltpu.VMEM((ROWS + 1, ORB, NARROW, 16, LANES), BF16),
             pltpu.VMEM((2, PANEL, ROWS * MAIN), BF16),
             pltpu.VMEM((64, 1024), BF16),
         ],
-        compiler_params=params(),
+        compiler_params=params(24),
         cost_estimate=pl.CostEstimate(
             flops=OUTER_FLOPS, bytes_accessed=8 << 20, transcendentals=0
         ),
         name="outer",
-    )(sums, *gas, *lefts, quad)
+    )(*sums, *gas, *lefts, quad)
     got_outer = exchange(packed_outer, OUTER_CHUNK)
     packed_inner = pl.pallas_call(
         lambda *refs: inner_kernel(rows_total, *refs),
         out_shape=sds((1024, INNER_CHUNK), BF16),
-        in_specs=[VM] * 16,
+        in_specs=[VM] * 20,
         out_specs=VM,
         scratch_shapes=[
             pltpu.VMEM((2 * ROWS + 1, ORB, NARROW, 16, LANES), BF16),
@@ -426,12 +443,12 @@
             pltpu.VMEM((3, PANEL, ROWS * MAIN), BF16),
             pltpu.VMEM((128, 1024), BF16),
         ],
-        compiler_params=params(),
+        compiler_params=params(54),
         cost_estimate=pl.CostEstimate(
             flops=INNER_FLOPS, bytes_accessed=12 << 20, transcendentals=0
         ),
         name="inner",
-    )(sums, *gas, *gbs, *lefts, quad, left_over)
+    )(*sums, *gas, *gbs, *lefts, quad, left_over)
     packed_inner, got_outer = lax.optimization_barrier((packed_inner, got_outer))
     got_inner = exchange(packed_inner, INNER_CHUNK)
     spread = jnp.asarray(spread_matrix(), BF16)
@@ -444,7 +461,7 @@
             pltpu.VMEM((ORB, 2, PANEL, 256), BF16),
             pltpu.SemaphoreType.DMA((18,)),
         ],
-        compiler_params=params(),
+        compiler_params=params(14),
         name="unpack_outer",
     )(got_outer, spread)
     out = pl.pallas_call(
@@ -458,7 +475,7 @@
             pltpu.SemaphoreType.DMA((11,)),
         ],
         input_output_aliases={2: 0},
-        compiler_params=params(),
+        compiler_params=params(16),
         name="unpack_inner",
     )(got_inner, spread, out)
     return out.reshape(ORB, 5, PANEL, 256)

time: 180 us -> 163 us (0.906)
  waiting for transfers between devices: 83.5 us -> 71.4 us
  Pallas kernels: 44.7 us -> 35 us
  starting transfers between devices: 45 us -> 47.9 us
  local copies, waits for them, and re-layouts: 4.2 us -> 6.88 us
    ppermute x9 -> x10, waiting for transfers between devices: 19.5 us -> 8.6 us  [the longest x6 8.59 us: direct_gather(): lax.ppermute(own, 'narrow', shift_perm(NARROW, step))]
    ppermute x9 -> x10, starting transfers between devices: 12.8 us -> 16.3 us  [the longest x6 9.72 us: direct_gather(): lax.ppermute(own, 'narrow', shift_perm(NARROW, step))]
    pallas_call x2, Pallas kernels: 6.99 us -> 4.3 us  [the longest x1 3.18 us: shards(): pl.pallas_call(prep_inner_kernel, out_shape=[sds((PANEL, 2304), BF16), sd...]
    pallas_call x1, Pallas kernels: 2.77 us -> 0.4 us  [shards(): pl.pallas_call(deal_kernel, out_shape=sds((1024, 1024), BF16), in_specs=[...]
    pallas_call x1, Pallas kernels: 9.84 us -> 7.86 us  [shards(): pl.pallas_call(lambda *refs: outer_kernel(rows_total, *refs), out_shape=[...]
    pallas_call x1, Pallas kernels: 4.4 us -> 2.41 us  [shards(): pl.pallas_call(unpack_outer_kernel, out_shape=sds((ORB, 5 * PANEL, 256),...]
    unnamed x16 -> x34, local copies, waits for them, and re-layouts: 2.45 us -> 3.9 us
  transfers between devices with their start and end apart: 14 -> 15, of which waited for: 6 -> 5; matrix products, arithmetic and copies ran while one was open for 1% -> 2% of each run, Pallas kernels for 20% -> 18%
where the time goes in v3:
time: 163 us
  waiting for transfers between devices  71.4 us (44%)
  starting transfers between devices  47.9 us (29%)
  Pallas kernels  35 us (21%)
  local copies, waits for them, and re-layouts  6.88 us (4%)
    all_to_all x2, waiting for transfers between devices, exchange(): got = lax.all_to_all(parts, 'wide', split_axis=0, concat_axis=0, tiled=True)  59.6 us
    all_to_all x2, starting transfers between devices, exchange(): got = lax.all_to_all(parts, 'wide', split_axis=0, concat_axis=0, tiled=True)  17.1 us
    pallas_call x1, Pallas kernels, shards(): pl.pallas_call(lambda *refs: inner_kernel(rows_total, *refs), out_shape=s...  15.1 us
    all_to_all x1, starting transfers between devices, shards(): lax.all_to_all(traces, 'wide', split_axis=0, concat_axis=0, tiled=True)  12.8 us
    ppermute x6, starting transfers between devices, direct_gather(): lax.ppermute(own, 'narrow', shift_perm(NARROW, step))  9.72 us
    ppermute x6, waiting for transfers between devices, direct_gather(): lax.ppermute(own, 'narrow', shift_perm(NARROW, step))  8.59 us
    pallas_call x1, Pallas kernels, shards(): pl.pallas_call(lambda *refs: outer_kernel(rows_total, *refs), out_shape=[...  7.86 us
    pallas_call x1, Pallas kernels, shards(): pl.pallas_call(unpack_inner_kernel, out_shape=sds((ORB, 5 * PANEL, 256),...  4.9 us
  transfers between devices with their start and end apart: 15, of which 5 were waited for; matrix products, arithmetic and copies ran while one was open for 2% of the time, Pallas kernels for 18%

profile of v3, /device:TPU:8, one launch (start us, length us, event | category | flops | bytes accessed | tf_op | source)
XLA Modules:
  0.0 162.6 jit_solution(14597419253812002538)
XLA Ops:
  0.0 1.6 copy-done
  1.6 0.7 copy-done.6
  2.2 1.1 prep_outer.1.ga.refs_4_
  3.4 1.6 collective-permute-start.1
  4.9 1.7 %collective-permute-start = (bf16[144,2944]{1,0:T(8,128)(2,1)S(1)}, bf16[144,2944]{1,0:T(8,128)(2,1)S(1)}, u32[]{:S(2)}, u32[]{:S(2)}) collective-permute-start(bf16[144,2944]{1,0:T(8,128)(2,1)S(1)} %prep_outer.1.ga.refs_4_), channel_id=1, source_target_pairs={{0,3},{1,0},{2,1},{3,2},{4,7},{5,4},{6,5},{7,6},{8,11},{9,8},{10,9... | collective-permute-start | bytes 2543624 | tf_op jit(solution)/shard_map/ppermute | solution.py:340
  6.7 3.2 %prep_inner.1 = (bf16[144,2304]{1,0:T(8,128)(2,1)}, bf16[3,144,640]{2,1,0:T(8,128)(2,1)}, bf16[2,3,144,640]{3,2,1,0:T(8,128)(2,1)S(1)}, bf16[3,144,640]{2,1,0:T(8,128)(2,1)}, f32[64,1,128]{2,1,0:T(1,128)}) custom-call(s32[256]{0:T(256)S(1)} %copy-done.7, bf16[3,9,144,256]{3,2,1,0:T(8,128)(2,1)S(1)} %bitcast.9, bf16[144,2944]{1,0:T(8,128)(2,1)S(1)} %prep_outer.1.ga.refs_4_), custom_call_target="tpu_custom_call" | custom-call | tf_op jit(solution)/shard_map/prep_inner/pallas_call | solution.py:381
  9.9 1.0 copy-done.9
  10.9 1.7 %collective-permute-start.3 = (bf16[3,144,640]{2,1,0:T(8,128)(2,1)}, bf16[3,144,640]{2,1,0:T(8,128)(2,1)}, u32[]{:S(2)}, u32[]{:S(2)}) collective-permute-start(bf16[3,144,640]{2,1,0:T(8,128)(2,1)} %get-tuple-element.35.refs_10_.refs_14_), channel_id=1, source_target_pairs={{0,252},{4,0},{8,4},{12,8},{16,12},{20,16},{24,20},{28,24},{32,28}... | collective-permute-start | bytes 1658888 | tf_op jit(solution)/shard_map/ppermute | solution.py:396
  12.6 12.8 %all-to-all-start = ((f32[64,1,128]{2,1,0:T(1,128)}), f32[64,1,128]{2,1,0:T(1,128)S(1)}, u32[]{:S(2)}, u32[]{:S(2)}) async-start(f32[64,1,128]{2,1,0:T(1,128)} %get-tuple-element.38), calls=%async_computation | async-start | bytes 65536 | tf_op jit(solution)/shard_map/all_to_all | solution.py:397
  25.6 0.9 slice.7
  26.6 0.9 slice.6
  27.4 1.1 collective-permute-start.8
  28.5 2.2 %collective-permute-start.7 = (bf16[80,2944]{1,0:T(8,128)(2,1)}, bf16[80,2944]{1,0:T(8,128)(2,1)S(1)}, u32[]{:S(2)}, u32[]{:S(2)}) collective-permute-start(bf16[80,2944]{1,0:T(8,128)(2,1)} %slice.6), channel_id=1, source_target_pairs={{0,3},{1,0},{2,1},{3,2},{4,7},{5,4},{6,5},{7,6},{8,11},{9,8},{10,9... | collective-permute-start | bytes 1413128 | tf_op jit(solution)/shard_map/ppermute | solution.py:348
  30.7 3.3 %all-to-all-done = f32[64,1,128]{2,1,0:T(1,128)S(1)} async-done(((f32[64,1,128]{2,1,0:T(1,128)}), f32[64,1,128]{2,1,0:T(1,128)S(1)}, u32[]{:S(2)}, u32[]{:S(2)}) %all-to-all-start) | async-done | bytes 32800 | tf_op jit(solution)/shard_map/all_to_all | solution.py:397
  34.0 0.4 collective-permute-start.6
  34.4 2.7 %collective-permute-start.5 = (f32[1,128]{1,0:T(1,128)S(1)}, f32[1,128]{1,0:T(1,128)S(1)}, u32[]{:S(2)}, u32[]{:S(2)}) collective-permute-start(f32[1,128]{1,0:T(1,128)S(1)} %bitcast.12), channel_id=1, source_target_pairs={{0,2},{1,3},{2,0},{3,1},{4,6},{5,7},{6,4},{7,5},{8,10},{9,11},{10,... | collective-permute-start | bytes 1544 | tf_op jit(solution)/shard_map/ppermute | solution.py:354
  37.1 1.4 collective-permute-start.4
  38.6 0.8 add_add_fusion
  39.3 1.1 reshape.145.wanted
  40.5 0.4 deal.1.refs_14_.refs_18_
  41.1 1.6 collective-permute-start.11
  42.7 3.6 %collective-permute-start.10 = (bf16[144,2304]{1,0:T(8,128)(2,1)}, bf16[144,2304]{1,0:T(8,128)(2,1)}, u32[]{:S(2)}, u32[]{:S(2)}) collective-permute-start(bf16[144,2304]{1,0:T(8,128)(2,1)} %get-tuple-element.52.refs_9_), channel_id=1, source_target_pairs={{0,2},{1,3},{2,0},{3,1},{4,6},{5,7},{6,4},{7,5},{8,10},{9,11},{10,... | collective-permute-start | bytes 1990664 | tf_op jit(solution)/shard_map/ppermute | solution.py:354
  46.3 7.9 %outer.1 = (bf16[1024,640]{1,0:T(8,128)(2,1)}, bf16[16,1024]{1,0:T(8,128)(2,1)S(1)}) custom-call(f32[1,128]{1,0:T(1,128)S(1)} %bitcast.14, f32[1,128]{1,0:T(1,128)S(1)} %collective-permute-done.4.refs_1_, f32[1,128]{1,0:T(1,128)S(1)} %collective-permute-done.5.refs_2_, f32[1,128]{1,0:T(1,128)S(1)} %collective-permute-done.6.refs_3_, ...), custom_call_target="tpu_custom_call" | custom-call | flops 30000001024 | bytes 8388608 | tf_op jit(solution)/shard_map/outer/pallas_call | solution.py:418
  54.2 0.6 copy-done.15
  54.8 11.3 %all-to-all-start.1 = ((bf16[64,16,640]{2,1,0:T(8,128)(2,1)}), bf16[64,16,640]{2,1,0:T(8,128)(2,1)S(1)}, u32[]{:S(2)}, u32[]{:S(2)}) async-start(bf16[64,16,640]{2,1,0:T(8,128)(2,1)} %bitcast.2), calls=%async_computation.1 | async-start | bytes 2621440 | tf_op jit(solution)/shard_map/all_to_all | solution.py:359
  66.1 8.4 %collective-permute-done.10.refs_11_ = bf16[144,2304]{1,0:T(8,128)(2,1)} collective-permute-done((bf16[144,2304]{1,0:T(8,128)(2,1)}, bf16[144,2304]{1,0:T(8,128)(2,1)}, u32[]{:S(2)}, u32[]{:S(2)}) %collective-permute-start.10) | collective-permute-done | bytes 663584 | tf_op jit(solution)/shard_map/ppermute | solution.py:354
  74.5 15.1 %inner.1 = bf16[1024,1024]{1,0:T(8,128)(2,1)} custom-call(f32[1,128]{1,0:T(1,128)} %bitcast.15, f32[1,128]{1,0:T(1,128)} %copy-done.14, f32[1,128]{1,0:T(1,128)} %copy-done.13, f32[1,128]{1,0:T(1,128)} %copy-done.12, bf16[144,2944]{1,0:T(8,128)(2,1)} %copy-done.2, bf16[144,2944]{1,0:T(8,128)(2,1)} %copy-done.4, bf16[80,2944]{1,0:T(8,128)(2,1)} %copy-done.11, ...), custom_call_target="tpu_custom_call" | custom-call | flops 70000001024 | bytes 12582912 | tf_op jit(solution)/shard_map/inner/pallas_call | solution.py:435
  89.7 10.9 %all-to-all-done.1 = bf16[64,16,640]{2,1,0:T(8,128)(2,1)S(1)} async-done(((bf16[64,16,640]{2,1,0:T(8,128)(2,1)}), bf16[64,16,640]{2,1,0:T(8,128)(2,1)S(1)}, u32[]{:S(2)}, u32[]{:S(2)}) %all-to-all-start.1) | async-done | bytes 1310752 | tf_op jit(solution)/shard_map/all_to_all | solution.py:359
  100.5 5.9 %all-to-all-start.2 = ((bf16[64,16,1024]{2,1,0:T(8,128)(2,1)}), bf16[64,16,1024]{2,1,0:T(8,128)(2,1)}, u32[]{:S(2)}, u32[]{:S(2)}) async-start(bf16[64,16,1024]{2,1,0:T(8,128)(2,1)} %bitcast.16), calls=%async_computation.2 | async-start | bytes 4194304 | tf_op jit(solution)/shard_map/all_to_all | solution.py:359
  106.4 2.4 %unpack_outer.1.begun = bf16[9,720,256]{2,1,0:T(8,128)(2,1)} custom-call(bf16[1024,640]{1,0:T(8,128)(2,1)S(1)} %bitcast.10, bf16[1024,1024]{1,0:T(8,128)(2,1)S(1)} %copy-done.1), custom_call_target="tpu_custom_call" | custom-call | tf_op jit(solution)/shard_map/unpack_outer/pallas_call | solution.py:455
  108.8 48.7 %all-to-all-done.2 = bf16[64,16,1024]{2,1,0:T(8,128)(2,1)} async-done(((bf16[64,16,1024]{2,1,0:T(8,128)(2,1)}), bf16[64,16,1024]{2,1,0:T(8,128)(2,1)}, u32[]{:S(2)}, u32[]{:S(2)}) %all-to-all-start.2) | async-done | bytes 2097184 | tf_op jit(solution)/shard_map/all_to_all | solution.py:359
  157.5 4.9 %unpack_inner.1 = bf16[9,720,256]{2,1,0:T(8,128)(2,1)} custom-call(bf16[1024,1024]{1,0:T(8,128)(2,1)} %bitcast.5.z, bf16[1024,1024]{1,0:T(8,128)(2,1)S(1)} %copy-done.1, bf16[9,720,256]{2,1,0:T(8,128)(2,1)} %unpack_outer.1.begun), custom_call_target="tpu_custom_call", output_to_operand_aliasing={{}: (2, {})} | custom-call | tf_op jit(solution)/shard_map/unpack_inner/pallas_call | solution.py:467
  (48 shorter events, 0.5 us)
Async XLA Ops:
  0.0 1.6 copy-start
  1.6 0.7 copy-start.6
  2.2 4.5 %copy-start.7 = (s32[256]{0:T(256)S(1)}, s32[256]{0:T(256)}, u32[]{:S(2)}) copy-start(s32[256]{0:T(256)} %link.3) | copy-start | bytes 3076
  3.4 42.9 %copy-start.2 = (bf16[144,2944]{1,0:T(8,128)(2,1)}, bf16[144,2944]{1,0:T(8,128)(2,1)S(1)}, u32[]{:S(2)}) copy-start(bf16[144,2944]{1,0:T(8,128)(2,1)S(1)} %prep_outer.1.ga.refs_4_) | copy-start | bytes 2543620
  3.4 22.1 %copy-start.16 = (s32[256]{0:T(256)S(1)}, s32[256]{0:T(256)}, u32[]{:S(2)}) copy-start(s32[256]{0:T(256)} %param.6) | copy-start | bytes 3076
  3.4 22.2 %collective-permute-start.1 = (bf16[144,2944]{1,0:T(8,128)(2,1)S(1)}, bf16[144,2944]{1,0:T(8,128)(2,1)S(1)}, u32[]{:S(2)}, u32[]{:S(2)}) collective-permute-start(bf16[144,2944]{1,0:T(8,128)(2,1)S(1)} %prep_outer.1.ga.refs_4_), channel_id=1, source_target_pairs={{0,1},{1,2},{2,3},{3,0},{4,5},{5,6},{6,7},{7,4},{8,9},{9,10},{10,1... | collective-permute-start | bytes 2543624 | tf_op jit(solution)/shard_map/ppermute | solution.py:341
  4.9 20.7 %collective-permute-start = (bf16[144,2944]{1,0:T(8,128)(2,1)S(1)}, bf16[144,2944]{1,0:T(8,128)(2,1)S(1)}, u32[]{:S(2)}, u32[]{:S(2)}) collective-permute-start(bf16[144,2944]{1,0:T(8,128)(2,1)S(1)} %prep_outer.1.ga.refs_4_), channel_id=1, source_target_pairs={{0,3},{1,0},{2,1},{3,2},{4,7},{5,4},{6,5},{7,6},{8,11},{9,8},{10,9... | collective-permute-start | bytes 2543624 | tf_op jit(solution)/shard_map/ppermute | solution.py:340
  9.9 1.0 copy-start.9
  10.9 14.7 %collective-permute-start.2 = (bf16[3,144,640]{2,1,0:T(8,128)(2,1)}, bf16[3,144,640]{2,1,0:T(8,128)(2,1)}, u32[]{:S(2)}, u32[]{:S(2)}) collective-permute-start(bf16[3,144,640]{2,1,0:T(8,128)(2,1)} %get-tuple-element.34.refs_12_.refs_16_), channel_id=1, source_target_pairs={{0,4},{4,8},{8,12},{12,16},{16,20},{20,24},{24,28},{28,32},{32,36}... | collective-permute-start | bytes 1658888 | tf_op jit(solution)/shard_map/ppermute | solution.py:395
  10.9 14.7 %collective-permute-start.3 = (bf16[3,144,640]{2,1,0:T(8,128)(2,1)}, bf16[3,144,640]{2,1,0:T(8,128)(2,1)}, u32[]{:S(2)}, u32[]{:S(2)}) collective-permute-start(bf16[3,144,640]{2,1,0:T(8,128)(2,1)} %get-tuple-element.35.refs_10_.refs_14_), channel_id=1, source_target_pairs={{0,252},{4,0},{8,4},{12,8},{16,12},{20,16},{24,20},{28,24},{32,28}... | collective-permute-start | bytes 1658888 | tf_op jit(solution)/shard_map/ppermute | solution.py:396
  12.6 21.3 %all-to-all-start = ((f32[64,1,128]{2,1,0:T(1,128)}), f32[64,1,128]{2,1,0:T(1,128)S(1)}, u32[]{:S(2)}, u32[]{:S(2)}) async-start(f32[64,1,128]{2,1,0:T(1,128)} %get-tuple-element.38), calls=%async_computation | async-start | bytes 65536 | tf_op jit(solution)/shard_map/all_to_all | solution.py:397
  25.6 20.7 %copy-start.5 = (bf16[144,2944]{1,0:T(8,128)(2,1)}, bf16[144,2944]{1,0:T(8,128)(2,1)S(1)}, u32[]{:S(2)}) copy-start(bf16[144,2944]{1,0:T(8,128)(2,1)S(1)} %collective-permute-done.1.refs_8_) | copy-start | bytes 2543620
  25.6 20.7 %copy-start.4 = (bf16[144,2944]{1,0:T(8,128)(2,1)}, bf16[144,2944]{1,0:T(8,128)(2,1)S(1)}, u32[]{:S(2)}) copy-start(bf16[144,2944]{1,0:T(8,128)(2,1)S(1)} %collective-permute-done.refs_5_) | copy-start | bytes 2543620
  27.4 13.7 %collective-permute-start.8 = (bf16[64,2944]{1,0:T(8,128)(2,1)}, bf16[64,2944]{1,0:T(8,128)(2,1)}, u32[]{:S(2)}, u32[]{:S(2)}) collective-permute-start(bf16[64,2944]{1,0:T(8,128)(2,1)} %slice.7), channel_id=1, source_target_pairs={{0,1},{1,2},{2,3},{3,0},{4,5},{5,6},{6,7},{7,4},{8,9},{9,10},{10,1... | collective-permute-start | bytes 1130504 | tf_op jit(solution)/shard_map/ppermute | solution.py:349
  28.5 12.6 %collective-permute-start.7 = (bf16[80,2944]{1,0:T(8,128)(2,1)}, bf16[80,2944]{1,0:T(8,128)(2,1)S(1)}, u32[]{:S(2)}, u32[]{:S(2)}) collective-permute-start(bf16[80,2944]{1,0:T(8,128)(2,1)} %slice.6), channel_id=1, source_target_pairs={{0,3},{1,0},{2,1},{3,2},{4,7},{5,4},{6,5},{7,6},{8,11},{9,8},{10,9... | collective-permute-start | bytes 1413128 | tf_op jit(solution)/shard_map/ppermute | solution.py:348
  34.0 20.1 %copy-start.8 = (f32[128]{0:T(128)}, f32[128]{0:T(128)S(1)}, u32[]{:S(2)}) copy-start(f32[128]{0:T(128)S(1)} %reduce_sum.11) | copy-start | bytes 1540
  34.0 6.8 %collective-permute-start.6 = (f32[1,128]{1,0:T(1,128)S(1)}, f32[1,128]{1,0:T(1,128)S(1)}, u32[]{:S(2)}, u32[]{:S(2)}) collective-permute-start(f32[1,128]{1,0:T(1,128)S(1)} %bitcast.11), channel_id=1, source_target_pairs={{0,1},{1,2},{2,3},{3,0},{4,5},{5,6},{6,7},{7,4},{8,9},{9,10},{10,1... | collective-permute-start | bytes 1544 | tf_op jit(solution)/shard_map/ppermute | solution.py:354
  34.4 6.5 %collective-permute-start.5 = (f32[1,128]{1,0:T(1,128)S(1)}, f32[1,128]{1,0:T(1,128)S(1)}, u32[]{:S(2)}, u32[]{:S(2)}) collective-permute-start(f32[1,128]{1,0:T(1,128)S(1)} %bitcast.12), channel_id=1, source_target_pairs={{0,2},{1,3},{2,0},{3,1},{4,6},{5,7},{6,4},{7,5},{8,10},{9,11},{10,... | collective-permute-start | bytes 1544 | tf_op jit(solution)/shard_map/ppermute | solution.py:354
  37.1 3.9 %collective-permute-start.4 = (f32[1,128]{1,0:T(1,128)S(1)}, f32[1,128]{1,0:T(1,128)S(1)}, u32[]{:S(2)}, u32[]{:S(2)}) collective-permute-start(f32[1,128]{1,0:T(1,128)S(1)} %bitcast.13), channel_id=1, source_target_pairs={{0,3},{1,0},{2,1},{3,2},{4,7},{5,4},{6,5},{7,6},{8,11},{9,8},{10,9... | collective-permute-start | bytes 1544 | tf_op jit(solution)/shard_map/ppermute | solution.py:354
  40.4 5.9 %copy-start.10 = (bf16[2,3,144,640]{3,2,1,0:T(8,128)(2,1)S(1)}, bf16[2,3,144,640]{3,2,1,0:T(8,128)(2,1)}, u32[]{:S(2)}) copy-start(bf16[2,3,144,640]{3,2,1,0:T(8,128)(2,1)} %copy-done.9) | copy-start | bytes 3317764
  40.9 13.3 %copy-start.3 = (bf16[1024,1024]{1,0:T(8,128)(2,1)}, bf16[1024,1024]{1,0:T(8,128)(2,1)S(1)}, u32[]{:S(2)}) copy-start(bf16[1024,1024]{1,0:T(8,128)(2,1)S(1)} %deal.1.refs_14_.refs_18_) | copy-start | bytes 6291460
  40.9 13.3 %copy-start.12 = (f32[1,128]{1,0:T(1,128)}, f32[1,128]{1,0:T(1,128)S(1)}, u32[]{:S(2)}) copy-start(f32[1,128]{1,0:T(1,128)S(1)} %collective-permute-done.6.refs_3_) | copy-start | bytes 1540
  40.9 13.3 %copy-start.13 = (f32[1,128]{1,0:T(1,128)}, f32[1,128]{1,0:T(1,128)S(1)}, u32[]{:S(2)}) copy-start(f32[1,128]{1,0:T(1,128)S(1)} %collective-permute-done.5.refs_2_) | copy-start | bytes 1540
  41.1 13.1 %copy-start.14 = (f32[1,128]{1,0:T(1,128)}, f32[1,128]{1,0:T(1,128)S(1)}, u32[]{:S(2)}) copy-start(f32[1,128]{1,0:T(1,128)S(1)} %collective-permute-done.4.refs_1_) | copy-start | bytes 1540
  41.1 13.1 %copy-start.11 = (bf16[80,2944]{1,0:T(8,128)(2,1)}, bf16[80,2944]{1,0:T(8,128)(2,1)S(1)}, u32[]{:S(2)}) copy-start(bf16[80,2944]{1,0:T(8,128)(2,1)S(1)} %collective-permute-done.7.refs_6_) | copy-start | bytes 1413124
  41.1 25.0 %collective-permute-start.11 = (bf16[144,2304]{1,0:T(8,128)(2,1)}, bf16[144,2304]{1,0:T(8,128)(2,1)}, u32[]{:S(2)}, u32[]{:S(2)}) collective-permute-start(bf16[144,2304]{1,0:T(8,128)(2,1)} %get-tuple-element.52.refs_9_), channel_id=1, source_target_pairs={{0,1},{1,2},{2,3},{3,0},{4,5},{5,6},{6,7},{7,4},{8,9},{9,10},{10,1... | collective-permute-start | bytes 1990664 | tf_op jit(solution)/shard_map/ppermute | solution.py:354
  42.7 31.8 %collective-permute-start.10 = (bf16[144,2304]{1,0:T(8,128)(2,1)}, bf16[144,2304]{1,0:T(8,128)(2,1)}, u32[]{:S(2)}, u32[]{:S(2)}) collective-permute-start(bf16[144,2304]{1,0:T(8,128)(2,1)} %get-tuple-element.52.refs_9_), channel_id=1, source_target_pairs={{0,2},{1,3},{2,0},{3,1},{4,6},{5,7},{6,4},{7,5},{8,10},{9,11},{10,... | collective-permute-start | bytes 1990664 | tf_op jit(solution)/shard_map/ppermute | solution.py:354
  46.3 28.3 %collective-permute-start.9 = (bf16[144,2304]{1,0:T(8,128)(2,1)}, bf16[144,2304]{1,0:T(8,128)(2,1)}, u32[]{:S(2)}, u32[]{:S(2)}) collective-permute-start(bf16[144,2304]{1,0:T(8,128)(2,1)} %get-tuple-element.52.refs_9_), channel_id=1, source_target_pairs={{0,3},{1,0},{2,1},{3,2},{4,7},{5,4},{6,5},{7,6},{8,11},{9,8},{10,9... | collective-permute-start | bytes 1990664 | tf_op jit(solution)/shard_map/ppermute | solution.py:354
  54.2 0.6 copy-start.15
  54.8 45.7 %all-to-all-start.1 = ((bf16[64,16,640]{2,1,0:T(8,128)(2,1)}), bf16[64,16,640]{2,1,0:T(8,128)(2,1)S(1)}, u32[]{:S(2)}, u32[]{:S(2)}) async-start(bf16[64,16,640]{2,1,0:T(8,128)(2,1)} %bitcast.2), calls=%async_computation.1 | async-start | bytes 2621440 | tf_op jit(solution)/shard_map/all_to_all | solution.py:359
  100.5 5.9 %copy-start.1 = (bf16[1024,1024]{1,0:T(8,128)(2,1)S(1)}, bf16[1024,1024]{1,0:T(8,128)(2,1)}, u32[]{:S(2)}) copy-start(bf16[1024,1024]{1,0:T(8,128)(2,1)} %constant.37.clone.spread) | copy-start | bytes 6291460
  100.5 57.0 %all-to-all-start.2 = ((bf16[64,16,1024]{2,1,0:T(8,128)(2,1)}), bf16[64,16,1024]{2,1,0:T(8,128)(2,1)}, u32[]{:S(2)}, u32[]{:S(2)}) async-start(bf16[64,16,1024]{2,1,0:T(8,128)(2,1)} %bitcast.16), calls=%async_computation.2 | async-start | bytes 4194304 | tf_op jit(solution)/shard_map/all_to_all | solution.py:359

commit v4 on v3

--- a/solution.py
+++ b/solution.py
@@ -163,16 +163,20 @@
             )
 
 
-def deal(quad, fresh, group, slabs):
-    lanes = [slice(r * MAIN + group * 256, r * MAIN + group * 256 + 256) for r in range(ROWS)]
-    main = jnp.concatenate([fresh[:, :128, l].reshape(slabs * 128, 256) for l in lanes], axis=1)
-    rem = jnp.concatenate([fresh[:, 128:, l].reshape(slabs * 16, 256) for l in lanes], axis=1)
-    return nt(quad[...], main), nt(quad[...], rem)
+def put_fresh(rows, value, r, s, slabs):
+    for g in range(2):
+        piece = value[:, g * 256 : (g + 1) * 256].astype(BF16)
+        lanes = slice(r * 256, (r + 1) * 256)
+        begin = (g * slabs + s) * 128
+        rows[begin : begin + 128, lanes] = piece[:128]
+        begin = slabs * 256 + (g * slabs + s) * 16
+        rows[begin : begin + 16, lanes] = piece[128:]
 
 
 def outer_kernel(
-    rows_total, sum0, sum1, sum2, sum3, ga0, ga1, ga2, ga3, ga4, a_prev, a_first, a_mid, a_last, a_next, quad,
-    out, left_over, full, fresh, last,
+    rows_total, sum0, sum1, sum2, sum3, ga0, ga1, ga2, ga3, ga4,
+    a_prev, a_first, a_mid, a_last, a_next, quad,
+    out, left_over, full, rows,
 ):
     gas = (ga0, ga1, ga2, ga3, ga4)
     twice = twice_weight((sum0, sum1, sum2, sum3), rows_total)
@@ -191,26 +195,21 @@
                 b = full[ROWS].reshape(BLOCK, LANES)
                 prod = jnp.dot(lefts[r + 2][2][:, :BLOCK], b, preferred_element_type=F32)
             value = prod + twice * (0.0 - prod)
-            fresh[s, :, r * MAIN : (r + 1) * MAIN] = value[:, :MAIN].astype(BF16)
+            put_fresh(rows, value, r, s, 2)
             tail = value[:, MAIN:BLOCK].astype(BF16)
             for half in range(2):
                 lane = r * 256 + (2 * s + half) * ATOMS
-                last[:, lane : lane + ATOMS] = tail[half * 64 : half * 64 + 64]
+                rows[576:640, lane : lane + ATOMS] = tail[half * 64 : half * 64 + 64]
             lane = r * 256 + s * ATOMS
             left_over[:, lane : lane + ATOMS] = tail[128:]
-    rems = []
-    for g in range(2):
-        main, rem = deal(quad, fresh, g, 2)
-        out[:, g * 256 : (g + 1) * 256] = main.astype(BF16)
-        rems.append(rem)
-    rems.append(nt(quad[...], last[...]))
-    out[:, 512:] = jnp.concatenate(rems, axis=1).astype(BF16)
+    for k in range(0, 1024, 256):
+        out[k : k + 256, :] = nt(quad[k : k + 256, :], rows[...]).astype(BF16)
 
 
 def inner_kernel(
     rows_total, sum0, sum1, sum2, sum3, ga0, ga1, ga2, ga3, ga4, gb0, gb1, gb2, gb3,
     a_prev, a_first, a_mid, a_last, a_next, quad, left_over,
-    out, full, acc, fresh, last,
+    out, full, acc, rows,
 ):
     gas = (ga0, ga1, ga2, ga3, ga4)
     gbs = (gb0, gb1, gb2, gb3)
@@ -222,8 +221,9 @@
     def left(r, low, high):
         return jnp.concatenate([lefts[r + 1][j][:, :BLOCK] for j in range(low, high)], axis=0)
 
-    last[112:, :] = left_over[...]
-    last[96:112, :] = jnp.zeros((16, 1024), BF16)
+    rows[960:976, :] = jnp.zeros((16, 1024), BF16)
+    rows[976:992, :] = left_over[...]
+    rows[992:, :] = jnp.zeros((32, 1024), BF16)
     for r in range(ROWS):
         value = jnp.dot(
             left(r, 0, 3), full[ROWS + 1 + r].reshape(BLOCK, LANES), preferred_element_type=F32
@@ -246,23 +246,24 @@
         for s in range(3):
             prod = acc[s]
             value = prod + twice * (lefts[r + 1][s].astype(F32) - prod)
-            fresh[s, :, r * MAIN : (r + 1) * MAIN] = value[:, :MAIN].astype(BF16)
+            put_fresh(rows, value, r, s, 3)
             tail = value[:, MAIN:BLOCK].astype(BF16)
             for q, (low, high) in enumerate(INNER_QUARTERS):
                 begin, end = max(low, s * PANEL), min(high, (s + 1) * PANEL)
                 if begin < end:
                     lane = r * 256 + q * ATOMS
-                    last[begin - low : end - low, lane : lane + ATOMS] = tail[
+                    rows[864 + begin - low : 864 + end - low, lane : lane + ATOMS] = tail[
                         begin - s * PANEL : end - s * PANEL
                     ]
-    rems = []
-    for g in range(2):
-        main, rem = deal(quad, fresh, g, 3)
-        out[:, g * 384 : (g + 1) * 384] = main.astype(BF16)
-        rems.append(rem)
-    rems.append(nt(quad[...], last[...]))
-    rems.append(jnp.zeros((1024, 32), F32))
-    out[:, 768:] = jnp.concatenate(rems, axis=1).astype(BF16)
+    for k in range(0, 1024, 256):
+        out[k : k + 256, :] = nt(quad[k : k + 256, :], rows[...]).astype(BF16)
+
+
+def spread_out(z, lanes, spread):
+    for half in range(2):
+        value = tn(z[half * 512 : (half + 1) * 512, lanes], spread[...]).astype(BF16)
+        for q in range(4):
+            yield q, slice(half * 128, (half + 1) * 128), value[:, q * 128 : (q + 1) * 128]
 
 
 def unpack_outer_kernel(z, spread, out, held, sems):
@@ -277,20 +278,20 @@
         )
         copies[-1].start()
 
-    rest = tn(z[:, 512:], spread[...]).astype(BF16)
-    for q in range(4):
-        piece = rest[64:, q * 256 : (q + 1) * 256]
-        held[8, q // 2, (q % 2) * 64 : (q % 2) * 64 + 64, :] = piece
+    for q, lanes, value in spread_out(z, slice(512, 640), spread):
+        held[8, q // 2, (q % 2) * 64 : (q % 2) * 64 + 64, lanes] = value[64:]
+        for g in range(2):
+            for s in range(2):
+                begin = g * 32 + s * 16
+                held[4 * g + q, s, 128:, lanes] = value[begin : begin + 16]
     for s in range(2):
         send(8, s, 128)
     for g in range(2):
-        main = tn(z[:, g * 256 : (g + 1) * 256], spread[...]).astype(BF16)
+        for q, lanes, value in spread_out(z, slice(g * 256, (g + 1) * 256), spread):
+            for s in range(2):
+                held[4 * g + q, s, :128, lanes] = value[s * 128 : (s + 1) * 128]
         for q in range(4):
             for s in range(2):
-                lanes = slice(q * 256, (q + 1) * 256)
-                held[4 * g + q, s, :128, :] = main[s * 128 : (s + 1) * 128, lanes]
-                begin = g * 32 + s * 16
-                held[4 * g + q, s, 128:, :] = rest[begin : begin + 16, lanes]
                 send(4 * g + q, s, PANEL)
     for copy in copies:
         copy.wait()
@@ -304,31 +305,37 @@
         copies.append(pltpu.make_async_copy(src, dst, sems.at[len(copies)]))
         copies[-1].start()
 
-    rest = tn(z[:, 768:], spread[...]).astype(BF16)
-    for q, (low, high) in enumerate(INNER_QUARTERS):
-        held[8, low:high, :] = rest[96 : 96 + high - low, q * 256 : (q + 1) * 256]
+    for q, lanes, value in spread_out(z, slice(768, 1024), spread):
+        low, high = INNER_QUARTERS[q]
+        held[8, low:high, lanes] = value[96 : 96 + high - low]
+        if q < 2:
+            edge[q, :, lanes] = value[208:224]
+        for g in range(2):
+            for s in range(3):
+                begin = g * 48 + s * 16
+                held[4 * g + q, s * PANEL + 128 : (s + 1) * PANEL, lanes] = value[
+                    begin : begin + 16
+                ]
     send(held.at[8], out.at[8, PANEL : 4 * PANEL])
     for s in range(2):
-        edge[s] = rest[208:224, s * 256 : (s + 1) * 256]
         row = s * 4 * PANEL + 128
         send(edge.at[s], out.at[8, row : row + 16])
     for g in range(2):
-        main = tn(z[:, g * 384 : (g + 1) * 384], spread[...]).astype(BF16)
+        for q, lanes, value in spread_out(z, slice(g * 384, (g + 1) * 384), spread):
+            for s in range(3):
+                held[4 * g + q, s * PANEL : s * PANEL + 128, lanes] = value[
+                    s * 128 : (s + 1) * 128
+                ]
         for q in range(4):
-            for s in range(3):
-                lanes = slice(q * 256, (q + 1) * 256)
-                held[4 * g + q, s * PANEL : s * PANEL + 128, :] = main[s * 128 : (s + 1) * 128, lanes]
-                begin = g * 48 + s * 16
-                held[4 * g + q, s * PANEL + 128 : (s + 1) * PANEL, :] = rest[begin : begin + 16, lanes]
             send(held.at[4 * g + q], out.at[4 * g + q, PANEL : 4 * PANEL])
     for copy in copies:
         copy.wait()
 
 
 def spread_matrix():
-    w, q, j = np.meshgrid(np.arange(64), np.arange(4), np.arange(4), indexing="ij")
-    table = np.zeros((1024, 1024), np.float32)
-    table[np.arange(1024), (q * 256 + w * 4 + j).reshape(-1)] = 1.0
+    w, q, j = np.meshgrid(np.arange(32), np.arange(4), np.arange(4), indexing="ij")
+    table = np.zeros((512, 512), np.float32)
+    table[np.arange(512), (q * 128 + w * 4 + j).reshape(-1)] = 1.0
     return table
 
 
@@ -410,9 +417,7 @@
         compiler_params=params(8),
         name="deal",
     )(wanted)
-    gb, quad, a_prev, a_next, sums, gas = lax.optimization_barrier(
-        (gb, quad, a_prev, a_next, sums, gas)
-    )
+    gb, quad, a_prev, a_next, sums = lax.optimization_barrier((gb, quad, a_prev, a_next, sums))
     gbs = direct_gather(gb)
     lefts = (a_prev, a_first, a_mid, a_last, a_next)
     packed_outer, left_over = pl.pallas_call(
@@ -422,8 +427,7 @@
         out_specs=[VM, VM],
         scratch_shapes=[
             pltpu.VMEM((ROWS + 1, ORB, NARROW, 16, LANES), BF16),
-            pltpu.VMEM((2, PANEL, ROWS * MAIN), BF16),
-            pltpu.VMEM((64, 1024), BF16),
+            pltpu.VMEM((OUTER_CHUNK, 1024), BF16),
         ],
         compiler_params=params(24),
         cost_estimate=pl.CostEstimate(
@@ -440,8 +444,7 @@
         scratch_shapes=[
             pltpu.VMEM((2 * ROWS + 1, ORB, NARROW, 16, LANES), BF16),
             pltpu.VMEM((3, PANEL, LANES), F32),
-            pltpu.VMEM((3, PANEL, ROWS * MAIN), BF16),
-            pltpu.VMEM((128, 1024), BF16),
+            pltpu.VMEM((INNER_CHUNK, 1024), BF16),
         ],
         compiler_params=params(54),
         cost_estimate=pl.CostEstimate(

time: 163 us -> 160 us (0.982)
  Pallas kernels: 35 us -> 29.1 us
  local copies, waits for them, and re-layouts: 6.88 us -> 8.86 us
    pallas_call x1, Pallas kernels: 4.9 us -> 2.29 us  [shards(): pl.pallas_call(unpack_inner_kernel, out_shape=sds((ORB, 5 * PANEL, 256),...]
    unnamed x34 -> x36, local copies, waits for them, and re-layouts: 3.9 us -> 5.96 us
    pallas_call x1, Pallas kernels: 15.1 us -> 13.4 us  [shards(): pl.pallas_call(lambda *refs: inner_kernel(rows_total, *refs), out_shape=s...]
  transfers between devices with their start and end apart: 15 -> 15, of which waited for: 5 -> 5; matrix products, arithmetic and copies ran while one was open for 2% -> 2% of each run, Pallas kernels for 18% -> 16%
where the time goes in v4:
time: 160 us
  waiting for transfers between devices  72.8 us (46%)
  starting transfers between devices  47.6 us (30%)
  Pallas kernels  29.1 us (18%)
  local copies, waits for them, and re-layouts  8.86 us (6%)
    all_to_all x2, waiting for transfers between devices, exchange(): got = lax.all_to_all(parts, 'wide', split_axis=0, concat_axis=0, tiled=True)  60 us
    all_to_all x2, starting transfers between devices, exchange(): got = lax.all_to_all(parts, 'wide', split_axis=0, concat_axis=0, tiled=True)  16.8 us
    pallas_call x1, Pallas kernels, shards(): pl.pallas_call(lambda *refs: inner_kernel(rows_total, *refs), out_shape=s...  13.4 us
    all_to_all x1, starting transfers between devices, shards(): lax.all_to_all(traces, 'wide', split_axis=0, concat_axis=0, tiled=True)  12.8 us
    ppermute x6, starting transfers between devices, direct_gather(): lax.ppermute(own, 'narrow', shift_perm(NARROW, step))  9.63 us
    ppermute x6, waiting for transfers between devices, direct_gather(): lax.ppermute(own, 'narrow', shift_perm(NARROW, step))  9.48 us
    pallas_call x1, Pallas kernels, shards(): pl.pallas_call(lambda *refs: outer_kernel(rows_total, *refs), out_shape=[...  6.81 us
    unnamed x36, local copies, waits for them, and re-layouts  5.96 us
  transfers between devices with their start and end apart: 15, of which 5 were waited for; matrix products, arithmetic and copies ran while one was open for 2% of the time, Pallas kernels for 16%

profile of v4, /device:TPU:8, one launch (start us, length us, event | category | flops | bytes accessed | tf_op | source)
XLA Modules:
  0.0 159.7 jit_solution(18344624380802244216)
XLA Ops:
  0.0 1.6 copy-done
  1.6 0.7 copy-done.7
  2.2 1.1 prep_outer.1.ga.refs_4_
  3.4 1.6 collective-permute-start.1
  4.9 1.7 %collective-permute-start = (bf16[144,2944]{1,0:T(8,128)(2,1)S(1)}, bf16[144,2944]{1,0:T(8,128)(2,1)S(1)}, u32[]{:S(2)}, u32[]{:S(2)}) collective-permute-start(bf16[144,2944]{1,0:T(8,128)(2,1)S(1)} %prep_outer.1.ga.refs_4_), channel_id=1, source_target_pairs={{0,3},{1,0},{2,1},{3,2},{4,7},{5,4},{6,5},{7,6},{8,11},{9,8},{10,9... | collective-permute-start | bytes 2543624 | tf_op jit(solution)/shard_map/ppermute | solution.py:347
  6.7 3.2 %prep_inner.1 = (bf16[144,2304]{1,0:T(8,128)(2,1)}, bf16[3,144,640]{2,1,0:T(8,128)(2,1)}, bf16[2,3,144,640]{3,2,1,0:T(8,128)(2,1)S(1)}, bf16[3,144,640]{2,1,0:T(8,128)(2,1)}, f32[64,1,128]{2,1,0:T(1,128)}) custom-call(s32[256]{0:T(256)S(1)} %copy-done.8, bf16[3,9,144,256]{3,2,1,0:T(8,128)(2,1)S(1)} %bitcast.9, bf16[144,2944]{1,0:T(8,128)(2,1)S(1)} %prep_outer.1.ga.refs_4_), custom_call_target="tpu_custom_call" | custom-call | tf_op jit(solution)/shard_map/prep_inner/pallas_call | solution.py:388
  9.9 1.0 copy-done.10
  10.9 1.7 %collective-permute-start.3 = (bf16[3,144,640]{2,1,0:T(8,128)(2,1)}, bf16[3,144,640]{2,1,0:T(8,128)(2,1)}, u32[]{:S(2)}, u32[]{:S(2)}) collective-permute-start(bf16[3,144,640]{2,1,0:T(8,128)(2,1)} %get-tuple-element.30.refs_10_.refs_14_), channel_id=1, source_target_pairs={{0,252},{4,0},{8,4},{12,8},{16,12},{20,16},{24,20},{28,24},{32,28}... | collective-permute-start | bytes 1658888 | tf_op jit(solution)/shard_map/ppermute | solution.py:403
  12.6 12.8 %all-to-all-start = ((f32[64,1,128]{2,1,0:T(1,128)}), f32[64,1,128]{2,1,0:T(1,128)S(1)}, u32[]{:S(2)}, u32[]{:S(2)}) async-start(f32[64,1,128]{2,1,0:T(1,128)} %get-tuple-element.33), calls=%async_computation | async-start | bytes 65536 | tf_op jit(solution)/shard_map/all_to_all | solution.py:404
  25.6 0.9 slice.7
  26.5 0.8 slice.6
  27.3 1.1 collective-permute-start.8
  28.4 2.2 %collective-permute-start.7 = (bf16[80,2944]{1,0:T(8,128)(2,1)}, bf16[80,2944]{1,0:T(8,128)(2,1)S(1)}, u32[]{:S(2)}, u32[]{:S(2)}) collective-permute-start(bf16[80,2944]{1,0:T(8,128)(2,1)} %slice.6), channel_id=1, source_target_pairs={{0,3},{1,0},{2,1},{3,2},{4,7},{5,4},{6,5},{7,6},{8,11},{9,8},{10,9... | collective-permute-start | bytes 1413128 | tf_op jit(solution)/shard_map/ppermute | solution.py:355
  30.6 3.3 %all-to-all-done = f32[64,1,128]{2,1,0:T(1,128)S(1)} async-done(((f32[64,1,128]{2,1,0:T(1,128)}), f32[64,1,128]{2,1,0:T(1,128)S(1)}, u32[]{:S(2)}, u32[]{:S(2)}) %all-to-all-start) | async-done | bytes 32800 | tf_op jit(solution)/shard_map/all_to_all | solution.py:404
  34.4 2.7 %collective-permute-start.5 = (f32[1,128]{1,0:T(1,128)S(1)}, f32[1,128]{1,0:T(1,128)S(1)}, u32[]{:S(2)}, u32[]{:S(2)}) collective-permute-start(f32[1,128]{1,0:T(1,128)S(1)} %bitcast.13), channel_id=1, source_target_pairs={{0,2},{1,3},{2,0},{3,1},{4,6},{5,7},{6,4},{7,5},{8,10},{9,11},{10,... | collective-permute-start | bytes 1544 | tf_op jit(solution)/shard_map/ppermute | solution.py:361
  37.1 1.4 collective-permute-start.4
  38.6 0.8 add_add_fusion
  39.3 1.1 reshape.145.wanted
  41.0 1.6 collective-permute-start.11
  42.6 3.5 %collective-permute-start.10 = (bf16[144,2304]{1,0:T(8,128)(2,1)}, bf16[144,2304]{1,0:T(8,128)(2,1)}, u32[]{:S(2)}, u32[]{:S(2)}) collective-permute-start(bf16[144,2304]{1,0:T(8,128)(2,1)} %get-tuple-element.42.refs_9_), channel_id=1, source_target_pairs={{0,2},{1,3},{2,0},{3,1},{4,6},{5,7},{6,4},{7,5},{8,10},{9,11},{10,... | collective-permute-start | bytes 1990664 | tf_op jit(solution)/shard_map/ppermute | solution.py:361
  46.2 6.8 %outer.1 = (bf16[1024,640]{1,0:T(8,128)(2,1)}, bf16[16,1024]{1,0:T(8,128)(2,1)S(1)}) custom-call(f32[1,128]{1,0:T(1,128)S(1)} %bitcast.15, f32[1,128]{1,0:T(1,128)S(1)} %collective-permute-done.4.refs_1_, f32[1,128]{1,0:T(1,128)S(1)} %collective-permute-done.5.refs_2_, f32[1,128]{1,0:T(1,128)S(1)} %collective-permute-done.6.refs_3_, ...), custom_call_target="tpu_custom_call" | custom-call | flops 30000001024 | bytes 8388608 | tf_op jit(solution)/shard_map/outer/pallas_call | solution.py:423
  53.0 0.6 copy-done.16
  53.6 11.3 %all-to-all-start.1 = ((bf16[64,16,640]{2,1,0:T(8,128)(2,1)}), bf16[64,16,640]{2,1,0:T(8,128)(2,1)S(1)}, u32[]{:S(2)}, u32[]{:S(2)}) async-start(bf16[64,16,640]{2,1,0:T(8,128)(2,1)} %bitcast.2), calls=%async_computation.1 | async-start | bytes 2621440 | tf_op jit(solution)/shard_map/all_to_all | solution.py:366
  65.0 9.4 %collective-permute-done.10.refs_11_ = bf16[144,2304]{1,0:T(8,128)(2,1)} collective-permute-done((bf16[144,2304]{1,0:T(8,128)(2,1)}, bf16[144,2304]{1,0:T(8,128)(2,1)}, u32[]{:S(2)}, u32[]{:S(2)}) %collective-permute-start.10) | collective-permute-done | bytes 663584 | tf_op jit(solution)/shard_map/ppermute | solution.py:361
  74.4 13.4 %inner.1 = bf16[1024,1024]{1,0:T(8,128)(2,1)} custom-call(f32[1,128]{1,0:T(1,128)} %bitcast.16, f32[1,128]{1,0:T(1,128)} %copy-done.15, f32[1,128]{1,0:T(1,128)} %copy-done.14, f32[1,128]{1,0:T(1,128)} %copy-done.13, bf16[144,2944]{1,0:T(8,128)(2,1)} %copy-done.1, bf16[144,2944]{1,0:T(8,128)(2,1)} %copy-done.5, bf16[80,2944]{1,0:T(8,128)(2,1)} %copy-done.12, ...), custom_call_target="tpu_custom_call" | custom-call | flops 70000001024 | bytes 12582912 | tf_op jit(solution)/shard_map/inner/pallas_call | solution.py:439
  87.8 11.6 %all-to-all-done.1 = bf16[64,16,640]{2,1,0:T(8,128)(2,1)S(1)} async-done(((bf16[64,16,640]{2,1,0:T(8,128)(2,1)}), bf16[64,16,640]{2,1,0:T(8,128)(2,1)S(1)}, u32[]{:S(2)}, u32[]{:S(2)}) %all-to-all-start.1) | async-done | bytes 1310752 | tf_op jit(solution)/shard_map/all_to_all | solution.py:366
  99.4 5.5 %all-to-all-start.2 = ((bf16[64,16,1024]{2,1,0:T(8,128)(2,1)}), bf16[64,16,1024]{2,1,0:T(8,128)(2,1)S(1)}, u32[]{:S(2)}, u32[]{:S(2)}) async-start(bf16[64,16,1024]{2,1,0:T(8,128)(2,1)} %bitcast.17), calls=%async_computation.2 | async-start | bytes 4194304 | tf_op jit(solution)/shard_map/all_to_all | solution.py:366
  104.9 1.0 copy-done.2
  105.9 1.8 %unpack_outer.1.begun = bf16[9,720,256]{2,1,0:T(8,128)(2,1)} custom-call(bf16[1024,640]{1,0:T(8,128)(2,1)S(1)} %bitcast.11, bf16[512,512]{1,0:T(8,128)(2,1)S(1)} %copy-done.2), custom_call_target="tpu_custom_call" | custom-call | tf_op jit(solution)/shard_map/unpack_outer/pallas_call | solution.py:458
  107.8 48.4 %all-to-all-done.2 = bf16[64,16,1024]{2,1,0:T(8,128)(2,1)S(1)} async-done(((bf16[64,16,1024]{2,1,0:T(8,128)(2,1)}), bf16[64,16,1024]{2,1,0:T(8,128)(2,1)S(1)}, u32[]{:S(2)}, u32[]{:S(2)}) %all-to-all-start.2) | async-done | bytes 2097184 | tf_op jit(solution)/shard_map/all_to_all | solution.py:366
  156.2 1.0 copy-done.3
  157.2 2.3 %unpack_inner.1 = bf16[9,720,256]{2,1,0:T(8,128)(2,1)} custom-call(bf16[1024,1024]{1,0:T(8,128)(2,1)S(1)} %bitcast.10, bf16[512,512]{1,0:T(8,128)(2,1)S(1)} %copy-done.3, bf16[9,720,256]{2,1,0:T(8,128)(2,1)} %unpack_outer.1.begun), custom_call_target="tpu_custom_call", output_to_operand_aliasing={{}: (2, {})} | custom-call | tf_op jit(solution)/shard_map/unpack_inner/pallas_call | solution.py:470
  (50 shorter events, 1.2 us)
Async XLA Ops:
  0.0 1.6 copy-start
  1.6 0.7 copy-start.7
  2.2 4.5 %copy-start.8 = (s32[256]{0:T(256)S(1)}, s32[256]{0:T(256)}, u32[]{:S(2)}) copy-start(s32[256]{0:T(256)} %link.3) | copy-start | bytes 3076
  3.4 42.8 %copy-start.1 = (bf16[144,2944]{1,0:T(8,128)(2,1)}, bf16[144,2944]{1,0:T(8,128)(2,1)S(1)}, u32[]{:S(2)}) copy-start(bf16[144,2944]{1,0:T(8,128)(2,1)S(1)} %prep_outer.1.ga.refs_4_) | copy-start | bytes 2543620
  3.4 22.1 %copy-start.17 = (s32[256]{0:T(256)S(1)}, s32[256]{0:T(256)}, u32[]{:S(2)}) copy-start(s32[256]{0:T(256)} %param.6) | copy-start | bytes 3076
  3.4 22.2 %collective-permute-start.1 = (bf16[144,2944]{1,0:T(8,128)(2,1)S(1)}, bf16[144,2944]{1,0:T(8,128)(2,1)S(1)}, u32[]{:S(2)}, u32[]{:S(2)}) collective-permute-start(bf16[144,2944]{1,0:T(8,128)(2,1)S(1)} %prep_outer.1.ga.refs_4_), channel_id=1, source_target_pairs={{0,1},{1,2},{2,3},{3,0},{4,5},{5,6},{6,7},{7,4},{8,9},{9,10},{10,1... | collective-permute-start | bytes 2543624 | tf_op jit(solution)/shard_map/ppermute | solution.py:348
  4.9 20.7 %collective-permute-start = (bf16[144,2944]{1,0:T(8,128)(2,1)S(1)}, bf16[144,2944]{1,0:T(8,128)(2,1)S(1)}, u32[]{:S(2)}, u32[]{:S(2)}) collective-permute-start(bf16[144,2944]{1,0:T(8,128)(2,1)S(1)} %prep_outer.1.ga.refs_4_), channel_id=1, source_target_pairs={{0,3},{1,0},{2,1},{3,2},{4,7},{5,4},{6,5},{7,6},{8,11},{9,8},{10,9... | collective-permute-start | bytes 2543624 | tf_op jit(solution)/shard_map/ppermute | solution.py:347
  9.9 1.0 copy-start.10
  10.9 14.7 %collective-permute-start.2 = (bf16[3,144,640]{2,1,0:T(8,128)(2,1)}, bf16[3,144,640]{2,1,0:T(8,128)(2,1)}, u32[]{:S(2)}, u32[]{:S(2)}) collective-permute-start(bf16[3,144,640]{2,1,0:T(8,128)(2,1)} %get-tuple-element.29.refs_12_.refs_16_), channel_id=1, source_target_pairs={{0,4},{4,8},{8,12},{12,16},{16,20},{20,24},{24,28},{28,32},{32,36}... | collective-permute-start | bytes 1658888 | tf_op jit(solution)/shard_map/ppermute | solution.py:402
  10.9 14.7 %collective-permute-start.3 = (bf16[3,144,640]{2,1,0:T(8,128)(2,1)}, bf16[3,144,640]{2,1,0:T(8,128)(2,1)}, u32[]{:S(2)}, u32[]{:S(2)}) collective-permute-start(bf16[3,144,640]{2,1,0:T(8,128)(2,1)} %get-tuple-element.30.refs_10_.refs_14_), channel_id=1, source_target_pairs={{0,252},{4,0},{8,4},{12,8},{16,12},{20,16},{24,20},{28,24},{32,28}... | collective-permute-start | bytes 1658888 | tf_op jit(solution)/shard_map/ppermute | solution.py:403
  12.6 21.3 %all-to-all-start = ((f32[64,1,128]{2,1,0:T(1,128)}), f32[64,1,128]{2,1,0:T(1,128)S(1)}, u32[]{:S(2)}, u32[]{:S(2)}) async-start(f32[64,1,128]{2,1,0:T(1,128)} %get-tuple-element.33), calls=%async_computation | async-start | bytes 65536 | tf_op jit(solution)/shard_map/all_to_all | solution.py:404
  25.6 20.5 %copy-start.6 = (bf16[144,2944]{1,0:T(8,128)(2,1)}, bf16[144,2944]{1,0:T(8,128)(2,1)S(1)}, u32[]{:S(2)}) copy-start(bf16[144,2944]{1,0:T(8,128)(2,1)S(1)} %collective-permute-done.1.refs_8_) | copy-start | bytes 2543620
  25.6 20.5 %copy-start.5 = (bf16[144,2944]{1,0:T(8,128)(2,1)}, bf16[144,2944]{1,0:T(8,128)(2,1)S(1)}, u32[]{:S(2)}) copy-start(bf16[144,2944]{1,0:T(8,128)(2,1)S(1)} %collective-permute-done.refs_5_) | copy-start | bytes 2543620
  27.3 18.8 %collective-permute-start.8 = (bf16[64,2944]{1,0:T(8,128)(2,1)}, bf16[64,2944]{1,0:T(8,128)(2,1)}, u32[]{:S(2)}, u32[]{:S(2)}) collective-permute-start(bf16[64,2944]{1,0:T(8,128)(2,1)} %slice.7), channel_id=1, source_target_pairs={{0,1},{1,2},{2,3},{3,0},{4,5},{5,6},{6,7},{7,4},{8,9},{9,10},{10,1... | collective-permute-start | bytes 1130504 | tf_op jit(solution)/shard_map/ppermute | solution.py:356
  28.4 17.7 %collective-permute-start.7 = (bf16[80,2944]{1,0:T(8,128)(2,1)}, bf16[80,2944]{1,0:T(8,128)(2,1)S(1)}, u32[]{:S(2)}, u32[]{:S(2)}) collective-permute-start(bf16[80,2944]{1,0:T(8,128)(2,1)} %slice.6), channel_id=1, source_target_pairs={{0,3},{1,0},{2,1},{3,2},{4,7},{5,4},{6,5},{7,6},{8,11},{9,8},{10,9... | collective-permute-start | bytes 1413128 | tf_op jit(solution)/shard_map/ppermute | solution.py:355
  34.0 18.9 %copy-start.9 = (f32[128]{0:T(128)}, f32[128]{0:T(128)S(1)}, u32[]{:S(2)}) copy-start(f32[128]{0:T(128)S(1)} %reduce_sum.11) | copy-start | bytes 1540
  34.0 6.8 %collective-permute-start.6 = (f32[1,128]{1,0:T(1,128)S(1)}, f32[1,128]{1,0:T(1,128)S(1)}, u32[]{:S(2)}, u32[]{:S(2)}) collective-permute-start(f32[1,128]{1,0:T(1,128)S(1)} %bitcast.12), channel_id=1, source_target_pairs={{0,1},{1,2},{2,3},{3,0},{4,5},{5,6},{6,7},{7,4},{8,9},{9,10},{10,1... | collective-permute-start | bytes 1544 | tf_op jit(solution)/shard_map/ppermute | solution.py:361
  34.4 6.5 %collective-permute-start.5 = (f32[1,128]{1,0:T(1,128)S(1)}, f32[1,128]{1,0:T(1,128)S(1)}, u32[]{:S(2)}, u32[]{:S(2)}) collective-permute-start(f32[1,128]{1,0:T(1,128)S(1)} %bitcast.13), channel_id=1, source_target_pairs={{0,2},{1,3},{2,0},{3,1},{4,6},{5,7},{6,4},{7,5},{8,10},{9,11},{10,... | collective-permute-start | bytes 1544 | tf_op jit(solution)/shard_map/ppermute | solution.py:361
  37.1 3.9 %collective-permute-start.4 = (f32[1,128]{1,0:T(1,128)S(1)}, f32[1,128]{1,0:T(1,128)S(1)}, u32[]{:S(2)}, u32[]{:S(2)}) collective-permute-start(f32[1,128]{1,0:T(1,128)S(1)} %bitcast.14), channel_id=1, source_target_pairs={{0,3},{1,0},{2,1},{3,2},{4,7},{5,4},{6,5},{7,6},{8,11},{9,8},{10,9... | collective-permute-start | bytes 1544 | tf_op jit(solution)/shard_map/ppermute | solution.py:361
  40.4 5.7 %copy-start.11 = (bf16[2,3,144,640]{3,2,1,0:T(8,128)(2,1)S(1)}, bf16[2,3,144,640]{3,2,1,0:T(8,128)(2,1)}, u32[]{:S(2)}) copy-start(bf16[2,3,144,640]{3,2,1,0:T(8,128)(2,1)} %copy-done.10) | copy-start | bytes 3317764
  40.9 12.1 %copy-start.4 = (bf16[1024,1024]{1,0:T(8,128)(2,1)}, bf16[1024,1024]{1,0:T(8,128)(2,1)S(1)}, u32[]{:S(2)}) copy-start(bf16[1024,1024]{1,0:T(8,128)(2,1)S(1)} %deal.1.refs_14_.refs_18_) | copy-start | bytes 6291460
  40.9 12.1 %copy-start.13 = (f32[1,128]{1,0:T(1,128)}, f32[1,128]{1,0:T(1,128)S(1)}, u32[]{:S(2)}) copy-start(f32[1,128]{1,0:T(1,128)S(1)} %collective-permute-done.6.refs_3_) | copy-start | bytes 1540
  40.9 12.1 %copy-start.14 = (f32[1,128]{1,0:T(1,128)}, f32[1,128]{1,0:T(1,128)S(1)}, u32[]{:S(2)}) copy-start(f32[1,128]{1,0:T(1,128)S(1)} %collective-permute-done.5.refs_2_) | copy-start | bytes 1540
  41.0 12.0 %copy-start.15 = (f32[1,128]{1,0:T(1,128)}, f32[1,128]{1,0:T(1,128)S(1)}, u32[]{:S(2)}) copy-start(f32[1,128]{1,0:T(1,128)S(1)} %collective-permute-done.4.refs_1_) | copy-start | bytes 1540
  41.0 24.0 %collective-permute-start.11 = (bf16[144,2304]{1,0:T(8,128)(2,1)}, bf16[144,2304]{1,0:T(8,128)(2,1)}, u32[]{:S(2)}, u32[]{:S(2)}) collective-permute-start(bf16[144,2304]{1,0:T(8,128)(2,1)} %get-tuple-element.42.refs_9_), channel_id=1, source_target_pairs={{0,1},{1,2},{2,3},{3,0},{4,5},{5,6},{6,7},{7,4},{8,9},{9,10},{10,1... | collective-permute-start | bytes 1990664 | tf_op jit(solution)/shard_map/ppermute | solution.py:361
  42.6 31.8 %collective-permute-start.10 = (bf16[144,2304]{1,0:T(8,128)(2,1)}, bf16[144,2304]{1,0:T(8,128)(2,1)}, u32[]{:S(2)}, u32[]{:S(2)}) collective-permute-start(bf16[144,2304]{1,0:T(8,128)(2,1)} %get-tuple-element.42.refs_9_), channel_id=1, source_target_pairs={{0,2},{1,3},{2,0},{3,1},{4,6},{5,7},{6,4},{7,5},{8,10},{9,11},{10,... | collective-permute-start | bytes 1990664 | tf_op jit(solution)/shard_map/ppermute | solution.py:361
  46.1 28.3 %collective-permute-start.9 = (bf16[144,2304]{1,0:T(8,128)(2,1)}, bf16[144,2304]{1,0:T(8,128)(2,1)}, u32[]{:S(2)}, u32[]{:S(2)}) collective-permute-start(bf16[144,2304]{1,0:T(8,128)(2,1)} %get-tuple-element.42.refs_9_), channel_id=1, source_target_pairs={{0,3},{1,0},{2,1},{3,2},{4,7},{5,4},{6,5},{7,6},{8,11},{9,8},{10,9... | collective-permute-start | bytes 1990664 | tf_op jit(solution)/shard_map/ppermute | solution.py:361
  46.1 6.9 %copy-start.12 = (bf16[80,2944]{1,0:T(8,128)(2,1)}, bf16[80,2944]{1,0:T(8,128)(2,1)S(1)}, u32[]{:S(2)}) copy-start(bf16[80,2944]{1,0:T(8,128)(2,1)S(1)} %collective-permute-done.7.refs_6_) | copy-start | bytes 1413124
  53.6 45.7 %all-to-all-start.1 = ((bf16[64,16,640]{2,1,0:T(8,128)(2,1)}), bf16[64,16,640]{2,1,0:T(8,128)(2,1)S(1)}, u32[]{:S(2)}, u32[]{:S(2)}) async-start(bf16[64,16,640]{2,1,0:T(8,128)(2,1)} %bitcast.2), calls=%async_computation.1 | async-start | bytes 2621440 | tf_op jit(solution)/shard_map/all_to_all | solution.py:366
  99.4 56.8 %all-to-all-start.2 = ((bf16[64,16,1024]{2,1,0:T(8,128)(2,1)}), bf16[64,16,1024]{2,1,0:T(8,128)(2,1)S(1)}, u32[]{:S(2)}, u32[]{:S(2)}) async-start(bf16[64,16,1024]{2,1,0:T(8,128)(2,1)} %bitcast.17), calls=%async_computation.2 | async-start | bytes 4194304 | tf_op jit(solution)/shard_map/all_to_all | solution.py:366
  104.9 1.0 copy-start.2
  156.2 1.0 copy-start.3
  (1 other events, 0.6 us)

commit v5 on v4

--- a/solution.py
+++ b/solution.py
@@ -12,6 +12,7 @@
 PANEL = 144
 LANES = 640
 ROWS = 4
+SPLIT = 80
 NARROW = 4
 WIDE = 64
 MAIN = 512
@@ -62,7 +63,7 @@
     out[:, tail : tail + ATOMS] = value[:, MAIN:BLOCK]
 
 
-def prep_outer_kernel(link, low, high, ga):
+def prep_outer_kernel(link, low, high, top, bottom):
     first = lax.axis_index("wide") * ROWS
     before = lane_mask(link, first, -1).astype(BF16)
     after = lane_mask(link, first, 0).astype(BF16)
@@ -73,8 +74,10 @@
             tiles = [high[0, o] * after for o in range(ORB)]
         value = packed_row(tiles, min(p, ROWS - 1), False)
         turned = jnp.dot(reorder, value, preferred_element_type=F32).astype(BF16)
-        put_panel(ga, ROWS + 1, p, turned)
-    ga[:, (ROWS + 1) * BLOCK :] = jnp.zeros((PANEL, ATOMS), BF16)
+        put_panel(top, ROWS + 1, p, turned[:SPLIT])
+        put_panel(bottom, ROWS + 1, p, turned[SPLIT:])
+    top[:, (ROWS + 1) * BLOCK :] = jnp.zeros((SPLIT, ATOMS), BF16)
+    bottom[:, (ROWS + 1) * BLOCK :] = jnp.zeros((PANEL - SPLIT, ATOMS), BF16)
 
 
 def prep_inner_kernel(link, x, ga, gb, a_first, a_mid, a_last, traces):
@@ -148,7 +151,12 @@
     if len(sources) == NARROW:
         places = tuple((shift, 0, ORB) for shift in range(NARROW))
     else:
-        places = ((0, 0, ORB), (1, 0, ORB), (2, 0, 5), (2, 5, 4), (3, 0, ORB))
+        cut = SPLIT // 16
+        places = tuple(
+            (shift, o, depth)
+            for shift in range(NARROW)
+            for o, depth in ((0, cut), (cut, ORB - cut))
+        )
     for (shift, o, depth), src in zip(places, sources):
         owner = lax.rem(narrow + shift, NARROW)
         for p in range(count):
@@ -174,11 +182,11 @@
 
 
 def outer_kernel(
-    rows_total, sum0, sum1, sum2, sum3, ga0, ga1, ga2, ga3, ga4,
+    rows_total, sum0, sum1, sum2, sum3, ga0, ga1, ga2, ga3, ga4, ga5, ga6, ga7,
     a_prev, a_first, a_mid, a_last, a_next, quad,
     out, left_over, full, rows,
 ):
-    gas = (ga0, ga1, ga2, ga3, ga4)
+    gas = (ga0, ga1, ga2, ga3, ga4, ga5, ga6, ga7)
     twice = twice_weight((sum0, sum1, sum2, sum3), rows_total)
     assemble(full, 0, ROWS + 1, gas)
     lefts = [a_prev, a_first, a_mid.at[0], a_mid.at[1], a_last, a_next]
@@ -207,11 +215,11 @@
 
 
 def inner_kernel(
-    rows_total, sum0, sum1, sum2, sum3, ga0, ga1, ga2, ga3, ga4, gb0, gb1, gb2, gb3,
+    rows_total, sum0, sum1, sum2, sum3, ga0, ga1, ga2, ga3, ga4, ga5, ga6, ga7, gb0, gb1, gb2, gb3,
     a_prev, a_first, a_mid, a_last, a_next, quad, left_over,
     out, full, acc, rows,
 ):
-    gas = (ga0, ga1, ga2, ga3, ga4)
+    gas = (ga0, ga1, ga2, ga3, ga4, ga5, ga6, ga7)
     gbs = (gb0, gb1, gb2, gb3)
     twice = twice_weight((sum0, sum1, sum2, sum3), rows_total)
     assemble(full, 0, ROWS + 1, gas)
@@ -343,18 +351,19 @@
     return [(i, (i - step) % count) for i in range(count)]
 
 
-def neighbours(own):
-    after = lax.ppermute(own, "narrow", shift_perm(NARROW, 1))
-    before = lax.ppermute(own, "narrow", shift_perm(NARROW, -1))
-    return after, before
-
-
-def opposite(after, before):
-    split = 80
-    top, bottom = lax.optimization_barrier((after[:split], before[split:]))
-    top = lax.ppermute(top, "narrow", shift_perm(NARROW, 1))
-    bottom = lax.ppermute(bottom, "narrow", shift_perm(NARROW, -1))
-    return top, bottom
+def ring_gather(top, bottom):
+    def up(value):
+        return lax.ppermute(value, "narrow", shift_perm(NARROW, 1))
+
+    def down(value):
+        return lax.ppermute(value, "narrow", shift_perm(NARROW, -1))
+
+    after_top, before_bottom = up(top), down(bottom)
+    after_bottom, before_top = up(bottom), down(top)
+    return [
+        top, bottom, after_top, after_bottom,
+        up(after_top), down(before_bottom), before_top, before_bottom,
+    ]
 
 
 def direct_gather(own):
@@ -371,20 +380,23 @@
     rows_total = link.shape[0]
     x = jnp.transpose(xblk, (0, 2, 1, 3))
     slab = (1, ORB, PANEL, ROWS * ATOMS)
-    ga = pl.pallas_call(
+    top, bottom = pl.pallas_call(
         prep_outer_kernel,
-        out_shape=sds((PANEL, 2944), BF16),
+        out_shape=[sds((SPLIT, 2944), BF16), sds((PANEL - SPLIT, 2944), BF16)],
         grid=(1,),
         in_specs=[
             SM,
             pl.BlockSpec(slab, lambda i: (0, 0, 0, 0)),
             pl.BlockSpec(slab, lambda i: (2, 0, 0, 0)),
         ],
-        out_specs=pl.BlockSpec((PANEL, 2944), lambda i: (0, 0)),
+        out_specs=[
+            pl.BlockSpec((SPLIT, 2944), lambda i: (0, 0)),
+            pl.BlockSpec((PANEL - SPLIT, 2944), lambda i: (0, 0)),
+        ],
         compiler_params=params(48),
         name="prep_outer",
     )(link, x, x)
-    after, before = neighbours(ga)
+    gas = ring_gather(top, bottom)
     gb, a_first, a_mid, a_last, traces = pl.pallas_call(
         prep_inner_kernel,
         out_shape=[
@@ -398,14 +410,12 @@
         out_specs=[VM] * 5,
         compiler_params=params(48),
         name="prep_inner",
-    )(link, x, ga)
+    )(link, x, top)
     a_prev = lax.ppermute(a_last, "wide", shift_perm(WIDE, -1))
     a_next = lax.ppermute(a_first, "wide", shift_perm(WIDE, 1))
     line = lax.all_to_all(traces, "wide", split_axis=0, concat_axis=0, tiled=True)
     line = jnp.sum(line, axis=0)
     sums = direct_gather(line)
-    after, before, a_prev, a_next = lax.optimization_barrier((after, before, a_prev, a_next))
-    gas = (ga, after, *opposite(after, before), before)
     wanted = jnp.broadcast_to(order.reshape(64, 1, 4), (64, 4, 4))
     quarter = jnp.arange(4, dtype=jnp.int32).reshape(1, 4, 1)
     wanted = ((wanted // ATOMS) * 256 + quarter * ATOMS + wanted % ATOMS).reshape(1024, 1)
@@ -417,13 +427,13 @@
         compiler_params=params(8),
         name="deal",
     )(wanted)
-    gb, quad, a_prev, a_next, sums = lax.optimization_barrier((gb, quad, a_prev, a_next, sums))
+    gb, quad, a_prev, a_next, gas = lax.optimization_barrier((gb, quad, a_prev, a_next, gas))
     gbs = direct_gather(gb)
     lefts = (a_prev, a_first, a_mid, a_last, a_next)
     packed_outer, left_over = pl.pallas_call(
         lambda *refs: outer_kernel(rows_total, *refs),
         out_shape=[sds((1024, OUTER_CHUNK), BF16), sds((16, 1024), BF16)],
-        in_specs=[VM] * 15,
+        in_specs=[VM] * 18,
         out_specs=[VM, VM],
         scratch_shapes=[
             pltpu.VMEM((ROWS + 1, ORB, NARROW, 16, LANES), BF16),
@@ -439,7 +449,7 @@
     packed_inner = pl.pallas_call(
         lambda *refs: inner_kernel(rows_total, *refs),
         out_shape=sds((1024, INNER_CHUNK), BF16),
-        in_specs=[VM] * 20,
+        in_specs=[VM] * 23,
         out_specs=VM,
         scratch_shapes=[
             pltpu.VMEM((2 * ROWS + 1, ORB, NARROW, 16, LANES), BF16),

time: 160 us -> 165 us (1.031)
  waiting for transfers between devices: 72.8 us -> 74.8 us
    unnamed x36 -> x38, local copies, waits for them, and re-layouts: 5.96 us -> 9.79 us
    ppermute x4 -> x6, waiting for transfers between devices: 0.01 us -> 3 us  [the longest x3 1.69 us: down(): return lax.ppermute(value, 'narrow', shift_perm(NARROW, -1))]
    ppermute x4 -> x6, starting transfers between devices: 6.55 us -> 9.31 us  [the longest x3 9.3 us: up(): return lax.ppermute(value, 'narrow', shift_perm(NARROW, 1))]
    ppermute x6, waiting for transfers between devices: 9.48 us -> 7.03 us  [direct_gather(): lax.ppermute(own, 'narrow', shift_perm(NARROW, step))]
    all_to_all x2, waiting for transfers between devices: 60 us -> 62.3 us  [exchange(): got = lax.all_to_all(parts, 'wide', split_axis=0, concat_axis=0, tiled=True)]
    slice x2 -> x0, local copies, waits for them, and re-layouts: 1.7 us -> none  [opposite(): top, bottom = lax.optimization_barrier((after[:split], before[split:]))]
  transfers between devices with their start and end apart: 15 -> 17, of which waited for: 5 -> 7; matrix products, arithmetic and copies ran while one was open for 2% -> 0% of each run, Pallas kernels for 16% -> 16%
where the time goes in v5:
time: 165 us; the launch traced here: 164 us
  waiting for transfers between devices  74.8 us (45%)
  starting transfers between devices  49.1 us (30%)
  Pallas kernels  29.4 us (18%)
  local copies, waits for them, and re-layouts  10.1 us (6%)
    all_to_all x2, waiting for transfers between devices, exchange(): got = lax.all_to_all(parts, 'wide', split_axis=0, concat_axis=0, tiled=True)  62.3 us
    all_to_all x2, starting transfers between devices, exchange(): got = lax.all_to_all(parts, 'wide', split_axis=0, concat_axis=0, tiled=True)  15.5 us
    pallas_call x1, Pallas kernels, shards(): pl.pallas_call(lambda *refs: inner_kernel(rows_total, *refs), out_shape=s...  13.5 us
    all_to_all x1, starting transfers between devices, shards(): lax.all_to_all(traces, 'wide', split_axis=0, concat_axis=0, tiled=True)  12.1 us
    ppermute x6, starting transfers between devices, direct_gather(): lax.ppermute(own, 'narrow', shift_perm(NARROW, step))  10.3 us
    unnamed x38, local copies, waits for them, and re-layouts  9.79 us
    ppermute x3, starting transfers between devices, up(): return lax.ppermute(value, 'narrow', shift_perm(NARROW, 1))  9.3 us
    pallas_call x1, Pallas kernels, shards(): pl.pallas_call(lambda *refs: outer_kernel(rows_total, *refs), out_shape=[...  7.18 us
  transfers between devices with their start and end apart: 17, of which 7 were waited for; matrix products, arithmetic and copies ran while one was open for 0% of the time, Pallas kernels for 16%

profile of v5, /device:TPU:8, one launch (start us, length us, event | category | flops | bytes accessed | tf_op | source)
XLA Modules:
  0.0 164.1 jit_solution(8523721675316261466)
XLA Ops:
  0.0 1.6 copy-done
  2.2 1.1 prep_outer.1
  3.4 2.8 %collective-permute-start.5 = (bf16[80,2944]{1,0:T(8,128)(2,1)S(1)}, bf16[80,2944]{1,0:T(8,128)(2,1)}, u32[]{:S(2)}, u32[]{:S(2)}) collective-permute-start(bf16[80,2944]{1,0:T(8,128)(2,1)S(1)} %get-tuple-element.34.ga.refs_4_), channel_id=1, source_target_pairs={{0,3},{1,0},{2,1},{3,2},{4,7},{5,4},{6,5},{7,6},{8,11},{9,8},{10,9... | collective-permute-start | bytes 1413128 | tf_op jit(solution)/shard_map/ppermute | solution.py:356
  6.2 3.2 %collective-permute-start.6 = (bf16[64,2944]{1,0:T(8,128)(2,1)S(1)}, bf16[64,2944]{1,0:T(8,128)(2,1)S(1)}, u32[]{:S(2)}, u32[]{:S(2)}) collective-permute-start(bf16[64,2944]{1,0:T(8,128)(2,1)S(1)} %get-tuple-element.35.refs_5_), channel_id=1, source_target_pairs={{0,3},{1,0},{2,1},{3,2},{4,7},{5,4},{6,5},{7,6},{8,11},{9,8},{10,9... | collective-permute-start | bytes 1130504 | tf_op jit(solution)/shard_map/ppermute | solution.py:356
  9.5 3.1 %prep_inner.1 = (bf16[144,2304]{1,0:T(8,128)(2,1)S(1)}, bf16[3,144,640]{2,1,0:T(8,128)(2,1)}, bf16[2,3,144,640]{3,2,1,0:T(8,128)(2,1)S(1)}, bf16[3,144,640]{2,1,0:T(8,128)(2,1)}, f32[64,1,128]{2,1,0:T(1,128)}) custom-call(s32[256]{0:T(256)S(1)} %copy-done.6, bf16[3,9,144,256]{3,2,1,0:T(8,128)(2,1)S(1)} %bitcast.9, ...), custom_call_target="tpu_custom_call" | custom-call | tf_op jit(solution)/shard_map/prep_inner/pallas_call | solution.py:400
  12.6 1.0 copy-done.8
  13.6 0.8 copy-done.10
  14.5 12.1 %all-to-all-start = ((f32[64,1,128]{2,1,0:T(1,128)}), f32[64,1,128]{2,1,0:T(1,128)S(1)}, u32[]{:S(2)}, u32[]{:S(2)}) async-start(f32[64,1,128]{2,1,0:T(1,128)} %get-tuple-element.29), calls=%async_computation | async-start | bytes 65536 | tf_op jit(solution)/shard_map/all_to_all | solution.py:416
  26.9 1.7 %collective-permute-start.4 = (bf16[3,144,640]{2,1,0:T(8,128)(2,1)}, bf16[3,144,640]{2,1,0:T(8,128)(2,1)}, u32[]{:S(2)}, u32[]{:S(2)}) collective-permute-start(bf16[3,144,640]{2,1,0:T(8,128)(2,1)} %get-tuple-element.32.refs_13_.refs_17_), channel_id=1, source_target_pairs={{0,252},{4,0},{8,4},{12,8},{16,12},{20,16},{24,20},{28,24},{32,28}... | collective-permute-start | bytes 1658888 | tf_op jit(solution)/shard_map/ppermute | solution.py:415
  28.6 0.8 copy-done.12
  29.4 3.2 %collective-permute-start.7 = (bf16[80,2944]{1,0:T(8,128)(2,1)}, bf16[80,2944]{1,0:T(8,128)(2,1)}, u32[]{:S(2)}, u32[]{:S(2)}) collective-permute-start(bf16[80,2944]{1,0:T(8,128)(2,1)} %collective-permute-done.5.refs_6_), channel_id=1, source_target_pairs={{0,3},{1,0},{2,1},{3,2},{4,7},{5,4},{6,5},{7,6},{8,11},{9,8},{10,9... | collective-permute-start | bytes 1413128 | tf_op jit(solution)/shard_map/ppermute | solution.py:356
  33.4 1.7 %all-to-all-done = f32[64,1,128]{2,1,0:T(1,128)S(1)} async-done(((f32[64,1,128]{2,1,0:T(1,128)}), f32[64,1,128]{2,1,0:T(1,128)S(1)}, u32[]{:S(2)}, u32[]{:S(2)}) %all-to-all-start) | async-done | bytes 32800 | tf_op jit(solution)/shard_map/all_to_all | solution.py:416
  35.3 0.8 collective-permute-done.3.refs_12_.refs_16_
  36.1 3.9 %collective-permute-start.1 = (f32[1,128]{1,0:T(1,128)S(1)}, f32[1,128]{1,0:T(1,128)S(1)}, u32[]{:S(2)}, u32[]{:S(2)}) collective-permute-start(f32[1,128]{1,0:T(1,128)S(1)} %bitcast.13), channel_id=1, source_target_pairs={{0,2},{1,3},{2,0},{3,1},{4,6},{5,7},{6,4},{7,5},{8,10},{9,11},{10,... | collective-permute-start | bytes 1544 | tf_op jit(solution)/shard_map/ppermute | solution.py:370
  40.0 1.7 %collective-permute-done.9.refs_9_ = bf16[64,2944]{1,0:T(8,128)(2,1)} collective-permute-done((bf16[64,2944]{1,0:T(8,128)(2,1)}, bf16[64,2944]{1,0:T(8,128)(2,1)}, u32[]{:S(2)}, u32[]{:S(2)}) %collective-permute-start.9) | collective-permute-done | bytes 376864 | tf_op jit(solution)/shard_map/ppermute | solution.py:359
  41.7 1.3 collective-permute-done.7.refs_8_
  43.0 1.9 %collective-permute-start.13 = (bf16[144,2304]{1,0:T(8,128)(2,1)}, bf16[144,2304]{1,0:T(8,128)(2,1)}, u32[]{:S(2)}, u32[]{:S(2)}) collective-permute-start(bf16[144,2304]{1,0:T(8,128)(2,1)} %copy-done.10), channel_id=1, source_target_pairs={{0,1},{1,2},{2,3},{3,0},{4,5},{5,6},{6,7},{7,4},{8,9},{9,10},{10,1... | collective-permute-start | bytes 1990664 | tf_op jit(solution)/shard_map/ppermute | solution.py:370
  44.9 3.3 %collective-permute-start.12 = (bf16[144,2304]{1,0:T(8,128)(2,1)}, bf16[144,2304]{1,0:T(8,128)(2,1)}, u32[]{:S(2)}, u32[]{:S(2)}) collective-permute-start(bf16[144,2304]{1,0:T(8,128)(2,1)} %copy-done.10), channel_id=1, source_target_pairs={{0,2},{1,3},{2,0},{3,1},{4,6},{5,7},{6,4},{7,5},{8,10},{9,11},{10,... | collective-permute-start | bytes 1990664 | tf_op jit(solution)/shard_map/ppermute | solution.py:370
  48.2 1.1 collective-permute-start.11
  49.4 1.2 copy-done.9
  50.6 1.0 copy-done.13
  51.6 7.2 %outer.1 = (bf16[1024,640]{1,0:T(8,128)(2,1)}, bf16[16,1024]{1,0:T(8,128)(2,1)S(1)}) custom-call(f32[1,128]{1,0:T(1,128)S(1)} %bitcast.15, f32[1,128]{1,0:T(1,128)S(1)} %collective-permute-done.refs_1_, f32[1,128]{1,0:T(1,128)S(1)} %collective-permute-done.1.refs_2_, f32[1,128]{1,0:T(1,128)S(1)} %collective-permute-done.2.refs_3_, ...), custom_call_target="tpu_custom_call" | custom-call | flops 30000001024 | bytes 8388608 | tf_op jit(solution)/shard_map/outer/pallas_call | solution.py:433
  59.4 10.0 %all-to-all-start.1 = ((bf16[64,16,640]{2,1,0:T(8,128)(2,1)}), bf16[64,16,640]{2,1,0:T(8,128)(2,1)S(1)}, u32[]{:S(2)}, u32[]{:S(2)}) async-start(bf16[64,16,640]{2,1,0:T(8,128)(2,1)} %bitcast.2), calls=%async_computation.1 | async-start | bytes 2621440 | tf_op jit(solution)/shard_map/all_to_all | solution.py:375
  69.4 7.0 %collective-permute-done.12.refs_14_ = bf16[144,2304]{1,0:T(8,128)(2,1)} collective-permute-done((bf16[144,2304]{1,0:T(8,128)(2,1)}, bf16[144,2304]{1,0:T(8,128)(2,1)}, u32[]{:S(2)}, u32[]{:S(2)}) %collective-permute-start.12) | collective-permute-done | bytes 663584 | tf_op jit(solution)/shard_map/ppermute | solution.py:370
  76.5 13.5 %inner.1 = bf16[1024,1024]{1,0:T(8,128)(2,1)} custom-call(f32[1,128]{1,0:T(1,128)} %bitcast.16, f32[1,128]{1,0:T(1,128)} %copy-done.16, f32[1,128]{1,0:T(1,128)} %copy-done.15, f32[1,128]{1,0:T(1,128)} %copy-done.14, bf16[80,2944]{1,0:T(8,128)(2,1)} %copy-done.4, bf16[64,2944]{1,0:T(8,128)(2,1)} %copy-done.11, ...), custom_call_target="tpu_custom_call" | custom-call | flops 70000001024 | bytes 12582912 | tf_op jit(solution)/shard_map/inner/pallas_call | solution.py:449
  89.9 13.9 %all-to-all-done.1 = bf16[64,16,640]{2,1,0:T(8,128)(2,1)S(1)} async-done(((bf16[64,16,640]{2,1,0:T(8,128)(2,1)}), bf16[64,16,640]{2,1,0:T(8,128)(2,1)S(1)}, u32[]{:S(2)}, u32[]{:S(2)}) %all-to-all-start.1) | async-done | bytes 1310752 | tf_op jit(solution)/shard_map/all_to_all | solution.py:375
  103.8 5.5 %all-to-all-start.2 = ((bf16[64,16,1024]{2,1,0:T(8,128)(2,1)}), bf16[64,16,1024]{2,1,0:T(8,128)(2,1)S(1)}, u32[]{:S(2)}, u32[]{:S(2)}) async-start(bf16[64,16,1024]{2,1,0:T(8,128)(2,1)} %bitcast.17), calls=%async_computation.2 | async-start | bytes 4194304 | tf_op jit(solution)/shard_map/all_to_all | solution.py:375
  109.4 1.0 copy-done.1
  110.4 1.8 %unpack_outer.1.begun = bf16[9,720,256]{2,1,0:T(8,128)(2,1)} custom-call(bf16[1024,640]{1,0:T(8,128)(2,1)S(1)} %bitcast.11, bf16[512,512]{1,0:T(8,128)(2,1)S(1)} %copy-done.1), custom_call_target="tpu_custom_call" | custom-call | tf_op jit(solution)/shard_map/unpack_outer/pallas_call | solution.py:468
  112.3 48.4 %all-to-all-done.2 = bf16[64,16,1024]{2,1,0:T(8,128)(2,1)S(1)} async-done(((bf16[64,16,1024]{2,1,0:T(8,128)(2,1)}), bf16[64,16,1024]{2,1,0:T(8,128)(2,1)S(1)}, u32[]{:S(2)}, u32[]{:S(2)}) %all-to-all-start.2) | async-done | bytes 2097184 | tf_op jit(solution)/shard_map/all_to_all | solution.py:375
  160.6 1.0 copy-done.2
  161.7 2.3 %unpack_inner.1 = bf16[9,720,256]{2,1,0:T(8,128)(2,1)} custom-call(bf16[1024,1024]{1,0:T(8,128)(2,1)S(1)} %bitcast.10, bf16[512,512]{1,0:T(8,128)(2,1)S(1)} %copy-done.2, bf16[9,720,256]{2,1,0:T(8,128)(2,1)} %unpack_outer.1.begun), custom_call_target="tpu_custom_call", output_to_operand_aliasing={{}: (2, {})} | custom-call | tf_op jit(solution)/shard_map/unpack_inner/pallas_call | solution.py:480
  (54 shorter events, 2.6 us)
Async XLA Ops:
  0.0 9.5 %copy-start.6 = (s32[256]{0:T(256)S(1)}, s32[256]{0:T(256)}, u32[]{:S(2)}) copy-start(s32[256]{0:T(256)} %link.3) | copy-start | bytes 3076
  0.0 1.6 copy-start
  3.4 46.0 %copy-start.4 = (bf16[80,2944]{1,0:T(8,128)(2,1)}, bf16[80,2944]{1,0:T(8,128)(2,1)S(1)}, u32[]{:S(2)}) copy-start(bf16[80,2944]{1,0:T(8,128)(2,1)S(1)} %get-tuple-element.34.ga.refs_4_) | copy-start | bytes 1413124
  3.4 46.0 %copy-start.11 = (bf16[64,2944]{1,0:T(8,128)(2,1)}, bf16[64,2944]{1,0:T(8,128)(2,1)S(1)}, u32[]{:S(2)}) copy-start(bf16[64,2944]{1,0:T(8,128)(2,1)S(1)} %get-tuple-element.35.refs_5_) | copy-start | bytes 1130500
  3.4 23.4 %copy-start.18 = (s32[256]{0:T(256)S(1)}, s32[256]{0:T(256)}, u32[]{:S(2)}) copy-start(s32[256]{0:T(256)} %param.6) | copy-start | bytes 3076
  3.4 26.0 %collective-permute-start.5 = (bf16[80,2944]{1,0:T(8,128)(2,1)S(1)}, bf16[80,2944]{1,0:T(8,128)(2,1)}, u32[]{:S(2)}, u32[]{:S(2)}) collective-permute-start(bf16[80,2944]{1,0:T(8,128)(2,1)S(1)} %get-tuple-element.34.ga.refs_4_), channel_id=1, source_target_pairs={{0,3},{1,0},{2,1},{3,2},{4,7},{5,4},{6,5},{7,6},{8,11},{9,8},{10,9... | collective-permute-start | bytes 1413128 | tf_op jit(solution)/shard_map/ppermute | solution.py:356
  6.2 20.7 %collective-permute-start.8 = (bf16[64,2944]{1,0:T(8,128)(2,1)S(1)}, bf16[64,2944]{1,0:T(8,128)(2,1)}, u32[]{:S(2)}, u32[]{:S(2)}) collective-permute-start(bf16[64,2944]{1,0:T(8,128)(2,1)S(1)} %get-tuple-element.35.refs_5_), channel_id=1, source_target_pairs={{0,1},{1,2},{2,3},{3,0},{4,5},{5,6},{6,7},{7,4},{8,9},{9,10},{10,1... | collective-permute-start | bytes 1130504 | tf_op jit(solution)/shard_map/ppermute | solution.py:359
  6.2 22.4 %collective-permute-start.6 = (bf16[64,2944]{1,0:T(8,128)(2,1)S(1)}, bf16[64,2944]{1,0:T(8,128)(2,1)S(1)}, u32[]{:S(2)}, u32[]{:S(2)}) collective-permute-start(bf16[64,2944]{1,0:T(8,128)(2,1)S(1)} %get-tuple-element.35.refs_5_), channel_id=1, source_target_pairs={{0,3},{1,0},{2,1},{3,2},{4,7},{5,4},{6,5},{7,6},{8,11},{9,8},{10,9... | collective-permute-start | bytes 1130504 | tf_op jit(solution)/shard_map/ppermute | solution.py:356
  9.5 25.8 %collective-permute-start.10 = (bf16[80,2944]{1,0:T(8,128)(2,1)S(1)}, bf16[80,2944]{1,0:T(8,128)(2,1)}, u32[]{:S(2)}, u32[]{:S(2)}) collective-permute-start(bf16[80,2944]{1,0:T(8,128)(2,1)S(1)} %get-tuple-element.34.ga.refs_4_), channel_id=1, source_target_pairs={{0,1},{1,2},{2,3},{3,0},{4,5},{5,6},{6,7},{7,4},{8,9},{9,10},{10,1... | collective-permute-start | bytes 1413128 | tf_op jit(solution)/shard_map/ppermute | solution.py:359
  12.6 1.0 copy-start.8
  14.5 20.7 %all-to-all-start = ((f32[64,1,128]{2,1,0:T(1,128)}), f32[64,1,128]{2,1,0:T(1,128)S(1)}, u32[]{:S(2)}, u32[]{:S(2)}) async-start(f32[64,1,128]{2,1,0:T(1,128)} %get-tuple-element.29), calls=%async_computation | async-start | bytes 65536 | tf_op jit(solution)/shard_map/all_to_all | solution.py:416
  26.6 9.6 %collective-permute-start.3 = (bf16[3,144,640]{2,1,0:T(8,128)(2,1)}, bf16[3,144,640]{2,1,0:T(8,128)(2,1)}, u32[]{:S(2)}, u32[]{:S(2)}) collective-permute-start(bf16[3,144,640]{2,1,0:T(8,128)(2,1)} %get-tuple-element.31.refs_15_.refs_19_), channel_id=1, source_target_pairs={{0,4},{4,8},{8,12},{12,16},{16,20},{20,24},{24,28},{28,32},{32,36}... | collective-permute-start | bytes 1658888 | tf_op jit(solution)/shard_map/ppermute | solution.py:414
  26.9 13.1 %collective-permute-start.4 = (bf16[3,144,640]{2,1,0:T(8,128)(2,1)}, bf16[3,144,640]{2,1,0:T(8,128)(2,1)}, u32[]{:S(2)}, u32[]{:S(2)}) collective-permute-start(bf16[3,144,640]{2,1,0:T(8,128)(2,1)} %get-tuple-element.32.refs_13_.refs_17_), channel_id=1, source_target_pairs={{0,252},{4,0},{8,4},{12,8},{16,12},{20,16},{24,20},{28,24},{32,28}... | collective-permute-start | bytes 1658888 | tf_op jit(solution)/shard_map/ppermute | solution.py:415
  29.4 12.3 %collective-permute-start.9 = (bf16[64,2944]{1,0:T(8,128)(2,1)}, bf16[64,2944]{1,0:T(8,128)(2,1)}, u32[]{:S(2)}, u32[]{:S(2)}) collective-permute-start(bf16[64,2944]{1,0:T(8,128)(2,1)} %collective-permute-done.8.refs_11_), channel_id=1, source_target_pairs={{0,1},{1,2},{2,3},{3,0},{4,5},{5,6},{6,7},{7,4},{8,9},{9,10},{10,1... | collective-permute-start | bytes 1130504 | tf_op jit(solution)/shard_map/ppermute | solution.py:359
  29.4 13.6 %collective-permute-start.7 = (bf16[80,2944]{1,0:T(8,128)(2,1)}, bf16[80,2944]{1,0:T(8,128)(2,1)}, u32[]{:S(2)}, u32[]{:S(2)}) collective-permute-start(bf16[80,2944]{1,0:T(8,128)(2,1)} %collective-permute-done.5.refs_6_), channel_id=1, source_target_pairs={{0,3},{1,0},{2,1},{3,2},{4,7},{5,4},{6,5},{7,6},{8,11},{9,8},{10,9... | collective-permute-start | bytes 1413128 | tf_op jit(solution)/shard_map/ppermute | solution.py:356
  33.4 25.4 %copy-start.3 = (bf16[1024,1024]{1,0:T(8,128)(2,1)}, bf16[1024,1024]{1,0:T(8,128)(2,1)S(1)}, u32[]{:S(2)}) copy-start(bf16[1024,1024]{1,0:T(8,128)(2,1)S(1)} %deal.1.refs_17_.refs_21_) | copy-start | bytes 6291460
  35.2 23.5 %copy-start.7 = (f32[128]{0:T(128)}, f32[128]{0:T(128)S(1)}, u32[]{:S(2)}) copy-start(f32[128]{0:T(128)S(1)} %reduce_sum.11) | copy-start | bytes 1540
  35.2 12.9 %collective-permute-start.2 = (f32[1,128]{1,0:T(1,128)S(1)}, f32[1,128]{1,0:T(1,128)S(1)}, u32[]{:S(2)}, u32[]{:S(2)}) collective-permute-start(f32[1,128]{1,0:T(1,128)S(1)} %bitcast.12), channel_id=1, source_target_pairs={{0,1},{1,2},{2,3},{3,0},{4,5},{5,6},{6,7},{7,4},{8,9},{9,10},{10,1... | collective-permute-start | bytes 1544 | tf_op jit(solution)/shard_map/ppermute | solution.py:370
  36.1 13.2 %collective-permute-start.1 = (f32[1,128]{1,0:T(1,128)S(1)}, f32[1,128]{1,0:T(1,128)S(1)}, u32[]{:S(2)}, u32[]{:S(2)}) collective-permute-start(f32[1,128]{1,0:T(1,128)S(1)} %bitcast.13), channel_id=1, source_target_pairs={{0,2},{1,3},{2,0},{3,1},{4,6},{5,7},{6,4},{7,5},{8,10},{9,11},{10,... | collective-permute-start | bytes 1544 | tf_op jit(solution)/shard_map/ppermute | solution.py:370
  40.0 9.3 %collective-permute-start = (f32[1,128]{1,0:T(1,128)S(1)}, f32[1,128]{1,0:T(1,128)S(1)}, u32[]{:S(2)}, u32[]{:S(2)}) collective-permute-start(f32[1,128]{1,0:T(1,128)S(1)} %bitcast.14), channel_id=1, source_target_pairs={{0,3},{1,0},{2,1},{3,2},{4,7},{5,4},{6,5},{7,6},{8,11},{9,8},{10,9... | collective-permute-start | bytes 1544 | tf_op jit(solution)/shard_map/ppermute | solution.py:370
  43.0 26.4 %collective-permute-start.13 = (bf16[144,2304]{1,0:T(8,128)(2,1)}, bf16[144,2304]{1,0:T(8,128)(2,1)}, u32[]{:S(2)}, u32[]{:S(2)}) collective-permute-start(bf16[144,2304]{1,0:T(8,128)(2,1)} %copy-done.10), channel_id=1, source_target_pairs={{0,1},{1,2},{2,3},{3,0},{4,5},{5,6},{6,7},{7,4},{8,9},{9,10},{10,1... | collective-permute-start | bytes 1990664 | tf_op jit(solution)/shard_map/ppermute | solution.py:370
  44.9 31.6 %collective-permute-start.12 = (bf16[144,2304]{1,0:T(8,128)(2,1)}, bf16[144,2304]{1,0:T(8,128)(2,1)}, u32[]{:S(2)}, u32[]{:S(2)}) collective-permute-start(bf16[144,2304]{1,0:T(8,128)(2,1)} %copy-done.10), channel_id=1, source_target_pairs={{0,2},{1,3},{2,0},{3,1},{4,6},{5,7},{6,4},{7,5},{8,10},{9,11},{10,... | collective-permute-start | bytes 1990664 | tf_op jit(solution)/shard_map/ppermute | solution.py:370
  48.2 10.6 %copy-start.14 = (f32[1,128]{1,0:T(1,128)}, f32[1,128]{1,0:T(1,128)S(1)}, u32[]{:S(2)}) copy-start(f32[1,128]{1,0:T(1,128)S(1)} %collective-permute-done.2.refs_3_) | copy-start | bytes 1540
  48.2 28.3 %collective-permute-start.11 = (bf16[144,2304]{1,0:T(8,128)(2,1)}, bf16[144,2304]{1,0:T(8,128)(2,1)}, u32[]{:S(2)}, u32[]{:S(2)}) collective-permute-start(bf16[144,2304]{1,0:T(8,128)(2,1)} %copy-done.10), channel_id=1, source_target_pairs={{0,3},{1,0},{2,1},{3,2},{4,7},{5,4},{6,5},{7,6},{8,11},{9,8},{10,9... | collective-permute-start | bytes 1990664 | tf_op jit(solution)/shard_map/ppermute | solution.py:370
  49.3 9.5 %copy-start.15 = (f32[1,128]{1,0:T(1,128)}, f32[1,128]{1,0:T(1,128)S(1)}, u32[]{:S(2)}) copy-start(f32[1,128]{1,0:T(1,128)S(1)} %collective-permute-done.1.refs_2_) | copy-start | bytes 1540
  49.3 9.5 %copy-start.16 = (f32[1,128]{1,0:T(1,128)}, f32[1,128]{1,0:T(1,128)S(1)}, u32[]{:S(2)}) copy-start(f32[1,128]{1,0:T(1,128)S(1)} %collective-permute-done.refs_1_) | copy-start | bytes 1540
  49.3 1.2 copy-start.9
  50.6 1.0 copy-start.13
  59.4 44.4 %all-to-all-start.1 = ((bf16[64,16,640]{2,1,0:T(8,128)(2,1)}), bf16[64,16,640]{2,1,0:T(8,128)(2,1)S(1)}, u32[]{:S(2)}, u32[]{:S(2)}) async-start(bf16[64,16,640]{2,1,0:T(8,128)(2,1)} %bitcast.2), calls=%async_computation.1 | async-start | bytes 2621440 | tf_op jit(solution)/shard_map/all_to_all | solution.py:375
  103.8 56.8 %all-to-all-start.2 = ((bf16[64,16,1024]{2,1,0:T(8,128)(2,1)}), bf16[64,16,1024]{2,1,0:T(8,128)(2,1)S(1)}, u32[]{:S(2)}, u32[]{:S(2)}) async-start(bf16[64,16,1024]{2,1,0:T(8,128)(2,1)} %bitcast.17), calls=%async_computation.2 | async-start | bytes 4194304 | tf_op jit(solution)/shard_map/all_to_all | solution.py:375
  109.4 1.0 copy-start.1
  160.6 1.0 copy-start.2
  (4 other events, 2.9 us)

commit v6 on v4

--- a/solution.py
+++ b/solution.py
@@ -1,6 +1,5 @@
 import jax
 import jax.numpy as jnp
-import numpy as np
 from jax import lax
 from jax.experimental import pallas as pl
 from jax.experimental.pallas import tpu as pltpu
@@ -26,6 +25,7 @@
 VM = pl.BlockSpec(memory_space=pltpu.VMEM)
 SM = pl.BlockSpec(memory_space=pltpu.SMEM)
 ANY = pl.BlockSpec(memory_space=pl.ANY)
+HBM = pl.BlockSpec(memory_space=pltpu.HBM)
 sds = jax.ShapeDtypeStruct
 
 
@@ -176,7 +176,7 @@
 def outer_kernel(
     rows_total, sum0, sum1, sum2, sum3, ga0, ga1, ga2, ga3, ga4,
     a_prev, a_first, a_mid, a_last, a_next, quad,
-    out, left_over, full, rows,
+    out, left_over, full, rows, held, sems,
 ):
     gas = (ga0, ga1, ga2, ga3, ga4)
     twice = twice_weight((sum0, sum1, sum2, sum3), rows_total)
@@ -202,8 +202,17 @@
                 rows[576:640, lane : lane + ATOMS] = tail[half * 64 : half * 64 + 64]
             lane = r * 256 + s * ATOMS
             left_over[:, lane : lane + ATOMS] = tail[128:]
+    copies = []
     for k in range(0, 1024, 256):
-        out[k : k + 256, :] = nt(quad[k : k + 256, :], rows[...]).astype(BF16)
+        held[k : k + 256, :] = nt(quad[k : k + 256, :], rows[...]).astype(BF16)
+        copies.append(
+            pltpu.make_async_copy(
+                held.at[k : k + 256], out.at[k : k + 256], sems.at[len(copies)]
+            )
+        )
+        copies[-1].start()
+    for copy in copies:
+        copy.wait()
 
 
 def inner_kernel(
@@ -259,6 +268,13 @@
         out[k : k + 256, :] = nt(quad[k : k + 256, :], rows[...]).astype(BF16)
 
 
+def spread_matrix():
+    i = lax.broadcasted_iota(jnp.int32, (512, 512), 0)
+    lane = lax.broadcasted_iota(jnp.int32, (512, 512), 1)
+    wanted = ((i // 4) % 4) * 128 + (i // 16) * 4 + i % 4
+    return jnp.where(lane == wanted, 1.0, 0.0).astype(BF16)
+
+
 def spread_out(z, lanes, spread):
     for half in range(2):
         value = tn(z[half * 512 : (half + 1) * 512, lanes], spread[...]).astype(BF16)
@@ -266,7 +282,8 @@
             yield q, slice(half * 128, (half + 1) * 128), value[:, q * 128 : (q + 1) * 128]
 
 
-def unpack_outer_kernel(z, spread, out, held, sems):
+def unpack_outer_kernel(z, out, spread, held, sems):
+    spread[...] = spread_matrix()
     copies = []
 
     def send(o, s, high):
@@ -297,8 +314,9 @@
         copy.wait()
 
 
-def unpack_inner_kernel(z, spread, begun, out, held, edge, sems):
+def unpack_inner_kernel(z, begun, out, spread, held, edge, sems):
     del begun
+    spread[...] = spread_matrix()
     copies = []
 
     def send(src, dst):
@@ -330,13 +348,6 @@
             send(held.at[4 * g + q], out.at[4 * g + q, PANEL : 4 * PANEL])
     for copy in copies:
         copy.wait()
-
-
-def spread_matrix():
-    w, q, j = np.meshgrid(np.arange(32), np.arange(4), np.arange(4), indexing="ij")
-    table = np.zeros((512, 512), np.float32)
-    table[np.arange(512), (q * 128 + w * 4 + j).reshape(-1)] = 1.0
-    return table
 
 
 def shift_perm(count, step):
@@ -417,17 +428,19 @@
         compiler_params=params(8),
         name="deal",
     )(wanted)
-    gb, quad, a_prev, a_next, sums = lax.optimization_barrier((gb, quad, a_prev, a_next, sums))
+    gb, quad, a_prev, a_next = lax.optimization_barrier((gb, quad, a_prev, a_next))
     gbs = direct_gather(gb)
     lefts = (a_prev, a_first, a_mid, a_last, a_next)
     packed_outer, left_over = pl.pallas_call(
         lambda *refs: outer_kernel(rows_total, *refs),
         out_shape=[sds((1024, OUTER_CHUNK), BF16), sds((16, 1024), BF16)],
         in_specs=[VM] * 15,
-        out_specs=[VM, VM],
+        out_specs=[HBM, VM],
         scratch_shapes=[
             pltpu.VMEM((ROWS + 1, ORB, NARROW, 16, LANES), BF16),
             pltpu.VMEM((OUTER_CHUNK, 1024), BF16),
+            pltpu.VMEM((1024, OUTER_CHUNK), BF16),
+            pltpu.SemaphoreType.DMA((4,)),
         ],
         compiler_params=params(24),
         cost_estimate=pl.CostEstimate(
@@ -454,33 +467,34 @@
     )(*sums, *gas, *gbs, *lefts, quad, left_over)
     packed_inner, got_outer = lax.optimization_barrier((packed_inner, got_outer))
     got_inner = exchange(packed_inner, INNER_CHUNK)
-    spread = jnp.asarray(spread_matrix(), BF16)
     out = pl.pallas_call(
         unpack_outer_kernel,
         out_shape=sds((ORB, 5 * PANEL, 256), BF16),
-        in_specs=[VM, VM],
+        in_specs=[VM],
         out_specs=ANY,
         scratch_shapes=[
+            pltpu.VMEM((512, 512), BF16),
             pltpu.VMEM((ORB, 2, PANEL, 256), BF16),
             pltpu.SemaphoreType.DMA((18,)),
         ],
         compiler_params=params(14),
         name="unpack_outer",
-    )(got_outer, spread)
+    )(got_outer)
     out = pl.pallas_call(
         unpack_inner_kernel,
         out_shape=sds((ORB, 5 * PANEL, 256), BF16),
-        in_specs=[VM, VM, ANY],
+        in_specs=[VM, ANY],
         out_specs=ANY,
         scratch_shapes=[
+            pltpu.VMEM((512, 512), BF16),
             pltpu.VMEM((ORB, 3 * PANEL, 256), BF16),
             pltpu.VMEM((2, 16, 256), BF16),
             pltpu.SemaphoreType.DMA((11,)),
         ],
-        input_output_aliases={2: 0},
+        input_output_aliases={1: 0},
         compiler_params=params(16),
         name="unpack_inner",
-    )(got_inner, spread, out)
+    )(got_inner, out)
     return out.reshape(ORB, 5, PANEL, 256)
 
 

time: 160 us -> 158 us (0.988)
  local copies, waits for them, and re-layouts: 8.86 us -> 6.19 us
    unnamed x36 -> x32, local copies, waits for them, and re-layouts: 5.96 us -> 3.28 us
where the time goes in v6:
time: 158 us; the launch traced here: 157 us
  waiting for transfers between devices  73.7 us (47%)
  starting transfers between devices  47 us (30%)
  Pallas kernels  29 us (18%)
  local copies, waits for them, and re-layouts  6.19 us (4%)
    all_to_all x2, waiting for transfers between devices, exchange(): got = lax.all_to_all(parts, 'wide', split_axis=0, concat_axis=0, tiled=True)  60.6 us
    all_to_all x2, starting transfers between devices, exchange(): got = lax.all_to_all(parts, 'wide', split_axis=0, concat_axis=0, tiled=True)  16.5 us
    pallas_call x1, Pallas kernels, shards(): pl.pallas_call(lambda *refs: inner_kernel(rows_total, *refs), out_shape=s...  13.4 us
    all_to_all x1, starting transfers between devices, shards(): lax.all_to_all(traces, 'wide', split_axis=0, concat_axis=0, tiled=True)  12.8 us
    ppermute x6, waiting for transfers between devices, direct_gather(): lax.ppermute(own, 'narrow', shift_perm(NARROW, step))  9.7 us
    ppermute x6, starting transfers between devices, direct_gather(): lax.ppermute(own, 'narrow', shift_perm(NARROW, step))  9.42 us
    pallas_call x1, Pallas kernels, shards(): pl.pallas_call(lambda *refs: outer_kernel(rows_total, *refs), out_shape=[...  6.62 us
    all_to_all x1, waiting for transfers between devices, shards(): lax.all_to_all(traces, 'wide', split_axis=0, concat_axis=0, tiled=True)  3.33 us
  transfers between devices with their start and end apart: 15, of which 5 were waited for; matrix products, arithmetic and copies ran while one was open for 2% of the time, Pallas kernels for 16%

profile of v6, /device:TPU:8, one launch (start us, length us, event | category | flops | bytes accessed | tf_op | source)
XLA Modules:
  0.0 157.3 jit_solution(9640395855235158311)
XLA Ops:
  0.0 1.6 copy-done
  1.6 0.7 copy-done.5
  2.2 1.1 prep_outer.1.ga.refs_4_
  3.4 1.6 collective-permute-start.4
  4.9 1.7 %collective-permute-start.3 = (bf16[144,2944]{1,0:T(8,128)(2,1)S(1)}, bf16[144,2944]{1,0:T(8,128)(2,1)S(1)}, u32[]{:S(2)}, u32[]{:S(2)}) collective-permute-start(bf16[144,2944]{1,0:T(8,128)(2,1)S(1)} %prep_outer.1.ga.refs_4_), channel_id=1, source_target_pairs={{0,3},{1,0},{2,1},{3,2},{4,7},{5,4},{6,5},{7,6},{8,11},{9,8},{10,9... | collective-permute-start | bytes 2543624 | tf_op jit(solution)/shard_map/ppermute | solution.py:358
  6.7 3.2 %prep_inner.1 = (bf16[144,2304]{1,0:T(8,128)(2,1)}, bf16[3,144,640]{2,1,0:T(8,128)(2,1)}, bf16[2,3,144,640]{3,2,1,0:T(8,128)(2,1)S(1)}, bf16[3,144,640]{2,1,0:T(8,128)(2,1)}, f32[64,1,128]{2,1,0:T(1,128)}) custom-call(s32[256]{0:T(256)S(1)} %copy-done.6, bf16[3,9,144,256]{3,2,1,0:T(8,128)(2,1)S(1)} %bitcast.9, bf16[144,2944]{1,0:T(8,128)(2,1)S(1)} %prep_outer.1.ga.refs_4_), custom_call_target="tpu_custom_call" | custom-call | tf_op jit(solution)/shard_map/prep_inner/pallas_call | solution.py:399
  9.9 1.0 copy-done.8
  10.9 1.7 %collective-permute-start.6 = (bf16[3,144,640]{2,1,0:T(8,128)(2,1)}, bf16[3,144,640]{2,1,0:T(8,128)(2,1)}, u32[]{:S(2)}, u32[]{:S(2)}) collective-permute-start(bf16[3,144,640]{2,1,0:T(8,128)(2,1)} %get-tuple-element.26.refs_10_.refs_14_), channel_id=1, source_target_pairs={{0,252},{4,0},{8,4},{12,8},{16,12},{20,16},{24,20},{28,24},{32,28}... | collective-permute-start | bytes 1658888 | tf_op jit(solution)/shard_map/ppermute | solution.py:414
  12.6 12.8 %all-to-all-start = ((f32[64,1,128]{2,1,0:T(1,128)}), f32[64,1,128]{2,1,0:T(1,128)S(1)}, u32[]{:S(2)}, u32[]{:S(2)}) async-start(f32[64,1,128]{2,1,0:T(1,128)} %get-tuple-element.24), calls=%async_computation | async-start | bytes 65536 | tf_op jit(solution)/shard_map/all_to_all | solution.py:415
  25.6 0.9 slice.7
  26.5 0.8 slice.6
  27.3 1.1 collective-permute-start.8
  28.4 2.1 %collective-permute-start.7 = (bf16[80,2944]{1,0:T(8,128)(2,1)}, bf16[80,2944]{1,0:T(8,128)(2,1)S(1)}, u32[]{:S(2)}, u32[]{:S(2)}) collective-permute-start(bf16[80,2944]{1,0:T(8,128)(2,1)} %slice.6), channel_id=1, source_target_pairs={{0,3},{1,0},{2,1},{3,2},{4,7},{5,4},{6,5},{7,6},{8,11},{9,8},{10,9... | collective-permute-start | bytes 1413128 | tf_op jit(solution)/shard_map/ppermute | solution.py:366
  30.6 3.3 %all-to-all-done = f32[64,1,128]{2,1,0:T(1,128)S(1)} async-done(((f32[64,1,128]{2,1,0:T(1,128)}), f32[64,1,128]{2,1,0:T(1,128)S(1)}, u32[]{:S(2)}, u32[]{:S(2)}) %all-to-all-start) | async-done | bytes 32800 | tf_op jit(solution)/shard_map/all_to_all | solution.py:415
  34.4 0.8 add_add_fusion
  35.2 1.1 reshape.145.wanted
  36.3 2.8 %collective-permute-start.1 = (f32[1,128]{1,0:T(1,128)S(1)}, f32[1,128]{1,0:T(1,128)S(1)}, u32[]{:S(2)}, u32[]{:S(2)}) collective-permute-start(f32[1,128]{1,0:T(1,128)S(1)} %bitcast.13), channel_id=1, source_target_pairs={{0,2},{1,3},{2,0},{3,1},{4,6},{5,7},{6,4},{7,5},{8,10},{9,11},{10,... | collective-permute-start | bytes 1544 | tf_op jit(solution)/shard_map/ppermute | solution.py:372
  39.1 0.4 deal.1.refs_14_.refs_18_
  39.5 1.5 collective-permute-start
  41.0 0.6 collective-permute-start.11
  41.6 2.5 %collective-permute-start.10 = (bf16[144,2304]{1,0:T(8,128)(2,1)}, bf16[144,2304]{1,0:T(8,128)(2,1)}, u32[]{:S(2)}, u32[]{:S(2)}) collective-permute-start(bf16[144,2304]{1,0:T(8,128)(2,1)} %get-tuple-element.34.refs_9_), channel_id=1, source_target_pairs={{0,2},{1,3},{2,0},{3,1},{4,6},{5,7},{6,4},{7,5},{8,10},{9,11},{10,... | collective-permute-start | bytes 1990664 | tf_op jit(solution)/shard_map/ppermute | solution.py:372
  44.1 1.6 %collective-permute-start.9 = (bf16[144,2304]{1,0:T(8,128)(2,1)}, bf16[144,2304]{1,0:T(8,128)(2,1)}, u32[]{:S(2)}, u32[]{:S(2)}) collective-permute-start(bf16[144,2304]{1,0:T(8,128)(2,1)} %get-tuple-element.34.refs_9_), channel_id=1, source_target_pairs={{0,3},{1,0},{2,1},{3,2},{4,7},{5,4},{6,5},{7,6},{8,11},{9,8},{10,9... | collective-permute-start | bytes 1990664 | tf_op jit(solution)/shard_map/ppermute | solution.py:372
  45.8 6.6 %outer.1 = (bf16[1024,640]{1,0:T(8,128)(2,1)}, bf16[16,1024]{1,0:T(8,128)(2,1)S(1)}) custom-call(f32[1,128]{1,0:T(1,128)S(1)} %bitcast.15, f32[1,128]{1,0:T(1,128)S(1)} %collective-permute-done.refs_1_, f32[1,128]{1,0:T(1,128)S(1)} %collective-permute-done.1.refs_2_, f32[1,128]{1,0:T(1,128)S(1)} %collective-permute-done.2.refs_3_, ...), custom_call_target="tpu_custom_call" | custom-call | flops 30000001024 | bytes 8388608 | tf_op jit(solution)/shard_map/outer/pallas_call | solution.py:434
  52.5 11.0 %all-to-all-start.1 = ((bf16[64,16,640]{2,1,0:T(8,128)(2,1)}), bf16[64,16,640]{2,1,0:T(8,128)(2,1)S(1)}, u32[]{:S(2)}, u32[]{:S(2)}) async-start(bf16[64,16,640]{2,1,0:T(8,128)(2,1)} %bitcast.2), calls=%async_computation.1 | async-start | bytes 2621440 | tf_op jit(solution)/shard_map/all_to_all | solution.py:377
  63.5 9.1 %collective-permute-done.11.refs_12_ = bf16[144,2304]{1,0:T(8,128)(2,1)} collective-permute-done((bf16[144,2304]{1,0:T(8,128)(2,1)}, bf16[144,2304]{1,0:T(8,128)(2,1)}, u32[]{:S(2)}, u32[]{:S(2)}) %collective-permute-start.11) | collective-permute-done | bytes 663584 | tf_op jit(solution)/shard_map/ppermute | solution.py:372
  72.6 0.6 collective-permute-done.9.refs_10_
  73.2 13.4 %inner.1 = bf16[1024,1024]{1,0:T(8,128)(2,1)} custom-call(f32[1,128]{1,0:T(1,128)} %bitcast.16, f32[1,128]{1,0:T(1,128)} %copy-done.13, f32[1,128]{1,0:T(1,128)} %copy-done.12, f32[1,128]{1,0:T(1,128)} %copy-done.11, bf16[144,2944]{1,0:T(8,128)(2,1)} %copy-done.1, bf16[144,2944]{1,0:T(8,128)(2,1)} %copy-done.3, bf16[80,2944]{1,0:T(8,128)(2,1)} %copy-done.10, ...), custom_call_target="tpu_custom_call" | custom-call | flops 70000001024 | bytes 12582912 | tf_op jit(solution)/shard_map/inner/pallas_call | solution.py:452
  86.7 11.3 %all-to-all-done.1 = bf16[64,16,640]{2,1,0:T(8,128)(2,1)S(1)} async-done(((bf16[64,16,640]{2,1,0:T(8,128)(2,1)}), bf16[64,16,640]{2,1,0:T(8,128)(2,1)S(1)}, u32[]{:S(2)}, u32[]{:S(2)}) %all-to-all-start.1) | async-done | bytes 1310752 | tf_op jit(solution)/shard_map/all_to_all | solution.py:377
  98.0 5.5 %all-to-all-start.2 = ((bf16[64,16,1024]{2,1,0:T(8,128)(2,1)}), bf16[64,16,1024]{2,1,0:T(8,128)(2,1)S(1)}, u32[]{:S(2)}, u32[]{:S(2)}) async-start(bf16[64,16,1024]{2,1,0:T(8,128)(2,1)} %bitcast.17), calls=%async_computation.2 | async-start | bytes 4194304 | tf_op jit(solution)/shard_map/all_to_all | solution.py:377
  103.5 1.9 %unpack_outer.1.begun = bf16[9,720,256]{2,1,0:T(8,128)(2,1)} custom-call(bf16[1024,640]{1,0:T(8,128)(2,1)S(1)} %bitcast.11), custom_call_target="tpu_custom_call" | custom-call | tf_op jit(solution)/shard_map/unpack_outer/pallas_call | solution.py:470
  105.4 49.3 %all-to-all-done.2 = bf16[64,16,1024]{2,1,0:T(8,128)(2,1)S(1)} async-done(((bf16[64,16,1024]{2,1,0:T(8,128)(2,1)}), bf16[64,16,1024]{2,1,0:T(8,128)(2,1)S(1)}, u32[]{:S(2)}, u32[]{:S(2)}) %all-to-all-start.2) | async-done | bytes 2097184 | tf_op jit(solution)/shard_map/all_to_all | solution.py:377
  154.8 2.4 %unpack_inner.1 = bf16[9,720,256]{2,1,0:T(8,128)(2,1)} custom-call(bf16[1024,1024]{1,0:T(8,128)(2,1)S(1)} %bitcast.10, bf16[9,720,256]{2,1,0:T(8,128)(2,1)} %unpack_outer.1.begun), custom_call_target="tpu_custom_call", output_to_operand_aliasing={{}: (1, {})} | custom-call | tf_op jit(solution)/shard_map/unpack_inner/pallas_call | solution.py:483
  (46 shorter events, 0.7 us)
Async XLA Ops:
  0.0 1.6 copy-start
  1.6 0.7 copy-start.5
  2.2 4.5 %copy-start.6 = (s32[256]{0:T(256)S(1)}, s32[256]{0:T(256)}, u32[]{:S(2)}) copy-start(s32[256]{0:T(256)} %link.3) | copy-start | bytes 3076
  3.4 42.4 %copy-start.1 = (bf16[144,2944]{1,0:T(8,128)(2,1)}, bf16[144,2944]{1,0:T(8,128)(2,1)S(1)}, u32[]{:S(2)}) copy-start(bf16[144,2944]{1,0:T(8,128)(2,1)S(1)} %prep_outer.1.ga.refs_4_) | copy-start | bytes 2543620
  3.4 22.1 %copy-start.15 = (s32[256]{0:T(256)S(1)}, s32[256]{0:T(256)}, u32[]{:S(2)}) copy-start(s32[256]{0:T(256)} %param.5) | copy-start | bytes 3076
  3.4 22.2 %collective-permute-start.4 = (bf16[144,2944]{1,0:T(8,128)(2,1)S(1)}, bf16[144,2944]{1,0:T(8,128)(2,1)S(1)}, u32[]{:S(2)}, u32[]{:S(2)}) collective-permute-start(bf16[144,2944]{1,0:T(8,128)(2,1)S(1)} %prep_outer.1.ga.refs_4_), channel_id=1, source_target_pairs={{0,1},{1,2},{2,3},{3,0},{4,5},{5,6},{6,7},{7,4},{8,9},{9,10},{10,1... | collective-permute-start | bytes 2543624 | tf_op jit(solution)/shard_map/ppermute | solution.py:359
  4.9 20.7 %collective-permute-start.3 = (bf16[144,2944]{1,0:T(8,128)(2,1)S(1)}, bf16[144,2944]{1,0:T(8,128)(2,1)S(1)}, u32[]{:S(2)}, u32[]{:S(2)}) collective-permute-start(bf16[144,2944]{1,0:T(8,128)(2,1)S(1)} %prep_outer.1.ga.refs_4_), channel_id=1, source_target_pairs={{0,3},{1,0},{2,1},{3,2},{4,7},{5,4},{6,5},{7,6},{8,11},{9,8},{10,9... | collective-permute-start | bytes 2543624 | tf_op jit(solution)/shard_map/ppermute | solution.py:358
  9.9 1.0 copy-start.8
  10.9 14.7 %collective-permute-start.5 = (bf16[3,144,640]{2,1,0:T(8,128)(2,1)}, bf16[3,144,640]{2,1,0:T(8,128)(2,1)}, u32[]{:S(2)}, u32[]{:S(2)}) collective-permute-start(bf16[3,144,640]{2,1,0:T(8,128)(2,1)} %get-tuple-element.25.refs_12_.refs_16_), channel_id=1, source_target_pairs={{0,4},{4,8},{8,12},{12,16},{16,20},{20,24},{24,28},{28,32},{32,36}... | collective-permute-start | bytes 1658888 | tf_op jit(solution)/shard_map/ppermute | solution.py:413
  10.9 14.7 %collective-permute-start.6 = (bf16[3,144,640]{2,1,0:T(8,128)(2,1)}, bf16[3,144,640]{2,1,0:T(8,128)(2,1)}, u32[]{:S(2)}, u32[]{:S(2)}) collective-permute-start(bf16[3,144,640]{2,1,0:T(8,128)(2,1)} %get-tuple-element.26.refs_10_.refs_14_), channel_id=1, source_target_pairs={{0,252},{4,0},{8,4},{12,8},{16,12},{20,16},{24,20},{28,24},{32,28}... | collective-permute-start | bytes 1658888 | tf_op jit(solution)/shard_map/ppermute | solution.py:414
  12.6 21.3 %all-to-all-start = ((f32[64,1,128]{2,1,0:T(1,128)}), f32[64,1,128]{2,1,0:T(1,128)S(1)}, u32[]{:S(2)}, u32[]{:S(2)}) async-start(f32[64,1,128]{2,1,0:T(1,128)} %get-tuple-element.24), calls=%async_computation | async-start | bytes 65536 | tf_op jit(solution)/shard_map/all_to_all | solution.py:415
  25.6 20.2 %copy-start.4 = (bf16[144,2944]{1,0:T(8,128)(2,1)}, bf16[144,2944]{1,0:T(8,128)(2,1)S(1)}, u32[]{:S(2)}) copy-start(bf16[144,2944]{1,0:T(8,128)(2,1)S(1)} %collective-permute-done.4.refs_8_) | copy-start | bytes 2543620
  25.6 20.2 %copy-start.3 = (bf16[144,2944]{1,0:T(8,128)(2,1)}, bf16[144,2944]{1,0:T(8,128)(2,1)S(1)}, u32[]{:S(2)}) copy-start(bf16[144,2944]{1,0:T(8,128)(2,1)S(1)} %collective-permute-done.3.refs_5_) | copy-start | bytes 2543620
  27.3 18.5 %collective-permute-start.8 = (bf16[64,2944]{1,0:T(8,128)(2,1)}, bf16[64,2944]{1,0:T(8,128)(2,1)}, u32[]{:S(2)}, u32[]{:S(2)}) collective-permute-start(bf16[64,2944]{1,0:T(8,128)(2,1)} %slice.7), channel_id=1, source_target_pairs={{0,1},{1,2},{2,3},{3,0},{4,5},{5,6},{6,7},{7,4},{8,9},{9,10},{10,1... | collective-permute-start | bytes 1130504 | tf_op jit(solution)/shard_map/ppermute | solution.py:367
  28.4 17.4 %collective-permute-start.7 = (bf16[80,2944]{1,0:T(8,128)(2,1)}, bf16[80,2944]{1,0:T(8,128)(2,1)S(1)}, u32[]{:S(2)}, u32[]{:S(2)}) collective-permute-start(bf16[80,2944]{1,0:T(8,128)(2,1)} %slice.6), channel_id=1, source_target_pairs={{0,3},{1,0},{2,1},{3,2},{4,7},{5,4},{6,5},{7,6},{8,11},{9,8},{10,9... | collective-permute-start | bytes 1413128 | tf_op jit(solution)/shard_map/ppermute | solution.py:366
  34.0 18.4 %copy-start.7 = (f32[128]{0:T(128)}, f32[128]{0:T(128)S(1)}, u32[]{:S(2)}) copy-start(f32[128]{0:T(128)S(1)} %reduce_sum.11) | copy-start | bytes 1540
  34.0 7.0 %collective-permute-start.2 = (f32[1,128]{1,0:T(1,128)S(1)}, f32[1,128]{1,0:T(1,128)S(1)}, u32[]{:S(2)}, u32[]{:S(2)}) collective-permute-start(f32[1,128]{1,0:T(1,128)S(1)} %bitcast.12), channel_id=1, source_target_pairs={{0,1},{1,2},{2,3},{3,0},{4,5},{5,6},{6,7},{7,4},{8,9},{9,10},{10,1... | collective-permute-start | bytes 1544 | tf_op jit(solution)/shard_map/ppermute | solution.py:372
  36.3 9.6 %copy-start.9 = (bf16[2,3,144,640]{3,2,1,0:T(8,128)(2,1)S(1)}, bf16[2,3,144,640]{3,2,1,0:T(8,128)(2,1)}, u32[]{:S(2)}) copy-start(bf16[2,3,144,640]{3,2,1,0:T(8,128)(2,1)} %copy-done.8) | copy-start | bytes 3317764
  36.3 5.3 %collective-permute-start.1 = (f32[1,128]{1,0:T(1,128)S(1)}, f32[1,128]{1,0:T(1,128)S(1)}, u32[]{:S(2)}, u32[]{:S(2)}) collective-permute-start(f32[1,128]{1,0:T(1,128)S(1)} %bitcast.13), channel_id=1, source_target_pairs={{0,2},{1,3},{2,0},{3,1},{4,6},{5,7},{6,4},{7,5},{8,10},{9,11},{10,... | collective-permute-start | bytes 1544 | tf_op jit(solution)/shard_map/ppermute | solution.py:372
  39.5 13.0 %copy-start.2 = (bf16[1024,1024]{1,0:T(8,128)(2,1)}, bf16[1024,1024]{1,0:T(8,128)(2,1)S(1)}, u32[]{:S(2)}) copy-start(bf16[1024,1024]{1,0:T(8,128)(2,1)S(1)} %deal.1.refs_14_.refs_18_) | copy-start | bytes 6291460
  39.5 4.6 %collective-permute-start = (f32[1,128]{1,0:T(1,128)S(1)}, f32[1,128]{1,0:T(1,128)S(1)}, u32[]{:S(2)}, u32[]{:S(2)}) collective-permute-start(f32[1,128]{1,0:T(1,128)S(1)} %bitcast.14), channel_id=1, source_target_pairs={{0,3},{1,0},{2,1},{3,2},{4,7},{5,4},{6,5},{7,6},{8,11},{9,8},{10,9... | collective-permute-start | bytes 1544 | tf_op jit(solution)/shard_map/ppermute | solution.py:372
  41.0 11.4 %copy-start.11 = (f32[1,128]{1,0:T(1,128)}, f32[1,128]{1,0:T(1,128)S(1)}, u32[]{:S(2)}) copy-start(f32[1,128]{1,0:T(1,128)S(1)} %collective-permute-done.2.refs_3_) | copy-start | bytes 1540
  41.0 31.6 %collective-permute-start.11 = (bf16[144,2304]{1,0:T(8,128)(2,1)}, bf16[144,2304]{1,0:T(8,128)(2,1)}, u32[]{:S(2)}, u32[]{:S(2)}) collective-permute-start(bf16[144,2304]{1,0:T(8,128)(2,1)} %get-tuple-element.34.refs_9_), channel_id=1, source_target_pairs={{0,1},{1,2},{2,3},{3,0},{4,5},{5,6},{6,7},{7,4},{8,9},{9,10},{10,1... | collective-permute-start | bytes 1990664 | tf_op jit(solution)/shard_map/ppermute | solution.py:372
  41.6 10.9 %copy-start.12 = (f32[1,128]{1,0:T(1,128)}, f32[1,128]{1,0:T(1,128)S(1)}, u32[]{:S(2)}) copy-start(f32[1,128]{1,0:T(1,128)S(1)} %collective-permute-done.1.refs_2_) | copy-start | bytes 1540
  41.6 31.0 %collective-permute-start.10 = (bf16[144,2304]{1,0:T(8,128)(2,1)}, bf16[144,2304]{1,0:T(8,128)(2,1)}, u32[]{:S(2)}, u32[]{:S(2)}) collective-permute-start(bf16[144,2304]{1,0:T(8,128)(2,1)} %get-tuple-element.34.refs_9_), channel_id=1, source_target_pairs={{0,2},{1,3},{2,0},{3,1},{4,6},{5,7},{6,4},{7,5},{8,10},{9,11},{10,... | collective-permute-start | bytes 1990664 | tf_op jit(solution)/shard_map/ppermute | solution.py:372
  44.1 8.4 %copy-start.13 = (f32[1,128]{1,0:T(1,128)}, f32[1,128]{1,0:T(1,128)S(1)}, u32[]{:S(2)}) copy-start(f32[1,128]{1,0:T(1,128)S(1)} %collective-permute-done.refs_1_) | copy-start | bytes 1540
  44.1 29.1 %collective-permute-start.9 = (bf16[144,2304]{1,0:T(8,128)(2,1)}, bf16[144,2304]{1,0:T(8,128)(2,1)}, u32[]{:S(2)}, u32[]{:S(2)}) collective-permute-start(bf16[144,2304]{1,0:T(8,128)(2,1)} %get-tuple-element.34.refs_9_), channel_id=1, source_target_pairs={{0,3},{1,0},{2,1},{3,2},{4,7},{5,4},{6,5},{7,6},{8,11},{9,8},{10,9... | collective-permute-start | bytes 1990664 | tf_op jit(solution)/shard_map/ppermute | solution.py:372
  45.8 6.7 %copy-start.10 = (bf16[80,2944]{1,0:T(8,128)(2,1)}, bf16[80,2944]{1,0:T(8,128)(2,1)S(1)}, u32[]{:S(2)}) copy-start(bf16[80,2944]{1,0:T(8,128)(2,1)S(1)} %collective-permute-done.7.refs_6_) | copy-start | bytes 1413124
  52.5 20.7 %copy-start.14 = (bf16[16,1024]{1,0:T(8,128)(2,1)}, bf16[16,1024]{1,0:T(8,128)(2,1)S(1)}, u32[]{:S(2)}) copy-start(bf16[16,1024]{1,0:T(8,128)(2,1)S(1)} %get-tuple-element.39.refs_19_) | copy-start | bytes 98308
  52.5 45.4 %all-to-all-start.1 = ((bf16[64,16,640]{2,1,0:T(8,128)(2,1)}), bf16[64,16,640]{2,1,0:T(8,128)(2,1)S(1)}, u32[]{:S(2)}, u32[]{:S(2)}) async-start(bf16[64,16,640]{2,1,0:T(8,128)(2,1)} %bitcast.2), calls=%async_computation.1 | async-start | bytes 2621440 | tf_op jit(solution)/shard_map/all_to_all | solution.py:377
  98.0 56.8 %all-to-all-start.2 = ((bf16[64,16,1024]{2,1,0:T(8,128)(2,1)}), bf16[64,16,1024]{2,1,0:T(8,128)(2,1)S(1)}, u32[]{:S(2)}, u32[]{:S(2)}) async-start(bf16[64,16,1024]{2,1,0:T(8,128)(2,1)} %bitcast.17), calls=%async_computation.2 | async-start | bytes 4194304 | tf_op jit(solution)/shard_map/all_to_all | solution.py:377

commit v7 on v6

--- a/solution.py
+++ b/solution.py
@@ -137,7 +137,7 @@
 
 
 def twice_weight(sums, rows_total):
-    total = sums[0][...] + sums[1][...] + sums[2][...] + sums[3][...]
+    total = jnp.sum(sums[0][...] + sums[1][...] + sums[2][...] + sums[3][...], axis=0)
     tx = total[:, 0:1]
     sq = total[:, 1:2]
     return 2.0 * jax.nn.sigmoid(4.0 * (tx - sq) / (rows_total * BLOCK) + 5.0)
@@ -413,7 +413,6 @@
     a_prev = lax.ppermute(a_last, "wide", shift_perm(WIDE, -1))
     a_next = lax.ppermute(a_first, "wide", shift_perm(WIDE, 1))
     line = lax.all_to_all(traces, "wide", split_axis=0, concat_axis=0, tiled=True)
-    line = jnp.sum(line, axis=0)
     sums = direct_gather(line)
     after, before, a_prev, a_next = lax.optimization_barrier((after, before, a_prev, a_next))
     gas = (ga, after, *opposite(after, before), before)
@@ -428,7 +427,7 @@
         compiler_params=params(8),
         name="deal",
     )(wanted)
-    gb, quad, a_prev, a_next = lax.optimization_barrier((gb, quad, a_prev, a_next))
+    gb, quad, a_prev, a_next, *_ = lax.optimization_barrier((gb, quad, a_prev, a_next, sums[1]))
     gbs = direct_gather(gb)
     lefts = (a_prev, a_first, a_mid, a_last, a_next)
     packed_outer, left_over = pl.pallas_call(

time: 158 us -> 161 us (1.019)
    unnamed x32 -> x30, local copies, waits for them, and re-layouts: 3.28 us -> 3.9 us
where the time goes in v7:
time: 161 us; the launch traced here: 160 us
  waiting for transfers between devices  75.1 us (47%)
  starting transfers between devices  47.9 us (30%)
  Pallas kernels  29.1 us (18%)
  local copies, waits for them, and re-layouts  6.74 us (4%)
    all_to_all x2, waiting for transfers between devices, exchange(): got = lax.all_to_all(parts, 'wide', split_axis=0, concat_axis=0, tiled=True)  60.6 us
    all_to_all x2, starting transfers between devices, exchange(): got = lax.all_to_all(parts, 'wide', split_axis=0, concat_axis=0, tiled=True)  17.1 us
    pallas_call x1, Pallas kernels, shards(): pl.pallas_call(lambda *refs: inner_kernel(rows_total, *refs), out_shape=s...  13.5 us
    all_to_all x1, starting transfers between devices, shards(): lax.all_to_all(traces, 'wide', split_axis=0, concat_axis=0, tiled=True)  12.8 us
    ppermute x6, waiting for transfers between devices, direct_gather(): lax.ppermute(own, 'narrow', shift_perm(NARROW, step))  11.1 us
    ppermute x6, starting transfers between devices, direct_gather(): lax.ppermute(own, 'narrow', shift_perm(NARROW, step))  9.71 us
    pallas_call x1, Pallas kernels, shards(): pl.pallas_call(lambda *refs: outer_kernel(rows_total, *refs), out_shape=[...  6.61 us
    unnamed x30, local copies, waits for them, and re-layouts  3.9 us
  transfers between devices with their start and end apart: 15, of which 5 were waited for; matrix products, arithmetic and copies ran while one was open for 2% of the time, Pallas kernels for 16%

profile of v7, /device:TPU:8, one launch (start us, length us, event | category | flops | bytes accessed | tf_op | source)
XLA Modules:
  0.0 160.1 jit_solution(10351529104330879587)
XLA Ops:
  0.0 1.6 copy-done
  1.6 0.7 copy-done.6
  2.2 1.1 prep_outer.1.ga.refs_4_
  3.4 1.6 collective-permute-start.4
  4.9 1.7 %collective-permute-start.3 = (bf16[144,2944]{1,0:T(8,128)(2,1)S(1)}, bf16[144,2944]{1,0:T(8,128)(2,1)S(1)}, u32[]{:S(2)}, u32[]{:S(2)}) collective-permute-start(bf16[144,2944]{1,0:T(8,128)(2,1)S(1)} %prep_outer.1.ga.refs_4_), channel_id=1, source_target_pairs={{0,3},{1,0},{2,1},{3,2},{4,7},{5,4},{6,5},{7,6},{8,11},{9,8},{10,9... | collective-permute-start | bytes 2543624 | tf_op jit(solution)/shard_map/ppermute | solution.py:358
  6.7 3.2 %prep_inner.1 = (bf16[144,2304]{1,0:T(8,128)(2,1)}, bf16[3,144,640]{2,1,0:T(8,128)(2,1)}, bf16[2,3,144,640]{3,2,1,0:T(8,128)(2,1)S(1)}, bf16[3,144,640]{2,1,0:T(8,128)(2,1)}, f32[64,1,128]{2,1,0:T(1,128)}) custom-call(s32[256]{0:T(256)S(1)} %copy-done.7, bf16[3,9,144,256]{3,2,1,0:T(8,128)(2,1)S(1)} %bitcast.8, bf16[144,2944]{1,0:T(8,128)(2,1)S(1)} %prep_outer.1.ga.refs_4_), custom_call_target="tpu_custom_call" | custom-call | tf_op jit(solution)/shard_map/prep_inner/pallas_call | solution.py:399
  9.9 1.0 copy-done.8
  10.9 1.7 %collective-permute-start.6 = (bf16[3,144,640]{2,1,0:T(8,128)(2,1)}, bf16[3,144,640]{2,1,0:T(8,128)(2,1)}, u32[]{:S(2)}, u32[]{:S(2)}) collective-permute-start(bf16[3,144,640]{2,1,0:T(8,128)(2,1)} %get-tuple-element.26.refs_10_.refs_14_), channel_id=1, source_target_pairs={{0,252},{4,0},{8,4},{12,8},{16,12},{20,16},{24,20},{28,24},{32,28}... | collective-permute-start | bytes 1658888 | tf_op jit(solution)/shard_map/ppermute | solution.py:414
  12.6 12.8 %all-to-all-start = ((f32[64,1,128]{2,1,0:T(1,128)}), f32[64,1,128]{2,1,0:T(1,128)S(1)}, u32[]{:S(2)}, u32[]{:S(2)}) async-start(f32[64,1,128]{2,1,0:T(1,128)} %get-tuple-element.24), calls=%async_computation | async-start | bytes 65536 | tf_op jit(solution)/shard_map/all_to_all | solution.py:415
  25.6 0.8 slice.7
  26.5 0.8 slice.6
  27.3 1.1 collective-permute-start.8
  28.4 2.1 %collective-permute-start.7 = (bf16[80,2944]{1,0:T(8,128)(2,1)}, bf16[80,2944]{1,0:T(8,128)(2,1)}, u32[]{:S(2)}, u32[]{:S(2)}) collective-permute-start(bf16[80,2944]{1,0:T(8,128)(2,1)} %slice.6), channel_id=1, source_target_pairs={{0,3},{1,0},{2,1},{3,2},{4,7},{5,4},{6,5},{7,6},{8,11},{9,8},{10,9... | collective-permute-start | bytes 1413128 | tf_op jit(solution)/shard_map/ppermute | solution.py:366
  30.6 3.4 %all-to-all-done.refs_0_ = f32[64,1,128]{2,1,0:T(1,128)S(1)} async-done(((f32[64,1,128]{2,1,0:T(1,128)}), f32[64,1,128]{2,1,0:T(1,128)S(1)}, u32[]{:S(2)}, u32[]{:S(2)}) %all-to-all-start) | async-done | bytes 32800 | tf_op jit(solution)/shard_map/all_to_all | solution.py:415
  34.2 2.7 %collective-permute-start.1 = (f32[64,1,128]{2,1,0:T(1,128)S(1)}, f32[64,1,128]{2,1,0:T(1,128)S(1)}, u32[]{:S(2)}, u32[]{:S(2)}) collective-permute-start(f32[64,1,128]{2,1,0:T(1,128)S(1)} %all-to-all-done.refs_0_), channel_id=1, source_target_pairs={{0,2},{1,3},{2,0},{3,1},{4,6},{5,7},{6,4},{7,5},{8,10},{9,11},{10,... | collective-permute-start | bytes 98312 | tf_op jit(solution)/shard_map/ppermute | solution.py:372
  37.0 1.4 collective-permute-start
  38.4 0.8 add_add_fusion
  39.2 1.1 reshape.144.wanted
  40.3 0.4 deal.1.refs_14_.refs_18_
  40.7 1.5 collective-permute-done.refs_1_
  42.2 0.8 collective-permute-start.11
  43.0 4.5 %collective-permute-start.10 = (bf16[144,2304]{1,0:T(8,128)(2,1)}, bf16[144,2304]{1,0:T(8,128)(2,1)}, u32[]{:S(2)}, u32[]{:S(2)}) collective-permute-start(bf16[144,2304]{1,0:T(8,128)(2,1)} %get-tuple-element.34.refs_9_), channel_id=1, source_target_pairs={{0,2},{1,3},{2,0},{3,1},{4,6},{5,7},{6,4},{7,5},{8,10},{9,11},{10,... | collective-permute-start | bytes 1990664 | tf_op jit(solution)/shard_map/ppermute | solution.py:372
  47.6 6.6 %outer.1 = (bf16[1024,640]{1,0:T(8,128)(2,1)}, bf16[16,1024]{1,0:T(8,128)(2,1)S(1)}) custom-call(f32[64,1,128]{2,1,0:T(1,128)S(1)} %all-to-all-done.refs_0_, f32[64,1,128]{2,1,0:T(1,128)} %collective-permute-done.refs_1_, f32[64,1,128]{2,1,0:T(1,128)S(1)} %collective-permute-done.1.refs_2_, f32[64,1,128]{2,1,0:T(1,128)S(1)} %collective-permute-done.2.refs_3_, ...), custom_call_target="tpu_custom_call" | custom-call | flops 30000001024 | bytes 8388608 | tf_op jit(solution)/shard_map/outer/pallas_call | solution.py:433
  54.2 0.6 copy-done.13
  54.8 11.3 %all-to-all-start.1 = ((bf16[64,16,640]{2,1,0:T(8,128)(2,1)}), bf16[64,16,640]{2,1,0:T(8,128)(2,1)S(1)}, u32[]{:S(2)}, u32[]{:S(2)}) async-start(bf16[64,16,640]{2,1,0:T(8,128)(2,1)} %bitcast.1), calls=%async_computation.1 | async-start | bytes 2621440 | tf_op jit(solution)/shard_map/all_to_all | solution.py:377
  66.2 9.6 %collective-permute-done.10.refs_11_ = bf16[144,2304]{1,0:T(8,128)(2,1)} collective-permute-done((bf16[144,2304]{1,0:T(8,128)(2,1)}, bf16[144,2304]{1,0:T(8,128)(2,1)}, u32[]{:S(2)}, u32[]{:S(2)}) %collective-permute-start.10) | collective-permute-done | bytes 663584 | tf_op jit(solution)/shard_map/ppermute | solution.py:372
  75.8 13.5 %inner.1 = bf16[1024,1024]{1,0:T(8,128)(2,1)} custom-call(f32[64,1,128]{2,1,0:T(1,128)} %copy-done.5, f32[64,1,128]{2,1,0:T(1,128)} %collective-permute-done.refs_1_, f32[64,1,128]{2,1,0:T(1,128)} %copy-done.12, f32[64,1,128]{2,1,0:T(1,128)} %copy-done.11, bf16[144,2944]{1,0:T(8,128)(2,1)} %copy-done.1, bf16[144,2944]{1,0:T(8,128)(2,1)} %copy-done.3, ...), custom_call_target="tpu_custom_call" | custom-call | flops 70000001024 | bytes 12582912 | tf_op jit(solution)/shard_map/inner/pallas_call | solution.py:451
  89.3 11.3 %all-to-all-done.1 = bf16[64,16,640]{2,1,0:T(8,128)(2,1)S(1)} async-done(((bf16[64,16,640]{2,1,0:T(8,128)(2,1)}), bf16[64,16,640]{2,1,0:T(8,128)(2,1)S(1)}, u32[]{:S(2)}, u32[]{:S(2)}) %all-to-all-start.1) | async-done | bytes 1310752 | tf_op jit(solution)/shard_map/all_to_all | solution.py:377
  100.6 5.7 %all-to-all-start.2 = ((bf16[64,16,1024]{2,1,0:T(8,128)(2,1)}), bf16[64,16,1024]{2,1,0:T(8,128)(2,1)S(1)}, u32[]{:S(2)}, u32[]{:S(2)}) async-start(bf16[64,16,1024]{2,1,0:T(8,128)(2,1)} %bitcast.11), calls=%async_computation.2 | async-start | bytes 4194304 | tf_op jit(solution)/shard_map/all_to_all | solution.py:377
  106.3 1.9 %unpack_outer.1.begun = bf16[9,720,256]{2,1,0:T(8,128)(2,1)} custom-call(bf16[1024,640]{1,0:T(8,128)(2,1)S(1)} %bitcast.10), custom_call_target="tpu_custom_call" | custom-call | tf_op jit(solution)/shard_map/unpack_outer/pallas_call | solution.py:469
  108.3 49.3 %all-to-all-done.2 = bf16[64,16,1024]{2,1,0:T(8,128)(2,1)S(1)} async-done(((bf16[64,16,1024]{2,1,0:T(8,128)(2,1)}), bf16[64,16,1024]{2,1,0:T(8,128)(2,1)S(1)}, u32[]{:S(2)}, u32[]{:S(2)}) %all-to-all-start.2) | async-done | bytes 2097184 | tf_op jit(solution)/shard_map/all_to_all | solution.py:377
  157.6 2.4 %unpack_inner.1 = bf16[9,720,256]{2,1,0:T(8,128)(2,1)} custom-call(bf16[1024,1024]{1,0:T(8,128)(2,1)S(1)} %bitcast.9, bf16[9,720,256]{2,1,0:T(8,128)(2,1)} %unpack_outer.1.begun), custom_call_target="tpu_custom_call", output_to_operand_aliasing={{}: (1, {})} | custom-call | tf_op jit(solution)/shard_map/unpack_inner/pallas_call | solution.py:482
  (43 shorter events, 0.5 us)
Async XLA Ops:
  0.0 1.6 copy-start
  1.6 0.7 copy-start.6
  2.2 4.5 %copy-start.7 = (s32[256]{0:T(256)S(1)}, s32[256]{0:T(256)}, u32[]{:S(2)}) copy-start(s32[256]{0:T(256)} %link.3) | copy-start | bytes 3076
  3.4 44.2 %copy-start.1 = (bf16[144,2944]{1,0:T(8,128)(2,1)}, bf16[144,2944]{1,0:T(8,128)(2,1)S(1)}, u32[]{:S(2)}) copy-start(bf16[144,2944]{1,0:T(8,128)(2,1)S(1)} %prep_outer.1.ga.refs_4_) | copy-start | bytes 2543620
  3.4 22.1 %copy-start.14 = (s32[256]{0:T(256)S(1)}, s32[256]{0:T(256)}, u32[]{:S(2)}) copy-start(s32[256]{0:T(256)} %param.5) | copy-start | bytes 3076
  3.4 22.2 %collective-permute-start.4 = (bf16[144,2944]{1,0:T(8,128)(2,1)S(1)}, bf16[144,2944]{1,0:T(8,128)(2,1)S(1)}, u32[]{:S(2)}, u32[]{:S(2)}) collective-permute-start(bf16[144,2944]{1,0:T(8,128)(2,1)S(1)} %prep_outer.1.ga.refs_4_), channel_id=1, source_target_pairs={{0,1},{1,2},{2,3},{3,0},{4,5},{5,6},{6,7},{7,4},{8,9},{9,10},{10,1... | collective-permute-start | bytes 2543624 | tf_op jit(solution)/shard_map/ppermute | solution.py:359
  4.9 20.7 %collective-permute-start.3 = (bf16[144,2944]{1,0:T(8,128)(2,1)S(1)}, bf16[144,2944]{1,0:T(8,128)(2,1)S(1)}, u32[]{:S(2)}, u32[]{:S(2)}) collective-permute-start(bf16[144,2944]{1,0:T(8,128)(2,1)S(1)} %prep_outer.1.ga.refs_4_), channel_id=1, source_target_pairs={{0,3},{1,0},{2,1},{3,2},{4,7},{5,4},{6,5},{7,6},{8,11},{9,8},{10,9... | collective-permute-start | bytes 2543624 | tf_op jit(solution)/shard_map/ppermute | solution.py:358
  9.9 1.0 copy-start.8
  10.9 14.7 %collective-permute-start.5 = (bf16[3,144,640]{2,1,0:T(8,128)(2,1)}, bf16[3,144,640]{2,1,0:T(8,128)(2,1)}, u32[]{:S(2)}, u32[]{:S(2)}) collective-permute-start(bf16[3,144,640]{2,1,0:T(8,128)(2,1)} %get-tuple-element.25.refs_12_.refs_16_), channel_id=1, source_target_pairs={{0,4},{4,8},{8,12},{12,16},{16,20},{20,24},{24,28},{28,32},{32,36}... | collective-permute-start | bytes 1658888 | tf_op jit(solution)/shard_map/ppermute | solution.py:413
  10.9 14.7 %collective-permute-start.6 = (bf16[3,144,640]{2,1,0:T(8,128)(2,1)}, bf16[3,144,640]{2,1,0:T(8,128)(2,1)}, u32[]{:S(2)}, u32[]{:S(2)}) collective-permute-start(bf16[3,144,640]{2,1,0:T(8,128)(2,1)} %get-tuple-element.26.refs_10_.refs_14_), channel_id=1, source_target_pairs={{0,252},{4,0},{8,4},{12,8},{16,12},{20,16},{24,20},{28,24},{32,28}... | collective-permute-start | bytes 1658888 | tf_op jit(solution)/shard_map/ppermute | solution.py:414
  12.6 21.3 %all-to-all-start = ((f32[64,1,128]{2,1,0:T(1,128)}), f32[64,1,128]{2,1,0:T(1,128)S(1)}, u32[]{:S(2)}, u32[]{:S(2)}) async-start(f32[64,1,128]{2,1,0:T(1,128)} %get-tuple-element.24), calls=%async_computation | async-start | bytes 65536 | tf_op jit(solution)/shard_map/all_to_all | solution.py:415
  25.6 21.9 %copy-start.4 = (bf16[144,2944]{1,0:T(8,128)(2,1)}, bf16[144,2944]{1,0:T(8,128)(2,1)S(1)}, u32[]{:S(2)}) copy-start(bf16[144,2944]{1,0:T(8,128)(2,1)S(1)} %collective-permute-done.4.refs_8_) | copy-start | bytes 2543620
  25.6 21.9 %copy-start.3 = (bf16[144,2944]{1,0:T(8,128)(2,1)}, bf16[144,2944]{1,0:T(8,128)(2,1)S(1)}, u32[]{:S(2)}) copy-start(bf16[144,2944]{1,0:T(8,128)(2,1)S(1)} %collective-permute-done.3.refs_5_) | copy-start | bytes 2543620
  27.3 20.2 %collective-permute-start.8 = (bf16[64,2944]{1,0:T(8,128)(2,1)}, bf16[64,2944]{1,0:T(8,128)(2,1)S(1)}, u32[]{:S(2)}, u32[]{:S(2)}) collective-permute-start(bf16[64,2944]{1,0:T(8,128)(2,1)} %slice.7), channel_id=1, source_target_pairs={{0,1},{1,2},{2,3},{3,0},{4,5},{5,6},{6,7},{7,4},{8,9},{9,10},{10,1... | collective-permute-start | bytes 1130504 | tf_op jit(solution)/shard_map/ppermute | solution.py:367
  28.4 19.1 %collective-permute-start.7 = (bf16[80,2944]{1,0:T(8,128)(2,1)}, bf16[80,2944]{1,0:T(8,128)(2,1)}, u32[]{:S(2)}, u32[]{:S(2)}) collective-permute-start(bf16[80,2944]{1,0:T(8,128)(2,1)} %slice.6), channel_id=1, source_target_pairs={{0,3},{1,0},{2,1},{3,2},{4,7},{5,4},{6,5},{7,6},{8,11},{9,8},{10,9... | collective-permute-start | bytes 1413128 | tf_op jit(solution)/shard_map/ppermute | solution.py:366
  34.0 20.2 %copy-start.5 = (f32[64,1,128]{2,1,0:T(1,128)}, f32[64,1,128]{2,1,0:T(1,128)S(1)}, u32[]{:S(2)}) copy-start(f32[64,1,128]{2,1,0:T(1,128)S(1)} %all-to-all-done.refs_0_) | copy-start | bytes 98308
  34.0 9.0 %collective-permute-start.2 = (f32[64,1,128]{2,1,0:T(1,128)S(1)}, f32[64,1,128]{2,1,0:T(1,128)S(1)}, u32[]{:S(2)}, u32[]{:S(2)}) collective-permute-start(f32[64,1,128]{2,1,0:T(1,128)S(1)} %all-to-all-done.refs_0_), channel_id=1, source_target_pairs={{0,1},{1,2},{2,3},{3,0},{4,5},{5,6},{6,7},{7,4},{8,9},{9,10},{10,1... | collective-permute-start | bytes 98312 | tf_op jit(solution)/shard_map/ppermute | solution.py:372
  34.2 13.2 %collective-permute-start.1 = (f32[64,1,128]{2,1,0:T(1,128)S(1)}, f32[64,1,128]{2,1,0:T(1,128)S(1)}, u32[]{:S(2)}, u32[]{:S(2)}) collective-permute-start(f32[64,1,128]{2,1,0:T(1,128)S(1)} %all-to-all-done.refs_0_), channel_id=1, source_target_pairs={{0,2},{1,3},{2,0},{3,1},{4,6},{5,7},{6,4},{7,5},{8,10},{9,11},{10,... | collective-permute-start | bytes 98312 | tf_op jit(solution)/shard_map/ppermute | solution.py:372
  37.0 5.2 %collective-permute-start = (f32[64,1,128]{2,1,0:T(1,128)S(1)}, f32[64,1,128]{2,1,0:T(1,128)}, u32[]{:S(2)}, u32[]{:S(2)}) collective-permute-start(f32[64,1,128]{2,1,0:T(1,128)S(1)} %all-to-all-done.refs_0_), channel_id=1, source_target_pairs={{0,3},{1,0},{2,1},{3,2},{4,7},{5,4},{6,5},{7,6},{8,11},{9,8},{10,9... | collective-permute-start | bytes 98312 | tf_op jit(solution)/shard_map/ppermute | solution.py:372
  40.3 7.3 %copy-start.9 = (bf16[2,3,144,640]{3,2,1,0:T(8,128)(2,1)S(1)}, bf16[2,3,144,640]{3,2,1,0:T(8,128)(2,1)}, u32[]{:S(2)}) copy-start(bf16[2,3,144,640]{3,2,1,0:T(8,128)(2,1)} %copy-done.8) | copy-start | bytes 3317764
  40.7 13.5 %copy-start.2 = (bf16[1024,1024]{1,0:T(8,128)(2,1)}, bf16[1024,1024]{1,0:T(8,128)(2,1)S(1)}, u32[]{:S(2)}) copy-start(bf16[1024,1024]{1,0:T(8,128)(2,1)S(1)} %deal.1.refs_14_.refs_18_) | copy-start | bytes 6291460
  42.2 24.0 %collective-permute-start.11 = (bf16[144,2304]{1,0:T(8,128)(2,1)}, bf16[144,2304]{1,0:T(8,128)(2,1)}, u32[]{:S(2)}, u32[]{:S(2)}) collective-permute-start(bf16[144,2304]{1,0:T(8,128)(2,1)} %get-tuple-element.34.refs_9_), channel_id=1, source_target_pairs={{0,1},{1,2},{2,3},{3,0},{4,5},{5,6},{6,7},{7,4},{8,9},{9,10},{10,1... | collective-permute-start | bytes 1990664 | tf_op jit(solution)/shard_map/ppermute | solution.py:372
  43.0 11.2 %copy-start.11 = (f32[64,1,128]{2,1,0:T(1,128)}, f32[64,1,128]{2,1,0:T(1,128)S(1)}, u32[]{:S(2)}) copy-start(f32[64,1,128]{2,1,0:T(1,128)S(1)} %collective-permute-done.2.refs_3_) | copy-start | bytes 98308
  43.0 32.8 %collective-permute-start.10 = (bf16[144,2304]{1,0:T(8,128)(2,1)}, bf16[144,2304]{1,0:T(8,128)(2,1)}, u32[]{:S(2)}, u32[]{:S(2)}) collective-permute-start(bf16[144,2304]{1,0:T(8,128)(2,1)} %get-tuple-element.34.refs_9_), channel_id=1, source_target_pairs={{0,2},{1,3},{2,0},{3,1},{4,6},{5,7},{6,4},{7,5},{8,10},{9,11},{10,... | collective-permute-start | bytes 1990664 | tf_op jit(solution)/shard_map/ppermute | solution.py:372
  47.5 6.7 %copy-start.12 = (f32[64,1,128]{2,1,0:T(1,128)}, f32[64,1,128]{2,1,0:T(1,128)S(1)}, u32[]{:S(2)}) copy-start(f32[64,1,128]{2,1,0:T(1,128)S(1)} %collective-permute-done.1.refs_2_) | copy-start | bytes 98308
  47.5 28.3 %collective-permute-start.9 = (bf16[144,2304]{1,0:T(8,128)(2,1)}, bf16[144,2304]{1,0:T(8,128)(2,1)}, u32[]{:S(2)}, u32[]{:S(2)}) collective-permute-start(bf16[144,2304]{1,0:T(8,128)(2,1)} %get-tuple-element.34.refs_9_), channel_id=1, source_target_pairs={{0,3},{1,0},{2,1},{3,2},{4,7},{5,4},{6,5},{7,6},{8,11},{9,8},{10,9... | collective-permute-start | bytes 1990664 | tf_op jit(solution)/shard_map/ppermute | solution.py:372
  47.5 6.7 %copy-start.10 = (bf16[64,2944]{1,0:T(8,128)(2,1)}, bf16[64,2944]{1,0:T(8,128)(2,1)S(1)}, u32[]{:S(2)}) copy-start(bf16[64,2944]{1,0:T(8,128)(2,1)S(1)} %collective-permute-done.8.refs_7_) | copy-start | bytes 1130500
  54.2 0.6 copy-start.13
  54.8 45.7 %all-to-all-start.1 = ((bf16[64,16,640]{2,1,0:T(8,128)(2,1)}), bf16[64,16,640]{2,1,0:T(8,128)(2,1)S(1)}, u32[]{:S(2)}, u32[]{:S(2)}) async-start(bf16[64,16,640]{2,1,0:T(8,128)(2,1)} %bitcast.1), calls=%async_computation.1 | async-start | bytes 2621440 | tf_op jit(solution)/shard_map/all_to_all | solution.py:377
  100.6 57.0 %all-to-all-start.2 = ((bf16[64,16,1024]{2,1,0:T(8,128)(2,1)}), bf16[64,16,1024]{2,1,0:T(8,128)(2,1)S(1)}, u32[]{:S(2)}, u32[]{:S(2)}) async-start(bf16[64,16,1024]{2,1,0:T(8,128)(2,1)} %bitcast.11), calls=%async_computation.2 | async-start | bytes 4194304 | tf_op jit(solution)/shard_map/all_to_all | solution.py:377

commit v8 on v6

--- a/solution.py
+++ b/solution.py
@@ -407,7 +407,7 @@
         ],
         in_specs=[SM, VM, ANY],
         out_specs=[VM] * 5,
-        compiler_params=params(48),
+        compiler_params=params(52),
         name="prep_inner",
     )(link, x, ga)
     a_prev = lax.ppermute(a_last, "wide", shift_perm(WIDE, -1))

time: 158 us -> 158 us (level)
  transfers between devices with their start and end apart: 15 -> 15, of which waited for: 5 -> 5; matrix products, arithmetic and copies ran while one was open for 2% -> 2% of each run, Pallas kernels for 16% -> 17%
where the time goes in v8:
time: 158 us; the launch traced here: 157 us
  waiting for transfers between devices  73.7 us (47%)
  starting transfers between devices  46.7 us (30%)
  Pallas kernels  30.4 us (19%)
  local copies, waits for them, and re-layouts  5.19 us (3%)
    all_to_all x2, waiting for transfers between devices, exchange(): got = lax.all_to_all(parts, 'wide', split_axis=0, concat_axis=0, tiled=True)  60.3 us
    all_to_all x2, starting transfers between devices, exchange(): got = lax.all_to_all(parts, 'wide', split_axis=0, concat_axis=0, tiled=True)  16.2 us
    pallas_call x1, Pallas kernels, shards(): pl.pallas_call(lambda *refs: inner_kernel(rows_total, *refs), out_shape=s...  13.4 us
    all_to_all x1, starting transfers between devices, shards(): lax.all_to_all(traces, 'wide', split_axis=0, concat_axis=0, tiled=True)  12.8 us
    ppermute x6, waiting for transfers between devices, direct_gather(): lax.ppermute(own, 'narrow', shift_perm(NARROW, step))  10 us
    ppermute x6, starting transfers between devices, direct_gather(): lax.ppermute(own, 'narrow', shift_perm(NARROW, step))  9.42 us
    pallas_call x1, Pallas kernels, shards(): pl.pallas_call(lambda *refs: outer_kernel(rows_total, *refs), out_shape=[...  6.61 us
    pallas_call x1, Pallas kernels, shards(): pl.pallas_call(prep_inner_kernel, out_shape=[sds((PANEL, 2304), BF16), sd...  4.52 us
  transfers between devices with their start and end apart: 15, of which 5 were waited for; matrix products, arithmetic and copies ran while one was open for 2% of the time, Pallas kernels for 17%

profile of v8, /device:TPU:8, one launch (start us, length us, event | category | flops | bytes accessed | tf_op | source)
XLA Modules:
  0.0 157.3 jit_solution(3469513963937498826)
XLA Ops:
  0.0 1.6 copy-done
  1.6 0.7 copy-done.6
  2.2 1.1 prep_outer.1.ga.refs_4_
  3.4 1.6 collective-permute-start.4
  4.9 1.7 %collective-permute-start.3 = (bf16[144,2944]{1,0:T(8,128)(2,1)S(1)}, bf16[144,2944]{1,0:T(8,128)(2,1)S(1)}, u32[]{:S(2)}, u32[]{:S(2)}) collective-permute-start(bf16[144,2944]{1,0:T(8,128)(2,1)S(1)} %prep_outer.1.ga.refs_4_), channel_id=1, source_target_pairs={{0,3},{1,0},{2,1},{3,2},{4,7},{5,4},{6,5},{7,6},{8,11},{9,8},{10,9... | collective-permute-start | bytes 2543624 | tf_op jit(solution)/shard_map/ppermute | solution.py:358
  6.7 4.5 %prep_inner.1 = (bf16[144,2304]{1,0:T(8,128)(2,1)}, bf16[3,144,640]{2,1,0:T(8,128)(2,1)}, bf16[2,3,144,640]{3,2,1,0:T(8,128)(2,1)}, bf16[3,144,640]{2,1,0:T(8,128)(2,1)}, f32[64,1,128]{2,1,0:T(1,128)}) custom-call(s32[256]{0:T(256)S(1)} %copy-done.7, bf16[3,9,144,256]{3,2,1,0:T(8,128)(2,1)} %bitcast.7, bf16[144,2944]{1,0:T(8,128)(2,1)} %copy-done.1), custom_call_target="tpu_custom_call" | custom-call | tf_op jit(solution)/shard_map/prep_inner/pallas_call | solution.py:399
  11.2 1.7 %collective-permute-start.6 = (bf16[3,144,640]{2,1,0:T(8,128)(2,1)}, bf16[3,144,640]{2,1,0:T(8,128)(2,1)}, u32[]{:S(2)}, u32[]{:S(2)}) collective-permute-start(bf16[3,144,640]{2,1,0:T(8,128)(2,1)} %get-tuple-element.26.refs_10_.refs_14_), channel_id=1, source_target_pairs={{0,252},{4,0},{8,4},{12,8},{16,12},{20,16},{24,20},{28,24},{32,28}... | collective-permute-start | bytes 1658888 | tf_op jit(solution)/shard_map/ppermute | solution.py:414
  13.0 12.8 %all-to-all-start = ((f32[64,1,128]{2,1,0:T(1,128)}), f32[64,1,128]{2,1,0:T(1,128)S(1)}, u32[]{:S(2)}, u32[]{:S(2)}) async-start(f32[64,1,128]{2,1,0:T(1,128)} %get-tuple-element.24), calls=%async_computation | async-start | bytes 65536 | tf_op jit(solution)/shard_map/all_to_all | solution.py:415
  26.0 0.9 slice.7
  26.9 0.8 slice.6
  27.7 0.7 collective-permute-start.8
  28.4 2.5 %collective-permute-start.7 = (bf16[80,2944]{1,0:T(8,128)(2,1)}, bf16[80,2944]{1,0:T(8,128)(2,1)S(1)}, u32[]{:S(2)}, u32[]{:S(2)}) collective-permute-start(bf16[80,2944]{1,0:T(8,128)(2,1)} %slice.6), channel_id=1, source_target_pairs={{0,3},{1,0},{2,1},{3,2},{4,7},{5,4},{6,5},{7,6},{8,11},{9,8},{10,9... | collective-permute-start | bytes 1413128 | tf_op jit(solution)/shard_map/ppermute | solution.py:366
  31.0 3.3 %all-to-all-done = f32[64,1,128]{2,1,0:T(1,128)S(1)} async-done(((f32[64,1,128]{2,1,0:T(1,128)}), f32[64,1,128]{2,1,0:T(1,128)S(1)}, u32[]{:S(2)}, u32[]{:S(2)}) %all-to-all-start) | async-done | bytes 32800 | tf_op jit(solution)/shard_map/all_to_all | solution.py:415
  34.4 0.4 collective-permute-start.2
  34.7 0.8 add_add_fusion
  35.5 1.1 reshape.145.wanted
  36.6 2.8 %collective-permute-start.1 = (f32[1,128]{1,0:T(1,128)S(1)}, f32[1,128]{1,0:T(1,128)S(1)}, u32[]{:S(2)}, u32[]{:S(2)}) collective-permute-start(f32[1,128]{1,0:T(1,128)S(1)} %bitcast.13), channel_id=1, source_target_pairs={{0,2},{1,3},{2,0},{3,1},{4,6},{5,7},{6,4},{7,5},{8,10},{9,11},{10,... | collective-permute-start | bytes 1544 | tf_op jit(solution)/shard_map/ppermute | solution.py:372
  39.4 0.4 deal.1.refs_14_.refs_18_
  39.9 1.5 collective-permute-start
  41.4 0.6 collective-permute-start.11
  42.0 2.5 %collective-permute-start.10 = (bf16[144,2304]{1,0:T(8,128)(2,1)}, bf16[144,2304]{1,0:T(8,128)(2,1)}, u32[]{:S(2)}, u32[]{:S(2)}) collective-permute-start(bf16[144,2304]{1,0:T(8,128)(2,1)} %get-tuple-element.34.refs_9_), channel_id=1, source_target_pairs={{0,2},{1,3},{2,0},{3,1},{4,6},{5,7},{6,4},{7,5},{8,10},{9,11},{10,... | collective-permute-start | bytes 1990664 | tf_op jit(solution)/shard_map/ppermute | solution.py:372
  44.5 1.6 %collective-permute-start.9 = (bf16[144,2304]{1,0:T(8,128)(2,1)}, bf16[144,2304]{1,0:T(8,128)(2,1)}, u32[]{:S(2)}, u32[]{:S(2)}) collective-permute-start(bf16[144,2304]{1,0:T(8,128)(2,1)} %get-tuple-element.34.refs_9_), channel_id=1, source_target_pairs={{0,3},{1,0},{2,1},{3,2},{4,7},{5,4},{6,5},{7,6},{8,11},{9,8},{10,9... | collective-permute-start | bytes 1990664 | tf_op jit(solution)/shard_map/ppermute | solution.py:372
  46.2 6.6 %outer.1 = (bf16[1024,640]{1,0:T(8,128)(2,1)}, bf16[16,1024]{1,0:T(8,128)(2,1)S(1)}) custom-call(f32[1,128]{1,0:T(1,128)S(1)} %bitcast.15, f32[1,128]{1,0:T(1,128)S(1)} %collective-permute-done.refs_1_, f32[1,128]{1,0:T(1,128)S(1)} %collective-permute-done.1.refs_2_, f32[1,128]{1,0:T(1,128)S(1)} %collective-permute-done.2.refs_3_, ...), custom_call_target="tpu_custom_call" | custom-call | flops 30000001024 | bytes 8388608 | tf_op jit(solution)/shard_map/outer/pallas_call | solution.py:434
  52.9 10.7 %all-to-all-start.1 = ((bf16[64,16,640]{2,1,0:T(8,128)(2,1)}), bf16[64,16,640]{2,1,0:T(8,128)(2,1)S(1)}, u32[]{:S(2)}, u32[]{:S(2)}) async-start(bf16[64,16,640]{2,1,0:T(8,128)(2,1)} %bitcast.2), calls=%async_computation.1 | async-start | bytes 2621440 | tf_op jit(solution)/shard_map/all_to_all | solution.py:377
  63.5 9.4 %collective-permute-done.11.refs_12_ = bf16[144,2304]{1,0:T(8,128)(2,1)} collective-permute-done((bf16[144,2304]{1,0:T(8,128)(2,1)}, bf16[144,2304]{1,0:T(8,128)(2,1)}, u32[]{:S(2)}, u32[]{:S(2)}) %collective-permute-start.11) | collective-permute-done | bytes 663584 | tf_op jit(solution)/shard_map/ppermute | solution.py:372
  73.0 0.6 collective-permute-done.9.refs_10_
  73.6 13.4 %inner.1 = bf16[1024,1024]{1,0:T(8,128)(2,1)} custom-call(f32[1,128]{1,0:T(1,128)} %bitcast.16, f32[1,128]{1,0:T(1,128)} %copy-done.13, f32[1,128]{1,0:T(1,128)} %copy-done.12, f32[1,128]{1,0:T(1,128)} %copy-done.11, bf16[144,2944]{1,0:T(8,128)(2,1)} %copy-done.1, bf16[144,2944]{1,0:T(8,128)(2,1)} %copy-done.4, bf16[80,2944]{1,0:T(8,128)(2,1)} %copy-done.10, ...), custom_call_target="tpu_custom_call" | custom-call | flops 70000001024 | bytes 12582912 | tf_op jit(solution)/shard_map/inner/pallas_call | solution.py:452
  87.0 11.0 %all-to-all-done.1 = bf16[64,16,640]{2,1,0:T(8,128)(2,1)S(1)} async-done(((bf16[64,16,640]{2,1,0:T(8,128)(2,1)}), bf16[64,16,640]{2,1,0:T(8,128)(2,1)S(1)}, u32[]{:S(2)}, u32[]{:S(2)}) %all-to-all-start.1) | async-done | bytes 1310752 | tf_op jit(solution)/shard_map/all_to_all | solution.py:377
  98.0 5.5 %all-to-all-start.2 = ((bf16[64,16,1024]{2,1,0:T(8,128)(2,1)}), bf16[64,16,1024]{2,1,0:T(8,128)(2,1)S(1)}, u32[]{:S(2)}, u32[]{:S(2)}) async-start(bf16[64,16,1024]{2,1,0:T(8,128)(2,1)} %bitcast.17), calls=%async_computation.2 | async-start | bytes 4194304 | tf_op jit(solution)/shard_map/all_to_all | solution.py:377
  103.5 1.9 %unpack_outer.1.begun = bf16[9,720,256]{2,1,0:T(8,128)(2,1)} custom-call(bf16[1024,640]{1,0:T(8,128)(2,1)S(1)} %bitcast.11), custom_call_target="tpu_custom_call" | custom-call | tf_op jit(solution)/shard_map/unpack_outer/pallas_call | solution.py:470
  105.4 49.3 %all-to-all-done.2 = bf16[64,16,1024]{2,1,0:T(8,128)(2,1)S(1)} async-done(((bf16[64,16,1024]{2,1,0:T(8,128)(2,1)}), bf16[64,16,1024]{2,1,0:T(8,128)(2,1)S(1)}, u32[]{:S(2)}, u32[]{:S(2)}) %all-to-all-start.2) | async-done | bytes 2097184 | tf_op jit(solution)/shard_map/all_to_all | solution.py:377
  154.7 2.4 %unpack_inner.1 = bf16[9,720,256]{2,1,0:T(8,128)(2,1)} custom-call(bf16[1024,1024]{1,0:T(8,128)(2,1)S(1)} %bitcast.10, bf16[9,720,256]{2,1,0:T(8,128)(2,1)} %unpack_outer.1.begun), custom_call_target="tpu_custom_call", output_to_operand_aliasing={{}: (1, {})} | custom-call | tf_op jit(solution)/shard_map/unpack_inner/pallas_call | solution.py:483
  (46 shorter events, 0.3 us)
Async XLA Ops:
  0.0 1.6 copy-start
  1.6 0.7 copy-start.6
  2.2 4.5 %copy-start.7 = (s32[256]{0:T(256)S(1)}, s32[256]{0:T(256)}, u32[]{:S(2)}) copy-start(s32[256]{0:T(256)} %link.3) | copy-start | bytes 3076
  3.4 3.3 %copy-start.1 = (bf16[144,2944]{1,0:T(8,128)(2,1)}, bf16[144,2944]{1,0:T(8,128)(2,1)S(1)}, u32[]{:S(2)}) copy-start(bf16[144,2944]{1,0:T(8,128)(2,1)S(1)} %prep_outer.1.ga.refs_4_) | copy-start | bytes 2543620
  3.4 22.4 %copy-start.15 = (s32[256]{0:T(256)S(1)}, s32[256]{0:T(256)}, u32[]{:S(2)}) copy-start(s32[256]{0:T(256)} %param.5) | copy-start | bytes 3076
  3.4 22.6 %collective-permute-start.4 = (bf16[144,2944]{1,0:T(8,128)(2,1)S(1)}, bf16[144,2944]{1,0:T(8,128)(2,1)S(1)}, u32[]{:S(2)}, u32[]{:S(2)}) collective-permute-start(bf16[144,2944]{1,0:T(8,128)(2,1)S(1)} %prep_outer.1.ga.refs_4_), channel_id=1, source_target_pairs={{0,1},{1,2},{2,3},{3,0},{4,5},{5,6},{6,7},{7,4},{8,9},{9,10},{10,1... | collective-permute-start | bytes 2543624 | tf_op jit(solution)/shard_map/ppermute | solution.py:359
  4.9 21.0 %collective-permute-start.3 = (bf16[144,2944]{1,0:T(8,128)(2,1)S(1)}, bf16[144,2944]{1,0:T(8,128)(2,1)S(1)}, u32[]{:S(2)}, u32[]{:S(2)}) collective-permute-start(bf16[144,2944]{1,0:T(8,128)(2,1)S(1)} %prep_outer.1.ga.refs_4_), channel_id=1, source_target_pairs={{0,3},{1,0},{2,1},{3,2},{4,7},{5,4},{6,5},{7,6},{8,11},{9,8},{10,9... | collective-permute-start | bytes 2543624 | tf_op jit(solution)/shard_map/ppermute | solution.py:358
  11.2 14.7 %collective-permute-start.5 = (bf16[3,144,640]{2,1,0:T(8,128)(2,1)}, bf16[3,144,640]{2,1,0:T(8,128)(2,1)}, u32[]{:S(2)}, u32[]{:S(2)}) collective-permute-start(bf16[3,144,640]{2,1,0:T(8,128)(2,1)} %get-tuple-element.25.refs_12_.refs_16_), channel_id=1, source_target_pairs={{0,4},{4,8},{8,12},{12,16},{16,20},{20,24},{24,28},{28,32},{32,36}... | collective-permute-start | bytes 1658888 | tf_op jit(solution)/shard_map/ppermute | solution.py:413
  11.2 14.7 %collective-permute-start.6 = (bf16[3,144,640]{2,1,0:T(8,128)(2,1)}, bf16[3,144,640]{2,1,0:T(8,128)(2,1)}, u32[]{:S(2)}, u32[]{:S(2)}) collective-permute-start(bf16[3,144,640]{2,1,0:T(8,128)(2,1)} %get-tuple-element.26.refs_10_.refs_14_), channel_id=1, source_target_pairs={{0,252},{4,0},{8,4},{12,8},{16,12},{20,16},{24,20},{28,24},{32,28}... | collective-permute-start | bytes 1658888 | tf_op jit(solution)/shard_map/ppermute | solution.py:414
  13.0 21.3 %all-to-all-start = ((f32[64,1,128]{2,1,0:T(1,128)}), f32[64,1,128]{2,1,0:T(1,128)S(1)}, u32[]{:S(2)}, u32[]{:S(2)}) async-start(f32[64,1,128]{2,1,0:T(1,128)} %get-tuple-element.24), calls=%async_computation | async-start | bytes 65536 | tf_op jit(solution)/shard_map/all_to_all | solution.py:415
  25.9 20.2 %copy-start.5 = (bf16[144,2944]{1,0:T(8,128)(2,1)}, bf16[144,2944]{1,0:T(8,128)(2,1)S(1)}, u32[]{:S(2)}) copy-start(bf16[144,2944]{1,0:T(8,128)(2,1)S(1)} %collective-permute-done.4.refs_8_) | copy-start | bytes 2543620
  26.0 20.2 %copy-start.4 = (bf16[144,2944]{1,0:T(8,128)(2,1)}, bf16[144,2944]{1,0:T(8,128)(2,1)S(1)}, u32[]{:S(2)}) copy-start(bf16[144,2944]{1,0:T(8,128)(2,1)S(1)} %collective-permute-done.3.refs_5_) | copy-start | bytes 2543620
  26.9 19.3 %copy-start.2 = (bf16[144,2944]{1,0:T(8,128)(2,1)S(1)}, bf16[144,2944]{1,0:T(8,128)(2,1)}, u32[]{:S(2)}) copy-start(bf16[144,2944]{1,0:T(8,128)(2,1)} %copy-done.1) | copy-start | bytes 2543620
  27.7 18.4 %collective-permute-start.8 = (bf16[64,2944]{1,0:T(8,128)(2,1)}, bf16[64,2944]{1,0:T(8,128)(2,1)}, u32[]{:S(2)}, u32[]{:S(2)}) collective-permute-start(bf16[64,2944]{1,0:T(8,128)(2,1)} %slice.7), channel_id=1, source_target_pairs={{0,1},{1,2},{2,3},{3,0},{4,5},{5,6},{6,7},{7,4},{8,9},{9,10},{10,1... | collective-permute-start | bytes 1130504 | tf_op jit(solution)/shard_map/ppermute | solution.py:367
  28.4 17.7 %collective-permute-start.7 = (bf16[80,2944]{1,0:T(8,128)(2,1)}, bf16[80,2944]{1,0:T(8,128)(2,1)S(1)}, u32[]{:S(2)}, u32[]{:S(2)}) collective-permute-start(bf16[80,2944]{1,0:T(8,128)(2,1)} %slice.6), channel_id=1, source_target_pairs={{0,3},{1,0},{2,1},{3,2},{4,7},{5,4},{6,5},{7,6},{8,11},{9,8},{10,9... | collective-permute-start | bytes 1413128 | tf_op jit(solution)/shard_map/ppermute | solution.py:366
  34.4 18.4 %copy-start.8 = (f32[128]{0:T(128)}, f32[128]{0:T(128)S(1)}, u32[]{:S(2)}) copy-start(f32[128]{0:T(128)S(1)} %reduce_sum.11) | copy-start | bytes 1540
  34.4 7.0 %collective-permute-start.2 = (f32[1,128]{1,0:T(1,128)S(1)}, f32[1,128]{1,0:T(1,128)S(1)}, u32[]{:S(2)}, u32[]{:S(2)}) collective-permute-start(f32[1,128]{1,0:T(1,128)S(1)} %bitcast.12), channel_id=1, source_target_pairs={{0,1},{1,2},{2,3},{3,0},{4,5},{5,6},{6,7},{7,4},{8,9},{9,10},{10,1... | collective-permute-start | bytes 1544 | tf_op jit(solution)/shard_map/ppermute | solution.py:372
  36.6 9.6 %copy-start.9 = (bf16[2,3,144,640]{3,2,1,0:T(8,128)(2,1)S(1)}, bf16[2,3,144,640]{3,2,1,0:T(8,128)(2,1)}, u32[]{:S(2)}) copy-start(bf16[2,3,144,640]{3,2,1,0:T(8,128)(2,1)} %get-tuple-element.36.refs_11_.refs_15_) | copy-start | bytes 3317764
  36.6 5.4 %collective-permute-start.1 = (f32[1,128]{1,0:T(1,128)S(1)}, f32[1,128]{1,0:T(1,128)S(1)}, u32[]{:S(2)}, u32[]{:S(2)}) collective-permute-start(f32[1,128]{1,0:T(1,128)S(1)} %bitcast.13), channel_id=1, source_target_pairs={{0,2},{1,3},{2,0},{3,1},{4,6},{5,7},{6,4},{7,5},{8,10},{9,11},{10,... | collective-permute-start | bytes 1544 | tf_op jit(solution)/shard_map/ppermute | solution.py:372
  39.9 13.0 %copy-start.3 = (bf16[1024,1024]{1,0:T(8,128)(2,1)}, bf16[1024,1024]{1,0:T(8,128)(2,1)S(1)}, u32[]{:S(2)}) copy-start(bf16[1024,1024]{1,0:T(8,128)(2,1)S(1)} %deal.1.refs_14_.refs_18_) | copy-start | bytes 6291460
  39.9 4.6 %collective-permute-start = (f32[1,128]{1,0:T(1,128)S(1)}, f32[1,128]{1,0:T(1,128)S(1)}, u32[]{:S(2)}, u32[]{:S(2)}) collective-permute-start(f32[1,128]{1,0:T(1,128)S(1)} %bitcast.14), channel_id=1, source_target_pairs={{0,3},{1,0},{2,1},{3,2},{4,7},{5,4},{6,5},{7,6},{8,11},{9,8},{10,9... | collective-permute-start | bytes 1544 | tf_op jit(solution)/shard_map/ppermute | solution.py:372
  41.4 11.4 %copy-start.11 = (f32[1,128]{1,0:T(1,128)}, f32[1,128]{1,0:T(1,128)S(1)}, u32[]{:S(2)}) copy-start(f32[1,128]{1,0:T(1,128)S(1)} %collective-permute-done.2.refs_3_) | copy-start | bytes 1540
  41.4 31.6 %collective-permute-start.11 = (bf16[144,2304]{1,0:T(8,128)(2,1)}, bf16[144,2304]{1,0:T(8,128)(2,1)}, u32[]{:S(2)}, u32[]{:S(2)}) collective-permute-start(bf16[144,2304]{1,0:T(8,128)(2,1)} %get-tuple-element.34.refs_9_), channel_id=1, source_target_pairs={{0,1},{1,2},{2,3},{3,0},{4,5},{5,6},{6,7},{7,4},{8,9},{9,10},{10,1... | collective-permute-start | bytes 1990664 | tf_op jit(solution)/shard_map/ppermute | solution.py:372
  42.0 10.9 %copy-start.12 = (f32[1,128]{1,0:T(1,128)}, f32[1,128]{1,0:T(1,128)S(1)}, u32[]{:S(2)}) copy-start(f32[1,128]{1,0:T(1,128)S(1)} %collective-permute-done.1.refs_2_) | copy-start | bytes 1540
  42.0 31.0 %collective-permute-start.10 = (bf16[144,2304]{1,0:T(8,128)(2,1)}, bf16[144,2304]{1,0:T(8,128)(2,1)}, u32[]{:S(2)}, u32[]{:S(2)}) collective-permute-start(bf16[144,2304]{1,0:T(8,128)(2,1)} %get-tuple-element.34.refs_9_), channel_id=1, source_target_pairs={{0,2},{1,3},{2,0},{3,1},{4,6},{5,7},{6,4},{7,5},{8,10},{9,11},{10,... | collective-permute-start | bytes 1990664 | tf_op jit(solution)/shard_map/ppermute | solution.py:372
  44.5 8.3 %copy-start.13 = (f32[1,128]{1,0:T(1,128)}, f32[1,128]{1,0:T(1,128)S(1)}, u32[]{:S(2)}) copy-start(f32[1,128]{1,0:T(1,128)S(1)} %collective-permute-done.refs_1_) | copy-start | bytes 1540
  44.5 29.1 %collective-permute-start.9 = (bf16[144,2304]{1,0:T(8,128)(2,1)}, bf16[144,2304]{1,0:T(8,128)(2,1)}, u32[]{:S(2)}, u32[]{:S(2)}) collective-permute-start(bf16[144,2304]{1,0:T(8,128)(2,1)} %get-tuple-element.34.refs_9_), channel_id=1, source_target_pairs={{0,3},{1,0},{2,1},{3,2},{4,7},{5,4},{6,5},{7,6},{8,11},{9,8},{10,9... | collective-permute-start | bytes 1990664 | tf_op jit(solution)/shard_map/ppermute | solution.py:372
  46.1 6.7 %copy-start.10 = (bf16[80,2944]{1,0:T(8,128)(2,1)}, bf16[80,2944]{1,0:T(8,128)(2,1)S(1)}, u32[]{:S(2)}) copy-start(bf16[80,2944]{1,0:T(8,128)(2,1)S(1)} %collective-permute-done.7.refs_6_) | copy-start | bytes 1413124
  52.9 20.7 %copy-start.14 = (bf16[16,1024]{1,0:T(8,128)(2,1)}, bf16[16,1024]{1,0:T(8,128)(2,1)S(1)}, u32[]{:S(2)}) copy-start(bf16[16,1024]{1,0:T(8,128)(2,1)S(1)} %get-tuple-element.39.refs_19_) | copy-start | bytes 98308
  52.9 45.1 %all-to-all-start.1 = ((bf16[64,16,640]{2,1,0:T(8,128)(2,1)}), bf16[64,16,640]{2,1,0:T(8,128)(2,1)S(1)}, u32[]{:S(2)}, u32[]{:S(2)}) async-start(bf16[64,16,640]{2,1,0:T(8,128)(2,1)} %bitcast.2), calls=%async_computation.1 | async-start | bytes 2621440 | tf_op jit(solution)/shard_map/all_to_all | solution.py:377
  98.0 56.8 %all-to-all-start.2 = ((bf16[64,16,1024]{2,1,0:T(8,128)(2,1)}), bf16[64,16,1024]{2,1,0:T(8,128)(2,1)S(1)}, u32[]{:S(2)}, u32[]{:S(2)}) async-start(bf16[64,16,1024]{2,1,0:T(8,128)(2,1)} %bitcast.17), calls=%async_computation.2 | async-start | bytes 4194304 | tf_op jit(solution)/shard_map/all_to_all | solution.py:377

commit v9 on v8

--- a/solution.py
+++ b/solution.py
@@ -392,7 +392,7 @@
             pl.BlockSpec(slab, lambda i: (2, 0, 0, 0)),
         ],
         out_specs=pl.BlockSpec((PANEL, 2944), lambda i: (0, 0)),
-        compiler_params=params(48),
+        compiler_params=params(52),
         name="prep_outer",
     )(link, x, x)
     after, before = neighbours(ga)

time: 158 us -> 157 us (level)
  no operation moved by 1% of the time
where the time goes in v9:
time: 157 us; the launch traced here: 156 us
  waiting for transfers between devices  73.7 us (47%)
  starting transfers between devices  46.6 us (30%)
  Pallas kernels  31.2 us (20%)
  local copies, waits for them, and re-layouts  3.62 us (2%)
    all_to_all x2, waiting for transfers between devices, exchange(): got = lax.all_to_all(parts, 'wide', split_axis=0, concat_axis=0, tiled=True)  60.2 us
    all_to_all x2, starting transfers between devices, exchange(): got = lax.all_to_all(parts, 'wide', split_axis=0, concat_axis=0, tiled=True)  16.1 us
    pallas_call x1, Pallas kernels, shards(): pl.pallas_call(lambda *refs: inner_kernel(rows_total, *refs), out_shape=s...  13.4 us
    all_to_all x1, starting transfers between devices, shards(): lax.all_to_all(traces, 'wide', split_axis=0, concat_axis=0, tiled=True)  12.8 us
    ppermute x6, waiting for transfers between devices, direct_gather(): lax.ppermute(own, 'narrow', shift_perm(NARROW, step))  10.1 us
    ppermute x6, starting transfers between devices, direct_gather(): lax.ppermute(own, 'narrow', shift_perm(NARROW, step))  9.42 us
    pallas_call x1, Pallas kernels, shards(): pl.pallas_call(lambda *refs: outer_kernel(rows_total, *refs), out_shape=[...  6.63 us
    pallas_call x1, Pallas kernels, shards(): pl.pallas_call(prep_inner_kernel, out_shape=[sds((PANEL, 2304), BF16), sd...  4.53 us
  transfers between devices with their start and end apart: 15, of which 5 were waited for; matrix products, arithmetic and copies ran while one was open for 2% of the time, Pallas kernels for 17%

profile of v9, /device:TPU:8, one launch (start us, length us, event | category | flops | bytes accessed | tf_op | source)
XLA Modules:
  0.0 156.5 jit_solution(3138129603255089965)
XLA Ops:
  0.0 0.7 copy-done.5
  0.7 1.9 %prep_outer.1.ga.refs_4_ = bf16[144,2944]{1,0:T(8,128)(2,1)S(1)} custom-call(s32[256]{0:T(256)S(1)} %copy-done.5, bf16[3,9,144,256]{3,2,1,0:T(8,128)(2,1)} %bitcast.14, bf16[3,9,144,256]{3,2,1,0:T(8,128)(2,1)} %bitcast.15), custom_call_target="tpu_custom_call" | custom-call | tf_op jit(solution)/shard_map/prep_outer/pallas_call | solution.py:385
  2.6 1.6 %collective-permute-start.4 = (bf16[144,2944]{1,0:T(8,128)(2,1)S(1)}, bf16[144,2944]{1,0:T(8,128)(2,1)S(1)}, u32[]{:S(2)}, u32[]{:S(2)}) collective-permute-start(bf16[144,2944]{1,0:T(8,128)(2,1)S(1)} %prep_outer.1.ga.refs_4_), channel_id=1, source_target_pairs={{0,1},{1,2},{2,3},{3,0},{4,5},{5,6},{6,7},{7,4},{8,9},{9,10},{10,1... | collective-permute-start | bytes 2543624 | tf_op jit(solution)/shard_map/ppermute | solution.py:359
  4.2 1.7 %collective-permute-start.3 = (bf16[144,2944]{1,0:T(8,128)(2,1)S(1)}, bf16[144,2944]{1,0:T(8,128)(2,1)S(1)}, u32[]{:S(2)}, u32[]{:S(2)}) collective-permute-start(bf16[144,2944]{1,0:T(8,128)(2,1)S(1)} %prep_outer.1.ga.refs_4_), channel_id=1, source_target_pairs={{0,3},{1,0},{2,1},{3,2},{4,7},{5,4},{6,5},{7,6},{8,11},{9,8},{10,9... | collective-permute-start | bytes 2543624 | tf_op jit(solution)/shard_map/ppermute | solution.py:358
  5.9 4.5 %prep_inner.1 = (bf16[144,2304]{1,0:T(8,128)(2,1)}, bf16[3,144,640]{2,1,0:T(8,128)(2,1)}, bf16[2,3,144,640]{3,2,1,0:T(8,128)(2,1)}, bf16[3,144,640]{2,1,0:T(8,128)(2,1)}, f32[64,1,128]{2,1,0:T(1,128)}) custom-call(s32[256]{0:T(256)S(1)} %copy-done.6, bf16[3,9,144,256]{3,2,1,0:T(8,128)(2,1)} %bitcast.16, bf16[144,2944]{1,0:T(8,128)(2,1)} %copy-done), custom_call_target="tpu_custom_call" | custom-call | tf_op jit(solution)/shard_map/prep_inner/pallas_call | solution.py:399
  10.4 1.7 %collective-permute-start.6 = (bf16[3,144,640]{2,1,0:T(8,128)(2,1)}, bf16[3,144,640]{2,1,0:T(8,128)(2,1)}, u32[]{:S(2)}, u32[]{:S(2)}) collective-permute-start(bf16[3,144,640]{2,1,0:T(8,128)(2,1)} %get-tuple-element.26.refs_10_.refs_14_), channel_id=1, source_target_pairs={{0,252},{4,0},{8,4},{12,8},{16,12},{20,16},{24,20},{28,24},{32,28}... | collective-permute-start | bytes 1658888 | tf_op jit(solution)/shard_map/ppermute | solution.py:414
  12.2 12.8 %all-to-all-start = ((f32[64,1,128]{2,1,0:T(1,128)}), f32[64,1,128]{2,1,0:T(1,128)S(1)}, u32[]{:S(2)}, u32[]{:S(2)}) async-start(f32[64,1,128]{2,1,0:T(1,128)} %get-tuple-element.24), calls=%async_computation | async-start | bytes 65536 | tf_op jit(solution)/shard_map/all_to_all | solution.py:415
  25.0 0.1 broadcast_in_dim.17
  25.2 0.9 slice.7
  26.1 0.8 slice.6
  26.9 0.7 collective-permute-start.8
  27.6 2.5 %collective-permute-start.7 = (bf16[80,2944]{1,0:T(8,128)(2,1)}, bf16[80,2944]{1,0:T(8,128)(2,1)S(1)}, u32[]{:S(2)}, u32[]{:S(2)}) collective-permute-start(bf16[80,2944]{1,0:T(8,128)(2,1)} %slice.6), channel_id=1, source_target_pairs={{0,3},{1,0},{2,1},{3,2},{4,7},{5,4},{6,5},{7,6},{8,11},{9,8},{10,9... | collective-permute-start | bytes 1413128 | tf_op jit(solution)/shard_map/ppermute | solution.py:366
  30.2 3.4 %all-to-all-done = f32[64,1,128]{2,1,0:T(1,128)S(1)} async-done(((f32[64,1,128]{2,1,0:T(1,128)}), f32[64,1,128]{2,1,0:T(1,128)S(1)}, u32[]{:S(2)}, u32[]{:S(2)}) %all-to-all-start) | async-done | bytes 32800 | tf_op jit(solution)/shard_map/all_to_all | solution.py:415
  33.6 0.4 collective-permute-start.2
  34.0 0.8 add_add_fusion
  34.7 1.1 reshape.145.wanted
  35.9 2.8 %collective-permute-start.1 = (f32[1,128]{1,0:T(1,128)S(1)}, f32[1,128]{1,0:T(1,128)S(1)}, u32[]{:S(2)}, u32[]{:S(2)}) collective-permute-start(f32[1,128]{1,0:T(1,128)S(1)} %bitcast.10), channel_id=1, source_target_pairs={{0,2},{1,3},{2,0},{3,1},{4,6},{5,7},{6,4},{7,5},{8,10},{9,11},{10,... | collective-permute-start | bytes 1544 | tf_op jit(solution)/shard_map/ppermute | solution.py:372
  38.7 0.4 deal.1.refs_14_.refs_18_
  39.1 1.5 collective-permute-start
  40.6 0.6 collective-permute-start.11
  41.2 2.5 %collective-permute-start.10 = (bf16[144,2304]{1,0:T(8,128)(2,1)}, bf16[144,2304]{1,0:T(8,128)(2,1)}, u32[]{:S(2)}, u32[]{:S(2)}) collective-permute-start(bf16[144,2304]{1,0:T(8,128)(2,1)} %get-tuple-element.34.refs_9_), channel_id=1, source_target_pairs={{0,2},{1,3},{2,0},{3,1},{4,6},{5,7},{6,4},{7,5},{8,10},{9,11},{10,... | collective-permute-start | bytes 1990664 | tf_op jit(solution)/shard_map/ppermute | solution.py:372
  43.7 1.6 %collective-permute-start.9 = (bf16[144,2304]{1,0:T(8,128)(2,1)}, bf16[144,2304]{1,0:T(8,128)(2,1)}, u32[]{:S(2)}, u32[]{:S(2)}) collective-permute-start(bf16[144,2304]{1,0:T(8,128)(2,1)} %get-tuple-element.34.refs_9_), channel_id=1, source_target_pairs={{0,3},{1,0},{2,1},{3,2},{4,7},{5,4},{6,5},{7,6},{8,11},{9,8},{10,9... | collective-permute-start | bytes 1990664 | tf_op jit(solution)/shard_map/ppermute | solution.py:372
  45.4 6.6 %outer.1 = (bf16[1024,640]{1,0:T(8,128)(2,1)}, bf16[16,1024]{1,0:T(8,128)(2,1)S(1)}) custom-call(f32[1,128]{1,0:T(1,128)S(1)} %bitcast.12, f32[1,128]{1,0:T(1,128)S(1)} %collective-permute-done.refs_1_, f32[1,128]{1,0:T(1,128)S(1)} %collective-permute-done.1.refs_2_, f32[1,128]{1,0:T(1,128)S(1)} %collective-permute-done.2.refs_3_, ...), custom_call_target="tpu_custom_call" | custom-call | flops 30000001024 | bytes 8388608 | tf_op jit(solution)/shard_map/outer/pallas_call | solution.py:434
  52.1 10.6 %all-to-all-start.1 = ((bf16[64,16,640]{2,1,0:T(8,128)(2,1)}), bf16[64,16,640]{2,1,0:T(8,128)(2,1)S(1)}, u32[]{:S(2)}, u32[]{:S(2)}) async-start(bf16[64,16,640]{2,1,0:T(8,128)(2,1)} %bitcast.2), calls=%async_computation.1 | async-start | bytes 2621440 | tf_op jit(solution)/shard_map/all_to_all | solution.py:377
  62.7 9.4 %collective-permute-done.11.refs_12_ = bf16[144,2304]{1,0:T(8,128)(2,1)} collective-permute-done((bf16[144,2304]{1,0:T(8,128)(2,1)}, bf16[144,2304]{1,0:T(8,128)(2,1)}, u32[]{:S(2)}, u32[]{:S(2)}) %collective-permute-start.11) | collective-permute-done | bytes 663584 | tf_op jit(solution)/shard_map/ppermute | solution.py:372
  72.2 0.6 collective-permute-done.9.refs_10_
  72.8 13.4 %inner.1 = bf16[1024,1024]{1,0:T(8,128)(2,1)} custom-call(f32[1,128]{1,0:T(1,128)} %bitcast.13, f32[1,128]{1,0:T(1,128)} %copy-done.12, f32[1,128]{1,0:T(1,128)} %copy-done.11, f32[1,128]{1,0:T(1,128)} %copy-done.10, bf16[144,2944]{1,0:T(8,128)(2,1)} %copy-done, bf16[144,2944]{1,0:T(8,128)(2,1)} %copy-done.3, bf16[80,2944]{1,0:T(8,128)(2,1)} %copy-done.9, ...), custom_call_target="tpu_custom_call" | custom-call | flops 70000001024 | bytes 12582912 | tf_op jit(solution)/shard_map/inner/pallas_call | solution.py:452
  86.2 10.9 %all-to-all-done.1 = bf16[64,16,640]{2,1,0:T(8,128)(2,1)S(1)} async-done(((bf16[64,16,640]{2,1,0:T(8,128)(2,1)}), bf16[64,16,640]{2,1,0:T(8,128)(2,1)S(1)}, u32[]{:S(2)}, u32[]{:S(2)}) %all-to-all-start.1) | async-done | bytes 1310752 | tf_op jit(solution)/shard_map/all_to_all | solution.py:377
  97.2 5.5 %all-to-all-start.2 = ((bf16[64,16,1024]{2,1,0:T(8,128)(2,1)}), bf16[64,16,1024]{2,1,0:T(8,128)(2,1)S(1)}, u32[]{:S(2)}, u32[]{:S(2)}) async-start(bf16[64,16,1024]{2,1,0:T(8,128)(2,1)} %bitcast.17), calls=%async_computation.2 | async-start | bytes 4194304 | tf_op jit(solution)/shard_map/all_to_all | solution.py:377
  102.7 1.9 %unpack_outer.1.begun = bf16[9,720,256]{2,1,0:T(8,128)(2,1)} custom-call(bf16[1024,640]{1,0:T(8,128)(2,1)S(1)} %bitcast.8), custom_call_target="tpu_custom_call" | custom-call | tf_op jit(solution)/shard_map/unpack_outer/pallas_call | solution.py:470
  104.6 49.3 %all-to-all-done.2 = bf16[64,16,1024]{2,1,0:T(8,128)(2,1)S(1)} async-done(((bf16[64,16,1024]{2,1,0:T(8,128)(2,1)}), bf16[64,16,1024]{2,1,0:T(8,128)(2,1)S(1)}, u32[]{:S(2)}, u32[]{:S(2)}) %all-to-all-start.2) | async-done | bytes 2097184 | tf_op jit(solution)/shard_map/all_to_all | solution.py:377
  153.9 2.4 %unpack_inner.1 = bf16[9,720,256]{2,1,0:T(8,128)(2,1)} custom-call(bf16[1024,1024]{1,0:T(8,128)(2,1)S(1)} %bitcast.7, bf16[9,720,256]{2,1,0:T(8,128)(2,1)} %unpack_outer.1.begun), custom_call_target="tpu_custom_call", output_to_operand_aliasing={{}: (1, {})} | custom-call | tf_op jit(solution)/shard_map/unpack_inner/pallas_call | solution.py:483
  (44 shorter events, 0.2 us)
Async XLA Ops:
  0.0 0.7 copy-start.5
  0.7 5.2 %copy-start.6 = (s32[256]{0:T(256)S(1)}, s32[256]{0:T(256)}, u32[]{:S(2)}) copy-start(s32[256]{0:T(256)} %link.3) | copy-start | bytes 3076
  2.6 3.3 %copy-start = (bf16[144,2944]{1,0:T(8,128)(2,1)}, bf16[144,2944]{1,0:T(8,128)(2,1)S(1)}, u32[]{:S(2)}) copy-start(bf16[144,2944]{1,0:T(8,128)(2,1)S(1)} %prep_outer.1.ga.refs_4_) | copy-start | bytes 2543620
  2.6 22.4 %copy-start.14 = (s32[256]{0:T(256)S(1)}, s32[256]{0:T(256)}, u32[]{:S(2)}) copy-start(s32[256]{0:T(256)} %param.5) | copy-start | bytes 3076
  2.6 22.6 %collective-permute-start.4 = (bf16[144,2944]{1,0:T(8,128)(2,1)S(1)}, bf16[144,2944]{1,0:T(8,128)(2,1)S(1)}, u32[]{:S(2)}, u32[]{:S(2)}) collective-permute-start(bf16[144,2944]{1,0:T(8,128)(2,1)S(1)} %prep_outer.1.ga.refs_4_), channel_id=1, source_target_pairs={{0,1},{1,2},{2,3},{3,0},{4,5},{5,6},{6,7},{7,4},{8,9},{9,10},{10,1... | collective-permute-start | bytes 2543624 | tf_op jit(solution)/shard_map/ppermute | solution.py:359
  4.2 21.0 %collective-permute-start.3 = (bf16[144,2944]{1,0:T(8,128)(2,1)S(1)}, bf16[144,2944]{1,0:T(8,128)(2,1)S(1)}, u32[]{:S(2)}, u32[]{:S(2)}) collective-permute-start(bf16[144,2944]{1,0:T(8,128)(2,1)S(1)} %prep_outer.1.ga.refs_4_), channel_id=1, source_target_pairs={{0,3},{1,0},{2,1},{3,2},{4,7},{5,4},{6,5},{7,6},{8,11},{9,8},{10,9... | collective-permute-start | bytes 2543624 | tf_op jit(solution)/shard_map/ppermute | solution.py:358
  10.4 14.7 %collective-permute-start.5 = (bf16[3,144,640]{2,1,0:T(8,128)(2,1)}, bf16[3,144,640]{2,1,0:T(8,128)(2,1)}, u32[]{:S(2)}, u32[]{:S(2)}) collective-permute-start(bf16[3,144,640]{2,1,0:T(8,128)(2,1)} %get-tuple-element.25.refs_12_.refs_16_), channel_id=1, source_target_pairs={{0,4},{4,8},{8,12},{12,16},{16,20},{20,24},{24,28},{28,32},{32,36}... | collective-permute-start | bytes 1658888 | tf_op jit(solution)/shard_map/ppermute | solution.py:413
  10.4 14.7 %collective-permute-start.6 = (bf16[3,144,640]{2,1,0:T(8,128)(2,1)}, bf16[3,144,640]{2,1,0:T(8,128)(2,1)}, u32[]{:S(2)}, u32[]{:S(2)}) collective-permute-start(bf16[3,144,640]{2,1,0:T(8,128)(2,1)} %get-tuple-element.26.refs_10_.refs_14_), channel_id=1, source_target_pairs={{0,252},{4,0},{8,4},{12,8},{16,12},{20,16},{24,20},{28,24},{32,28}... | collective-permute-start | bytes 1658888 | tf_op jit(solution)/shard_map/ppermute | solution.py:414
  12.2 21.3 %all-to-all-start = ((f32[64,1,128]{2,1,0:T(1,128)}), f32[64,1,128]{2,1,0:T(1,128)S(1)}, u32[]{:S(2)}, u32[]{:S(2)}) async-start(f32[64,1,128]{2,1,0:T(1,128)} %get-tuple-element.24), calls=%async_computation | async-start | bytes 65536 | tf_op jit(solution)/shard_map/all_to_all | solution.py:415
  25.2 20.2 %copy-start.4 = (bf16[144,2944]{1,0:T(8,128)(2,1)}, bf16[144,2944]{1,0:T(8,128)(2,1)S(1)}, u32[]{:S(2)}) copy-start(bf16[144,2944]{1,0:T(8,128)(2,1)S(1)} %collective-permute-done.4.refs_8_) | copy-start | bytes 2543620
  25.2 20.2 %copy-start.3 = (bf16[144,2944]{1,0:T(8,128)(2,1)}, bf16[144,2944]{1,0:T(8,128)(2,1)S(1)}, u32[]{:S(2)}) copy-start(bf16[144,2944]{1,0:T(8,128)(2,1)S(1)} %collective-permute-done.3.refs_5_) | copy-start | bytes 2543620
  26.1 19.3 %copy-start.1 = (bf16[144,2944]{1,0:T(8,128)(2,1)S(1)}, bf16[144,2944]{1,0:T(8,128)(2,1)}, u32[]{:S(2)}) copy-start(bf16[144,2944]{1,0:T(8,128)(2,1)} %copy-done) | copy-start | bytes 2543620
  26.9 18.5 %collective-permute-start.8 = (bf16[64,2944]{1,0:T(8,128)(2,1)}, bf16[64,2944]{1,0:T(8,128)(2,1)}, u32[]{:S(2)}, u32[]{:S(2)}) collective-permute-start(bf16[64,2944]{1,0:T(8,128)(2,1)} %slice.7), channel_id=1, source_target_pairs={{0,1},{1,2},{2,3},{3,0},{4,5},{5,6},{6,7},{7,4},{8,9},{9,10},{10,1... | collective-permute-start | bytes 1130504 | tf_op jit(solution)/shard_map/ppermute | solution.py:367
  27.6 17.7 %collective-permute-start.7 = (bf16[80,2944]{1,0:T(8,128)(2,1)}, bf16[80,2944]{1,0:T(8,128)(2,1)S(1)}, u32[]{:S(2)}, u32[]{:S(2)}) collective-permute-start(bf16[80,2944]{1,0:T(8,128)(2,1)} %slice.6), channel_id=1, source_target_pairs={{0,3},{1,0},{2,1},{3,2},{4,7},{5,4},{6,5},{7,6},{8,11},{9,8},{10,9... | collective-permute-start | bytes 1413128 | tf_op jit(solution)/shard_map/ppermute | solution.py:366
  33.6 18.4 %copy-start.7 = (f32[128]{0:T(128)}, f32[128]{0:T(128)S(1)}, u32[]{:S(2)}) copy-start(f32[128]{0:T(128)S(1)} %reduce_sum.11) | copy-start | bytes 1540
  33.6 7.0 %collective-permute-start.2 = (f32[1,128]{1,0:T(1,128)S(1)}, f32[1,128]{1,0:T(1,128)S(1)}, u32[]{:S(2)}, u32[]{:S(2)}) collective-permute-start(f32[1,128]{1,0:T(1,128)S(1)} %bitcast.9), channel_id=1, source_target_pairs={{0,1},{1,2},{2,3},{3,0},{4,5},{5,6},{6,7},{7,4},{8,9},{9,10},{10,1... | collective-permute-start | bytes 1544 | tf_op jit(solution)/shard_map/ppermute | solution.py:372
  35.8 9.6 %copy-start.8 = (bf16[2,3,144,640]{3,2,1,0:T(8,128)(2,1)S(1)}, bf16[2,3,144,640]{3,2,1,0:T(8,128)(2,1)}, u32[]{:S(2)}) copy-start(bf16[2,3,144,640]{3,2,1,0:T(8,128)(2,1)} %get-tuple-element.36.refs_11_.refs_15_) | copy-start | bytes 3317764
  35.9 5.3 %collective-permute-start.1 = (f32[1,128]{1,0:T(1,128)S(1)}, f32[1,128]{1,0:T(1,128)S(1)}, u32[]{:S(2)}, u32[]{:S(2)}) collective-permute-start(f32[1,128]{1,0:T(1,128)S(1)} %bitcast.10), channel_id=1, source_target_pairs={{0,2},{1,3},{2,0},{3,1},{4,6},{5,7},{6,4},{7,5},{8,10},{9,11},{10,... | collective-permute-start | bytes 1544 | tf_op jit(solution)/shard_map/ppermute | solution.py:372
  39.1 13.0 %copy-start.2 = (bf16[1024,1024]{1,0:T(8,128)(2,1)}, bf16[1024,1024]{1,0:T(8,128)(2,1)S(1)}, u32[]{:S(2)}) copy-start(bf16[1024,1024]{1,0:T(8,128)(2,1)S(1)} %deal.1.refs_14_.refs_18_) | copy-start | bytes 6291460
  39.1 4.6 %collective-permute-start = (f32[1,128]{1,0:T(1,128)S(1)}, f32[1,128]{1,0:T(1,128)S(1)}, u32[]{:S(2)}, u32[]{:S(2)}) collective-permute-start(f32[1,128]{1,0:T(1,128)S(1)} %bitcast.11), channel_id=1, source_target_pairs={{0,3},{1,0},{2,1},{3,2},{4,7},{5,4},{6,5},{7,6},{8,11},{9,8},{10,9... | collective-permute-start | bytes 1544 | tf_op jit(solution)/shard_map/ppermute | solution.py:372
  40.6 11.5 %copy-start.10 = (f32[1,128]{1,0:T(1,128)}, f32[1,128]{1,0:T(1,128)S(1)}, u32[]{:S(2)}) copy-start(f32[1,128]{1,0:T(1,128)S(1)} %collective-permute-done.2.refs_3_) | copy-start | bytes 1540
  40.6 31.6 %collective-permute-start.11 = (bf16[144,2304]{1,0:T(8,128)(2,1)}, bf16[144,2304]{1,0:T(8,128)(2,1)}, u32[]{:S(2)}, u32[]{:S(2)}) collective-permute-start(bf16[144,2304]{1,0:T(8,128)(2,1)} %get-tuple-element.34.refs_9_), channel_id=1, source_target_pairs={{0,1},{1,2},{2,3},{3,0},{4,5},{5,6},{6,7},{7,4},{8,9},{9,10},{10,1... | collective-permute-start | bytes 1990664 | tf_op jit(solution)/shard_map/ppermute | solution.py:372
  41.2 10.9 %copy-start.11 = (f32[1,128]{1,0:T(1,128)}, f32[1,128]{1,0:T(1,128)S(1)}, u32[]{:S(2)}) copy-start(f32[1,128]{1,0:T(1,128)S(1)} %collective-permute-done.1.refs_2_) | copy-start | bytes 1540
  41.2 31.0 %collective-permute-start.10 = (bf16[144,2304]{1,0:T(8,128)(2,1)}, bf16[144,2304]{1,0:T(8,128)(2,1)}, u32[]{:S(2)}, u32[]{:S(2)}) collective-permute-start(bf16[144,2304]{1,0:T(8,128)(2,1)} %get-tuple-element.34.refs_9_), channel_id=1, source_target_pairs={{0,2},{1,3},{2,0},{3,1},{4,6},{5,7},{6,4},{7,5},{8,10},{9,11},{10,... | collective-permute-start | bytes 1990664 | tf_op jit(solution)/shard_map/ppermute | solution.py:372
  43.7 8.4 %copy-start.12 = (f32[1,128]{1,0:T(1,128)}, f32[1,128]{1,0:T(1,128)S(1)}, u32[]{:S(2)}) copy-start(f32[1,128]{1,0:T(1,128)S(1)} %collective-permute-done.refs_1_) | copy-start | bytes 1540
  43.7 29.1 %collective-permute-start.9 = (bf16[144,2304]{1,0:T(8,128)(2,1)}, bf16[144,2304]{1,0:T(8,128)(2,1)}, u32[]{:S(2)}, u32[]{:S(2)}) collective-permute-start(bf16[144,2304]{1,0:T(8,128)(2,1)} %get-tuple-element.34.refs_9_), channel_id=1, source_target_pairs={{0,3},{1,0},{2,1},{3,2},{4,7},{5,4},{6,5},{7,6},{8,11},{9,8},{10,9... | collective-permute-start | bytes 1990664 | tf_op jit(solution)/shard_map/ppermute | solution.py:372
  45.4 6.7 %copy-start.9 = (bf16[80,2944]{1,0:T(8,128)(2,1)}, bf16[80,2944]{1,0:T(8,128)(2,1)S(1)}, u32[]{:S(2)}) copy-start(bf16[80,2944]{1,0:T(8,128)(2,1)S(1)} %collective-permute-done.7.refs_6_) | copy-start | bytes 1413124
  52.1 20.7 %copy-start.13 = (bf16[16,1024]{1,0:T(8,128)(2,1)}, bf16[16,1024]{1,0:T(8,128)(2,1)S(1)}, u32[]{:S(2)}) copy-start(bf16[16,1024]{1,0:T(8,128)(2,1)S(1)} %get-tuple-element.39.refs_19_) | copy-start | bytes 98308
  52.1 45.0 %all-to-all-start.1 = ((bf16[64,16,640]{2,1,0:T(8,128)(2,1)}), bf16[64,16,640]{2,1,0:T(8,128)(2,1)S(1)}, u32[]{:S(2)}, u32[]{:S(2)}) async-start(bf16[64,16,640]{2,1,0:T(8,128)(2,1)} %bitcast.2), calls=%async_computation.1 | async-start | bytes 2621440 | tf_op jit(solution)/shard_map/all_to_all | solution.py:377
  97.2 56.8 %all-to-all-start.2 = ((bf16[64,16,1024]{2,1,0:T(8,128)(2,1)}), bf16[64,16,1024]{2,1,0:T(8,128)(2,1)S(1)}, u32[]{:S(2)}, u32[]{:S(2)}) async-start(bf16[64,16,1024]{2,1,0:T(8,128)(2,1)} %bitcast.17), calls=%async_computation.2 | async-start | bytes 4194304 | tf_op jit(solution)/shard_map/all_to_all | solution.py:377
